TPU v7x, 256 devices: a whole 4x4x8 slice. The times are simulated.
256 devices in a mesh: gx: 4 (over x), gy: 8 (over y, core), gz: 8 (over z).
Axes of the slice: x: 4, y: 4, z: 8, core: 2. Of those that a mesh axis runs over, the one named last changes fastest.
Arguments:
- right_side: float32 [64, 256, 1024], P('gx', 'gy', 'gz'), may hold values from -6 to 6
- coefficient: float32 [64, 256, 1024], P('gx', 'gy', 'gz'), may hold values from 0.1 to 10
Outputs:
- solution: float32 [64, 256, 1024], P('gx', 'gy', 'gz')
All inputs are finite; a program needn't handle non-finite values.
Results may differ from a plain program's by a relative error of at most 0.0003.
Values sent between devices are 32-bit elements; how exact they have to be, the bound alone decides.
No kernel may reach another device: no remote copies, remote signals or barrier semaphores. Data moves between devices by JAX's collectives and lax.ppermute only.
A program may use at most 192 MiB of HBM per device.

v0:
```python
import functools

import jax
import jax.numpy as jnp
from jax import lax
from jax.experimental import pallas as pl
from jax.experimental.pallas import tpu as pltpu
from jax.sharding import PartitionSpec as P

SWEEPS = 2
ITERS = 20
F32 = jnp.float32
VMEM = pl.BlockSpec(memory_space=pltpu.VMEM)
SMEM = pl.BlockSpec(memory_space=pltpu.SMEM)


def lanes(rows):
    return lax.broadcasted_iota(jnp.int32, (rows, 128), 1)


def rows_of(rows):
    return lax.broadcasted_iota(jnp.int32, (rows, 128), 0)


def pick(values, index):
    return jnp.take_along_axis(values, index, axis=1, mode="promise_in_bounds")


def turn(values, shift):
    shift = shift % 128
    return pltpu.roll(values, shift, 1) if shift else values


def up(values):
    return pltpu.roll(values, values.shape[0] - 1, 0)


def down(values):
    return pltpu.roll(values, 1, 0)


def beside(other, x, q, colour, a):
    mid = other[x + 1, q]
    across = other[x + 1, 1 - q]
    back = (colour == 0) == ((a + q) % 2 == 0)
    return [
        other[x + 2, q],
        other[x, q],
        across if q == 0 else up(across),
        down(across) if q == 0 else across,
        mid,
        pltpu.roll(mid, 1 if back else 127, 1),
    ]


def planes(count, body):
    def pair(i, carry):
        for a in (0, 1):
            for q in (0, 1):
                body(2 * i + a, a, q)
        return carry

    lax.fori_loop(0, count // 2, pair, 0)


def set_up(count, rows, cond, src, wd, fd, dd):
    row = rows_of(rows)
    zero = jnp.zeros((2, rows, 128), F32)
    for colour in (0, 1):
        cond[colour, 0] = zero
        cond[colour, count + 1] = zero

    def body(x, a, q):
        for colour in (0, 1):
            other = cond.at[1 - colour]
            own = cond[colour, x + 1, q]
            near = beside(other, x, q, colour, a)
            if q == 0:
                near[3] = jnp.where(row > 0, near[3], 0.0)
            else:
                near[2] = jnp.where(row < rows - 1, near[2], 0.0)
            total = jnp.zeros((rows, 128), F32)
            faces = []
            for value in near:
                face = 2.0 * own * value / jnp.maximum(own + value, 1e-30)
                faces.append(face)
                total = total + jnp.where(value > 0.0, face, 2.0 * own)
            total = jnp.where(total > 0.0, total, 1.0)
            inverse = 1.0 / total
            for i, face in enumerate(faces):
                wd[colour, i, x, q] = face * inverse
            fd[colour, x, q] = src[colour, x, q] * inverse
            if colour == 0:
                dd[x, q] = total

    planes(count, body)


def relaxed(colour, x, a, q, v, wd, fd):
    near = beside(v.at[1 - colour], x, q, colour, a)
    total = fd[colour, x, q]
    for i, value in enumerate(near):
        total = total + wd[colour, i, x, q] * value
    return total


def half_sweep(colour, count, v, wd, fd):
    def body(x, a, q):
        v[colour, x + 1, q] = relaxed(colour, x, a, q, v, wd, fd)

    planes(count, body)


def clear_ends(count, rows, v):
    zero = jnp.zeros((2, rows, 128), F32)
    for colour in (0, 1):
        v[colour, 0] = zero
        v[colour, count + 1] = zero


def first_half(count, v, fd):
    def body(x, a, q):
        v[0, x + 1, q] = fd[0, x, q]

    planes(count, body)


def descend(count, rows, v, wd, fd, dd, cond, out_f, out_b):
    clear_ends(count, rows, v)
    first_half(count, v, fd)
    half_sweep(1, count, v, wd, fd)
    half_sweep(0, count, v, wd, fd)
    half_sweep(1, count, v, wd, fd)

    def body(i, carry):
        left = jnp.zeros((rows, 128), F32)
        mean = jnp.zeros((rows, 128), F32)
        for a in (0, 1):
            for q in (0, 1):
                x = 2 * i + a
                left = left + dd[x, q] * (relaxed(0, x, a, q, v, wd, fd) - v[0, x + 1, q])
                mean = mean + (cond[0, x + 1, q] + cond[1, x + 1, q])
        out_f[i] = 0.5 * left
        out_b[i] = 0.125 * mean
        return carry

    lax.fori_loop(0, count // 2, body, 0)


def ascend(count, v, wd, fd):
    for _ in range(SWEEPS):
        half_sweep(0, count, v, wd, fd)
        half_sweep(1, count, v, wd, fd)


def natural(v, x, a, q, shift, index):
    red, black = v[0, x + 1, q], v[1, x + 1, q]
    even, odd = (red, black) if (a + q) % 2 == 0 else (black, red)
    packed = jnp.where(lanes(even.shape[0]) < shift, even, turn(odd, shift))
    return pick(packed, index)


def split_kernel(f_ref, b_ref, lo_ref, hi_ref, zl_ref, zr_ref):
    lane = lanes(16)
    whole = 2 * (lane % 64) + lane // 64
    slot = lane // 8
    within = lane % 8
    first = 2 * (within % 4) + within // 4
    last = 120 + first
    for half, out in enumerate((lo_ref, hi_ref)):
        for q in (0, 1):
            left = jnp.zeros((16, 128), F32)
            right = jnp.zeros((16, 128), F32)
            for x in range(8):
                for arr, ref in enumerate((f_ref, b_ref)):
                    cells = ref[8 * half + x, pl.ds(q, 16, stride=2), :]
                    out[8 * arr + x, q] = pick(cells, whole)
                    here = slot == 2 * x + arr
                    left = jnp.where(here, pick(cells, first), left)
                    right = jnp.where(here, pick(cells, last), right)
            zl_ref[half, q] = left
            zr_ref[half, q] = right


def edge_kernel(a_ref, b_ref, c_ref, d_ref, lo_ref, hi_ref):
    for t, ref in enumerate((a_ref, b_ref, c_ref, d_ref)):
        def body(i, carry):
            for q in (0, 1):
                cells = ref[i, q]
                lo_ref[18 * t + i, 4 * q : 4 * q + 4] = cells[0:4]
                hi_ref[18 * t + i, 4 * q : 4 * q + 4] = cells[12:16]
            return carry

        lax.fori_loop(0, 18, body, 0)


def level0_down_kernel(
    scal, a_ref, b_ref, c_ref, d_ref, yl_ref, yr_ref,
    own_ref, zl_ref, zr_ref, black_ref, wd, fd,
    cond, src, v, dd, nat_f, nat_b,
):
    gx, gy, gz = scal[0], scal[1], scal[2]
    lane = lanes(24)
    row = rows_of(24)
    inside = (lane < 68) | (lane >= 124)
    inside = inside & ((gz > 0) | (lane < 124)) & ((gz < 7) | (lane < 64) | (lane >= 124))
    inside = inside & ((gy > 0) | (row >= 4)) & ((gy < 7) | (row < 20))
    keep = jnp.where(inside, 1.0, 0.0)
    for t, ref in enumerate((a_ref, b_ref, c_ref, d_ref)):
        here = keep
        if t == 0:
            here = keep * jnp.where(gx > 0, 1.0, 0.0)
        if t == 3:
            here = keep * jnp.where(gx < 3, 1.0, 0.0)

        def wide(i, q):
            return jnp.concatenate(
                [yl_ref[18 * t + i, 4 * q : 4 * q + 4], ref[i, q], yr_ref[18 * t + i, 4 * q : 4 * q + 4]], axis=0
            )

        ends = [(wide(16, q), wide(17, q)) for q in (0, 1)]
        for x in range(8):
            for q in (0, 1):
                from_left, from_right = ends[q]
                for arr in (0, 1):
                    s = 8 * (2 * x + arr)
                    main = wide(8 * arr + x, q)
                    even = jnp.where(
                        lane < 64, main,
                        jnp.where(lane < 96, turn(from_right, 64 - s), turn(from_left, 124 - s)),
                    )
                    odd = jnp.where(
                        lane < 64, turn(main, 64),
                        jnp.where(lane < 96, turn(from_right, 60 - s), turn(from_left, 120 - s)),
                    )
                    red, black = (even, odd) if (x + q) % 2 == 0 else (odd, even)
                    if arr == 0:
                        src[0, 8 * t + x, q] = red
                        src[1, 8 * t + x, q] = black
                    else:
                        cond[0, 8 * t + x + 1, q] = red * here
                        cond[1, 8 * t + x + 1, q] = black * here
    set_up(32, 24, cond, src, wd, fd, dd)
    descend(32, 24, v, wd, fd, dd, cond, nat_f, nat_b)
    black_ref[...] = v[1]
    lane8 = lanes(8)
    index = 2 * (lane8 % 32) + (lane8 // 32) % 2
    group = 32 * ((lane8 % 64) // 16) + lane8 % 16
    for x in range(0, 8, 2):
        for q in (0, 1):
            own = []
            for a in (0, 1):
                f = nat_f[4 + x + a, pl.ds(4 + q, 8, stride=2), :]
                b = nat_b[4 + x + a, pl.ds(4 + q, 8, stride=2), :]
                cells = jnp.where(lane8 < 64, pick(f, index), pick(b, index))
                own_ref[x + a, q] = cells
                own.append(cells)
            zl_ref[x // 2, q] = jnp.where(lane8 < 64, pick(own[0], group), pick(own[1], group))
            zr_ref[x // 2, q] = jnp.where(lane8 < 64, pick(own[0], group + 16), pick(own[1], group + 16))


def level1_down_kernel(
    scal, own_ref, yl_ref, yr_ref,
    out_ref, black_ref, wd, fd,
    cond, src, v, dd, nat_f, nat_b,
):
    gx, gy, gz = scal[0], scal[1], scal[2]
    lane = lanes(8)
    inside = (lane < 64) & ((gz > 0) | (lane >= 16)) & ((gz < 7) | (lane < 48))
    keep = jnp.where(inside, 1.0, 0.0)
    for block, ref in enumerate((yl_ref, own_ref, yr_ref)):
        here = keep
        if block == 0:
            here = keep * jnp.where(gy > 0, 1.0, 0.0)
        if block == 2:
            here = keep * jnp.where(gy < 7, 1.0, 0.0)
        rows = pl.ds(8 * block, 8)

        def body(s, carry):
            start = 8 * ((gx + 4 - s) % 4)
            for x in range(8):
                for q in (0, 1):
                    main = ref[16 * s + x, q]
                    from_left = ref[16 * s + 8 + x // 2, q]
                    from_right = ref[16 * s + 12 + x // 2, q]
                    parts = []
                    for g in range(4):
                        far = 64 * (x % 2) + 16 * g
                        parts.append(
                            jnp.where(
                                lane < 16, turn(from_left, -far),
                                jnp.where(lane < 48, turn(main, 16 - 32 * g), turn(from_right, 48 - far)),
                            )
                        )
                    red, black = (0, 1) if (x + q) % 2 == 0 else (1, 0)
                    src[0, start + x, q, rows] = parts[red]
                    src[1, start + x, q, rows] = parts[black]
                    cond[0, start + x + 1, q, rows] = parts[2 + red] * here
                    cond[1, start + x + 1, q, rows] = parts[2 + black] * here
            return carry

        lax.fori_loop(0, 4, body, 0)
    set_up(32, 24, cond, src, wd, fd, dd)
    descend(32, 24, v, wd, fd, dd, cond, nat_f, nat_b)
    black_ref[...] = v[1]
    index = 2 * (lane % 32) + (lane // 32) % 2
    for x in range(16):
        f = pick(nat_f[x, 8:16], index)
        b = pick(nat_b[x, 8:16], index)
        nat_f[x, 0:8] = jnp.where(lane < 64, f, b)
        for q in (0, 1):
            out_ref[x, 4 * q : 4 * q + 4] = nat_f[x, pl.ds(q, 4, stride=2), :]


def level2_down_kernel(
    scal, in_ref,
    out_ref, black_ref, wd, fd,
    cond, src, v, dd, nat_f, nat_b,
):
    gy, gz = scal[1], scal[2]
    chip = gy // 2
    lane = lanes(8)
    inside = (lane < 32) & ((gz > 0) | (lane >= 8)) & ((gz < 7) | (lane < 24))
    keep = jnp.where(inside, 1.0, 0.0)
    for s in range(4):
        rows = pl.ds(pl.multiple_of(8 * ((chip + 4 - s) % 4), 8), 8)

        def body(i, carry):
            for a in (0, 1):
                x = 2 * i + a
                for q in (0, 1):
                    main = jnp.concatenate(
                        [in_ref[0, s, x, 4 * q : 4 * q + 4], in_ref[1, s, x, 4 * q : 4 * q + 4]], axis=0
                    )
                    parts = [turn(main, -32 * g) for g in range(4)]
                    red, black = (0, 1) if (a + q) % 2 == 0 else (1, 0)
                    src[0, x, q, rows] = parts[red]
                    src[1, x, q, rows] = parts[black]
                    cond[0, x + 1, q, rows] = parts[2 + red] * keep
                    cond[1, x + 1, q, rows] = parts[2 + black] * keep
            return carry

        lax.fori_loop(0, 8, body, 0)
    set_up(16, 32, cond, src, wd, fd, dd)
    descend(16, 32, v, wd, fd, dd, cond, nat_f, nat_b)
    black_ref[...] = v[1]
    lane = lanes(16)
    index = 8 + 2 * (lane % 8) + (lane // 8) % 2
    for xg in (0, 1):
        for q in (0, 1):
            packed = jnp.zeros((16, 128), F32)
            for xi in range(4):
                f = pick(nat_f[4 * xg + xi, pl.ds(q, 16, stride=2), :], index)
                b = pick(nat_b[4 * xg + xi, pl.ds(q, 16, stride=2), :], index)
                packed = jnp.where(lane // 32 == xi, jnp.where(lane % 32 < 16, f, b), packed)
            for r in range(8):
                out_ref[r, xg, q] = packed


def coarse_kernel(
    scal, in_ref, out_ref,
    cond3, src3, v3, dd3, wd3, fd3, nat_f, nat_b,
    cond4, src4, v4, dd4, wd4, fd4, nat4, nat3,
):
    gz = scal[2]
    lane = lanes(16)
    for xg in (0, 1):
        for xi in range(4):
            x = 4 * xg + xi
            for q in (0, 1):
                parts = []
                for g in range(4):
                    cells = jnp.zeros((16, 128), F32)
                    for r in range(8):
                        cells = jnp.where(lane // 8 == r, turn(in_ref[r, xg, q], 8 * r - 32 * xi - 8 * g), cells)
                    parts.append(cells)
                red, black = (0, 1) if (x + q) % 2 == 0 else (1, 0)
                src3[0, x, q] = parts[red]
                src3[1, x, q] = parts[black]
                cond3[0, x + 1, q] = parts[2 + red]
                cond3[1, x + 1, q] = parts[2 + black]
    set_up(8, 16, cond3, src3, wd3, fd3, dd3)
    descend(8, 16, v3, wd3, fd3, dd3, cond3, nat_f, nat_b)
    lane8 = lanes(8)
    even = 2 * (lane8 % 32)
    on_grid = lane8 < 32
    for x in range(4):
        for q in (0, 1):
            f = nat_f[x, pl.ds(q, 8, stride=2), :]
            b = nat_b[x, pl.ds(q, 8, stride=2), :]
            for e in (0, 1):
                colour = (x + q + e) % 2
                src4[colour, x, q] = pick(f, even + e)
                cond4[colour, x + 1, q] = jnp.where(on_grid, pick(b, even + e), 0.0)
    set_up(4, 8, cond4, src4, wd4, fd4, dd4)
    clear_ends(4, 8, v4)
    first_half(4, v4, fd4)
    half_sweep(1, 4, v4, wd4, fd4)

    def step(_, carry):
        half_sweep(0, 4, v4, wd4, fd4)
        half_sweep(1, 4, v4, wd4, fd4)
        return carry

    lax.fori_loop(0, ITERS - 1, step, 0)
    index = (lane8 % 2) * 32 + (lane8 // 2) % 32
    for x in range(4):
        for q in (0, 1):
            nat4[x, pl.ds(q, 8, stride=2), :] = natural(v4, x, x % 2, q, 32, index)

    def add(x, a, q):
        v3[1, x + 1, q] = v3[1, x + 1, q] + nat4[x // 2]

    planes(8, add)
    ascend(8, v3, wd3, fd3)
    place = jnp.clip(16 * gz - 8 + lane, 0, 127)
    index = (place % 2) * 64 + place // 2
    for x in range(8):
        for q in (0, 1):
            nat3[x, pl.ds(q, 16, stride=2), :] = natural(v3, x, x % 2, q, 64, index)
    out_ref[...] = nat3[...]


def level2_up_kernel(scal, black_ref, wd, fd, add_ref, out_ref, v, nat):
    gy = scal[1]
    clear_ends(16, 32, v)

    def add(x, a, q):
        v[1, x + 1, q] = black_ref[x + 1, q] + add_ref[x // 2]

    planes(16, add)
    ascend(16, v, wd, fd)
    lane = lanes(32)
    index = (lane % 2) * 32 + (lane // 2) % 32

    def store(x, a, q):
        nat[x, pl.ds(8 + q, 32, stride=2), :] = natural(v, x, a, q, 32, index)

    planes(16, store)
    start = pl.multiple_of(8 * gy, 8)

    def hand_on(x, carry):
        out_ref[x] = nat[x, pl.ds(start, 24), :]
        return carry

    lax.fori_loop(0, 16, hand_on, 0)


def level1_up_kernel(scal, black_ref, wd, fd, add_ref, out_ref, v, nat):
    gx = scal[0]
    clear_ends(32, 24, v)

    def add(x, a, q):
        v[1, x + 1, q] = black_ref[x + 1, q] + add_ref[x // 2]

    planes(32, add)
    ascend(32, v, wd, fd)
    lane = lanes(24)
    place = jnp.where(lane < 96, lane, lane - 128) + 32
    index = (place % 2) * 64 + jnp.clip(place // 2, 0, 63)

    def store(x, a, q):
        nat[x + 4, pl.ds(q, 24, stride=2), :] = natural(v, x, a, q, 64, index)

    planes(32, store)

    def hand_on(x, carry):
        out_ref[x] = nat[8 * gx + x, 12:36]
        return carry

    lax.fori_loop(0, 16, hand_on, 0)


def level0_up_kernel(black_ref, wd, fd, add_ref, out_ref, v):
    clear_ends(32, 24, v)

    def add(x, a, q):
        v[1, x + 1, q] = black_ref[x + 1, q] + add_ref[x // 2]

    planes(32, add)
    ascend(32, v, wd, fd)
    lane = lanes(24)
    index = (lane % 2) * 64 + lane // 2

    def store(i, carry):
        for a in (0, 1):
            for q in (0, 1):
                x = 2 * i + a
                cells = natural(v, x + 8, a, q, 64, index)
                out_ref[x, pl.ds(q, 16, stride=2), :] = cells[4:20]
        return carry

    lax.fori_loop(0, 8, store, 0)


def arr(*shape):
    return jax.ShapeDtypeStruct(shape, F32)


def level_scratch(count, rows, nat_rows=None):
    return [
        pltpu.VMEM((2, count + 2, 2, rows, 128), F32),
        pltpu.VMEM((2, count, 2, rows, 128), F32),
        pltpu.VMEM((2, count + 2, 2, rows, 128), F32),
        pltpu.VMEM((count, 2, rows, 128), F32),
    ]


def nat_scratch(count, rows):
    return [pltpu.VMEM((count // 2, rows, 128), F32)] * 2


def weights_shape(count, rows):
    return [(2, 6, count, 2, rows, 128), (2, count, 2, rows, 128)]


def call(kernel, outs, scratch, *args, scal=None):
    specs = [VMEM] * len(args)
    if scal is not None:
        specs = [SMEM] + specs
        args = (scal,) + args
    return pl.pallas_call(
        kernel,
        out_shape=outs,
        in_specs=specs,
        out_specs=jax.tree.map(lambda _: VMEM, outs),
        scratch_shapes=scratch,
        compiler_params=pltpu.CompilerParams(vmem_limit_bytes=48 * 1024 * 1024),
    )(*args)


def ring(values, axis, step):
    count = lax.axis_size(axis)
    return lax.ppermute(values, axis, [(i, (i + step) % count) for i in range(count)])


def on_device(right_side, coefficient):
    scal = jnp.stack([lax.axis_index("gx"), lax.axis_index("gy"), lax.axis_index("gz")]).astype(jnp.int32)
    half = arr(16, 2, 16, 128)
    strip = arr(2, 2, 16, 128)
    lo, hi, zl, zr = call(split_kernel, [half, half, strip, strip], [], right_side, coefficient)
    from_left, from_right = ring(zr, "gz", 1), ring(zl, "gz", -1)
    lo = jnp.concatenate([lo, from_left[0:1], from_right[0:1]])
    hi = jnp.concatenate([hi, from_left[1:2], from_right[1:2]])
    before, after = ring(hi, "gx", 1), ring(lo, "gx", -1)
    bundles = (before, lo, hi, after)
    yl, yr = call(edge_kernel, [arr(72, 8, 128)] * 2, [], *bundles)
    from_left, from_right = ring(yr, "gy", 1), ring(yl, "gy", -1)
    own, zl, zr, black0, wd0, fd0 = call(
        level0_down_kernel,
        [arr(8, 2, 8, 128), arr(4, 2, 8, 128), arr(4, 2, 8, 128), arr(34, 2, 24, 128)]
        + [arr(*s) for s in weights_shape(32, 24)],
        level_scratch(32, 24) + nat_scratch(32, 24),
        *bundles, from_left, from_right, scal=scal,
    )
    from_left, from_right = ring(zr, "gz", 1), ring(zl, "gz", -1)
    bundle = jnp.concatenate([own, from_left, from_right])
    column = jnp.concatenate([bundle] + [ring(bundle, "gx", s) for s in (1, 2, 3)])
    from_left, from_right = ring(column, "gy", 1), ring(column, "gy", -1)
    own, black1, wd1, fd1 = call(
        level1_down_kernel,
        [arr(16, 8, 128), arr(34, 2, 24, 128)] + [arr(*s) for s in weights_shape(32, 24)],
        level_scratch(32, 24) + nat_scratch(32, 24),
        column, from_left, from_right, scal=scal,
    )
    own = own[None]
    sheet = jnp.concatenate([own] + [ring(own, "gy", 2 * s) for s in (1, 2, 3)])
    sheet = lax.all_gather(sheet, "gy", axis=0, axis_index_groups=[[0, 1], [2, 3], [4, 5], [6, 7]])
    own, black2, wd2, fd2 = call(
        level2_down_kernel,
        [arr(8, 2, 2, 16, 128), arr(18, 2, 32, 128)] + [arr(*s) for s in weights_shape(16, 32)],
        level_scratch(16, 32) + nat_scratch(16, 32),
        sheet, scal=scal,
    )
    whole = lax.all_to_all(own, "gz", 0, 0, tiled=True)
    correction = call(
        coarse_kernel,
        arr(8, 32, 128),
        level_scratch(8, 16) + [pltpu.VMEM(s, F32) for s in weights_shape(8, 16)] + nat_scratch(8, 16)
        + level_scratch(4, 8) + [pltpu.VMEM(s, F32) for s in weights_shape(4, 8)]
        + [pltpu.VMEM((4, 16, 128), F32), pltpu.VMEM((8, 32, 128), F32)],
        whole, scal=scal,
    )
    correction = call(
        level2_up_kernel, arr(16, 24, 128),
        [pltpu.VMEM((2, 18, 2, 32, 128), F32), pltpu.VMEM((16, 80, 128), F32)],
        black2, wd2, fd2, correction, scal=scal,
    )
    correction = call(
        level1_up_kernel, arr(16, 24, 128),
        [pltpu.VMEM((2, 34, 2, 24, 128), F32), pltpu.VMEM((40, 48, 128), F32)],
        black1, wd1, fd1, correction, scal=scal,
    )
    return call(
        level0_up_kernel, arr(16, 32, 128),
        [pltpu.VMEM((2, 34, 2, 24, 128), F32)],
        black0, wd0, fd0, correction,
    )


def solution(mesh):
    spec = P("gx", "gy", "gz")
    return jax.shard_map(on_device, mesh=mesh, in_specs=(spec, spec), out_specs=spec, check_vma=False)
```

profile of v0, /device:TPU:1, one launch (start us, length us, event | category | flops | bytes accessed | tf_op | source)
XLA Modules:
  0.0 167.9 jit_solution(11750186350918690216)
XLA Ops:
  0.0 0.0 copy-start
  0.0 0.9 copy-done
  1.0 0.0 copy-start.1
  1.0 0.9 copy-done.1
  1.9 1.0 shard_map.28
  2.9 2.5 %collective-permute-start = (f32[2,2,16,128]{3,2,1,0:T(8,128)S(1)}, f32[2,2,16,128]{3,2,1,0:T(8,128)S(1)}, u32[]{:S(2)}, u32[]{:S(2)}) collective-permute-start(f32[2,2,16,128]{3,2,1,0:T(8,128)S(1)} %get-tuple-element.26), channel_id=1, source_target_pairs={{0,1},{1,2},{2,3},{3,4},{4,5},{5,6},{6,7},{7,0},{8,9},{9,10},{10,1... | collective-permute-start | bytes 98312 | tf_op jit(solution)/shard_map/ppermute | solution.py:534
  5.4 4.0 %collective-permute-start.1 = (f32[2,2,16,128]{3,2,1,0:T(8,128)S(1)}, f32[2,2,16,128]{3,2,1,0:T(8,128)S(1)}, u32[]{:S(2)}, u32[]{:S(2)}) collective-permute-start(f32[2,2,16,128]{3,2,1,0:T(8,128)S(1)} %get-tuple-element.27), channel_id=1, source_target_pairs={{0,7},{1,0},{2,1},{3,2},{4,3},{5,4},{6,5},{7,6},{8,15},{9,8},{10,9... | collective-permute-start | bytes 98312 | tf_op jit(solution)/shard_map/ppermute | solution.py:534
  9.5 1.2 collective-permute-done
  10.7 0.0 collective-permute-done.1
  10.7 1.3 collective-permute-start.2
  12.0 1.5 collective-permute-start.3
  13.6 5.4 %collective-permute-done.2.a_ref = f32[18,2,16,128]{3,2,1,0:T(8,128)S(1)} collective-permute-done((f32[18,2,16,128]{3,2,1,0:T(8,128)S(1)}, f32[18,2,16,128]{3,2,1,0:T(8,128)S(1)}, u32[]{:S(2)}, u32[]{:S(2)}) %collective-permute-start.2) | collective-permute-done | bytes 294944 | tf_op jit(solution)/shard_map/ppermute | solution.py:534
  19.0 0.0 collective-permute-done.3.d_ref
  19.0 0.5 shard_map.29
  19.4 3.8 %collective-permute-start.4 = (f32[72,8,128]{2,1,0:T(8,128)S(1)}, f32[72,8,128]{2,1,0:T(8,128)S(1)}, u32[]{:S(2)}, u32[]{:S(2)}) collective-permute-start(f32[72,8,128]{2,1,0:T(8,128)S(1)} %get-tuple-element.29), channel_id=1, source_target_pairs={{0,8},{8,16},{16,24},{24,32},{32,40},{40,48},{48,56},{56,0},{1,9},... | collective-permute-start | bytes 884744 | tf_op jit(solution)/shard_map/ppermute | solution.py:534
  23.2 0.0 collective-permute-start.5
  23.2 0.1 pad_add_fusion.scal
  23.3 3.6 %collective-permute-done.4.yl_ref = f32[72,8,128]{2,1,0:T(8,128)S(1)} collective-permute-done((f32[72,8,128]{2,1,0:T(8,128)S(1)}, f32[72,8,128]{2,1,0:T(8,128)S(1)}, u32[]{:S(2)}, u32[]{:S(2)}) %collective-permute-start.4) | collective-permute-done | bytes 294944 | tf_op jit(solution)/shard_map/ppermute | solution.py:534
  26.9 2.5 %collective-permute-done.5.yr_ref = f32[72,8,128]{2,1,0:T(8,128)S(1)} collective-permute-done((f32[72,8,128]{2,1,0:T(8,128)S(1)}, f32[72,8,128]{2,1,0:T(8,128)S(1)}, u32[]{:S(2)}, u32[]{:S(2)}) %collective-permute-start.5) | collective-permute-done | bytes 294944 | tf_op jit(solution)/shard_map/ppermute | solution.py:534
  29.3 16.0 %shard_map.30 = (f32[8,2,8,128]{3,2,1,0:T(8,128)S(1)}, f32[4,2,8,128]{3,2,1,0:T(8,128)S(1)}, f32[4,2,8,128]{3,2,1,0:T(8,128)S(1)}, f32[34,2,24,128]{3,2,1,0:T(8,...) custom-call(s32[3]{0:T(128)S(1)} %pad_add_fusion.scal, ...), custom_call_target="tpu_custom_call" | custom-call | tf_op jit(solution)/shard_map/pallas_call | solution.py:522
  45.3 0.0 collective-permute-start.6
  45.3 2.7 %collective-permute-start.7 = (f32[4,2,8,128]{3,2,1,0:T(8,128)S(1)}, f32[4,2,8,128]{3,2,1,0:T(8,128)S(1)}, u32[]{:S(2)}, u32[]{:S(2)}) collective-permute-start(f32[4,2,8,128]{3,2,1,0:T(8,128)S(1)} %get-tuple-element.36), channel_id=1, source_target_pairs={{0,7},{1,0},{2,1},{3,2},{4,3},{5,4},{6,5},{7,6},{8,15},{9,8},{10,9... | collective-permute-start | bytes 98312 | tf_op jit(solution)/shard_map/ppermute | solution.py:534
  48.1 1.3 collective-permute-done.6
  49.4 0.0 collective-permute-done.7
  49.4 1.3 collective-permute-start.8
  50.7 2.6 %collective-permute-start.9 = (f32[16,2,8,128]{3,2,1,0:T(8,128)S(1)}, f32[16,2,8,128]{3,2,1,0:T(8,128)S(1)}, u32[]{:S(2)}, u32[]{:S(2)}) collective-permute-start(f32[16,2,8,128]{3,2,1,0:T(8,128)S(1)} %get-tuple-element.47), channel_id=1, source_target_pairs={{0,128},{64,192},{128,0},{192,64},{1,129},{65,193},{129,1},{193,65... | collective-permute-start | bytes 393224 | tf_op jit(solution)/shard_map/ppermute | solution.py:534
  53.3 0.7 collective-permute-start.10
  54.0 0.5 collective-permute-done.8
  54.5 3.7 %collective-permute-done.9 = f32[16,2,8,128]{3,2,1,0:T(8,128)S(1)} collective-permute-done((f32[16,2,8,128]{3,2,1,0:T(8,128)S(1)}, f32[16,2,8,128]{3,2,1,0:T(8,128)S(1)}, u32[]{:S(2)}, u32[]{:S(2)}) %collective-permute-start.9) | collective-permute-done | bytes 131104 | tf_op jit(solution)/shard_map/ppermute | solution.py:534
  58.2 0.6 collective-permute-done.10
  58.8 1.8 %collective-permute-start.12 = (f32[64,2,8,128]{3,2,1,0:T(8,128)S(1)}, f32[64,2,8,128]{3,2,1,0:T(8,128)S(1)}, u32[]{:S(2)}, u32[]{:S(2)}) collective-permute-start(f32[64,2,8,128]{3,2,1,0:T(8,128)S(1)} %constant_dynamic-update-slice_fusion.3.own_ref), channel_id=1, source_target_pairs={{0,56},{8,0},{16,8},{24,16},{32,24},{40,32},{48,40},{56,48},{1,57}... | collective-permute-start | bytes 1572872 | tf_op jit(solution)/shard_map/ppermute | solution.py:534
  60.6 1.2 collective-permute-start.11
  61.8 7.1 %collective-permute-done.12.yr_ref = f32[64,2,8,128]{3,2,1,0:T(8,128)S(1)} collective-permute-done((f32[64,2,8,128]{3,2,1,0:T(8,128)S(1)}, f32[64,2,8,128]{3,2,1,0:T(8,128)S(1)}, u32[]{:S(2)}, u32[]{:S(2)}) %collective-permute-start.12) | collective-permute-done | bytes 524320 | tf_op jit(solution)/shard_map/ppermute | solution.py:534
  69.0 0.0 collective-permute-done.11.yl_ref
  69.0 16.8 %shard_map.31 = (f32[16,8,128]{2,1,0:T(8,128)S(1)}, f32[34,2,24,128]{3,2,1,0:T(8,128)S(1)}, f32[2,6,32,2,24,128]{5,4,3,2,1,0:T(8,128)}, f32[2,32,2,24,128]{4,3,2,1,0:T(8,128)S(1)}) custom-call(s32[3]{0:T(128)S(1)} %pad_add_fusion.scal, f32[64,2,8,128]{3,2,1,0:T(8,128)S(1)} %constant_dynamic-update-slice_fusion.3.own_ref, ...), custom_call_target="tpu_custom_call" | custom-call | tf_op jit(solution)/shard_map/pallas_call | solution.py:522
  85.7 3.2 %collective-permute-start.15 = (f32[1,16,8,128]{3,2,1,0:T(8,128)S(1)}, f32[1,16,8,128]{3,2,1,0:T(8,128)S(1)}, u32[]{:S(2)}, u32[]{:S(2)}) collective-permute-start(f32[1,16,8,128]{3,2,1,0:T(8,128)S(1)} %bitcast.6), channel_id=1, source_target_pairs={{0,48},{8,56},{16,0},{24,8},{32,16},{40,24},{48,32},{56,40},{1,49}... | collective-permute-start | bytes 196616 | tf_op jit(solution)/shard_map/ppermute | solution.py:534
  89.0 0.0 collective-permute-start.14
  89.0 0.6 collective-permute-start.13
  89.6 1.6 collective-permute-done.15
  91.1 2.6 %collective-permute-done.14 = f32[1,16,8,128]{3,2,1,0:T(8,128)S(1)} collective-permute-done((f32[1,16,8,128]{3,2,1,0:T(8,128)S(1)}, f32[1,16,8,128]{3,2,1,0:T(8,128)S(1)}, u32[]{:S(2)}, u32[]{:S(2)}) %collective-permute-start.14) | collective-permute-done | bytes 65568 | tf_op jit(solution)/shard_map/ppermute | solution.py:534
  93.7 0.9 collective-permute-done.13
  94.6 3.6 %all-gather = f32[8,16,8,128]{3,2,1,0:T(8,128)S(1)} all-gather(f32[4,16,8,128]{3,2,1,0:T(8,128)S(1)} %pad_maximum_fusion.2), channel_id=2, replica_groups={{0,8},{16,24},{32,40},{48,56},{1,9},{17,25},{33,41},{49,57},{2,10},{18,..., dimensions={0}, use_global_device_ids=true | all-gather | bytes 786432 | tf_op jit(solution)/shard_map/all_gather | solution.py:568
  98.2 11.3 %shard_map.32 = (f32[8,2,2,16,128]{4,3,2,1,0:T(8,128)S(1)}, f32[18,2,32,128]{3,2,1,0:T(8,128)S(1)}, f32[2,6,16,2,32,128]{5,4,3,2,1,0:T(8,128)}, f32[2,16,2,32,128]{4,3,2,1,0:T(8,128)S(1)}) custom-call(s32[3]{0:T(128)S(1)} %pad_add_fusion.scal, f32[2,4,16,8,128]{4,3,2,1,0:T(8,128)S(1)} %bitcast.5), custom_call_target="tpu_custom_call" | custom-call | tf_op jit(solution)/shard_map/pallas_call | solution.py:522
  109.5 16.1 %all_to_all.5.in_ref = f32[8,2,2,16,128]{4,3,2,1,0:T(8,128)S(1)} all-to-all(f32[8,2,2,16,128]{4,3,2,1,0:T(8,128)S(1)} %get-tuple-element.44), channel_id=1, replica_groups=mesh['gx'=4,'gy'=8,'gz'=8] {'gz'}, dimensions={0} | all-to-all | bytes 524288 | tf_op jit(solution)/shard_map/all_to_all | solution.py:575
  125.6 11.5 %shard_map.33.add_ref = f32[8,32,128]{2,1,0:T(8,128)S(1)} custom-call(s32[3]{0:T(128)S(1)} %pad_add_fusion.scal, f32[8,2,2,16,128]{4,3,2,1,0:T(8,128)S(1)} %all_to_all.5.in_ref), custom_call_target="tpu_custom_call" | custom-call | tf_op jit(solution)/shard_map/pallas_call | solution.py:522
  137.0 7.2 %shard_map.34.add_ref = f32[16,24,128]{2,1,0:T(8,128)S(1)} custom-call(s32[3]{0:T(128)S(1)} %pad_add_fusion.scal, f32[18,2,32,128]{3,2,1,0:T(8,128)S(1)} %get-tuple-element.41.black_ref, f32[2,6,16,2,32,128]{5,4,3,2,1,0:T(8,128)} %get-tuple-element.42.wd, f32[2,16,2,32,128]{4,3,2,1,0:T(8,128)S(1)} %get-tuple-element.43.fd, f32[8,32,128]{2,1,0:T(8,128)S(1)} %shard_map.33.add_ref), custom_call_target="tpu_custom_call" | custom-call | tf_op jit(solution)/shard_map/pallas_call | solution.py:522
  144.2 12.1 %shard_map.35.add_ref = f32[16,24,128]{2,1,0:T(8,128)S(1)} custom-call(s32[3]{0:T(128)S(1)} %pad_add_fusion.scal, f32[34,2,24,128]{3,2,1,0:T(8,128)S(1)} %get-tuple-element.37.black_ref, f32[2,6,32,2,24,128]{5,4,3,2,1,0:T(8,128)} %get-tuple-element.38.wd, f32[2,32,2,24,128]{4,3,2,1,0:T(8,128)S(1)} %get-tuple-element.39.fd, f32[16,24,128]{2,1,0:T(8,128)S(1)} %shard_map.34.add_ref), custom_call_target="tpu_custom_call" | custom-call | tf_op jit(solution)/shard_map/pallas_call | solution.py:522
  156.4 11.5 %shard_map.36 = f32[16,32,128]{2,1,0:T(8,128)} custom-call(f32[34,2,24,128]{3,2,1,0:T(8,128)S(1)} %get-tuple-element.31.black_ref, f32[2,6,32,2,24,128]{5,4,3,2,1,0:T(8,128)} %get-tuple-element.32.wd, f32[2,32,2,24,128]{4,3,2,1,0:T(8,128)S(1)} %get-tuple-element.33.fd, f32[16,24,128]{2,1,0:T(8,128)S(1)} %shard_map.35.add_ref), custom_call_target="tpu_custom_call" | custom-call | tf_op jit(solution)/shard_map/pallas_call | solution.py:522
  (11 shorter events, 0.1 us)
Async XLA Ops:
  0.0 0.9 copy-start
  1.0 0.9 copy-start.1
  2.9 7.8 %collective-permute-start = (f32[2,2,16,128]{3,2,1,0:T(8,128)S(1)}, f32[2,2,16,128]{3,2,1,0:T(8,128)S(1)}, u32[]{:S(2)}, u32[]{:S(2)}) collective-permute-start(f32[2,2,16,128]{3,2,1,0:T(8,128)S(1)} %get-tuple-element.26), channel_id=1, source_target_pairs={{0,1},{1,2},{2,3},{3,4},{4,5},{5,6},{6,7},{7,0},{8,9},{9,10},{10,1... | collective-permute-start | bytes 98312 | tf_op jit(solution)/shard_map/ppermute | solution.py:534
  5.4 5.2 %collective-permute-start.1 = (f32[2,2,16,128]{3,2,1,0:T(8,128)S(1)}, f32[2,2,16,128]{3,2,1,0:T(8,128)S(1)}, u32[]{:S(2)}, u32[]{:S(2)}) collective-permute-start(f32[2,2,16,128]{3,2,1,0:T(8,128)S(1)} %get-tuple-element.27), channel_id=1, source_target_pairs={{0,7},{1,0},{2,1},{3,2},{4,3},{5,4},{6,5},{7,6},{8,15},{9,8},{10,9... | collective-permute-start | bytes 98312 | tf_op jit(solution)/shard_map/ppermute | solution.py:534
  10.7 8.2 %collective-permute-start.2 = (f32[18,2,16,128]{3,2,1,0:T(8,128)S(1)}, f32[18,2,16,128]{3,2,1,0:T(8,128)S(1)}, u32[]{:S(2)}, u32[]{:S(2)}) collective-permute-start(f32[18,2,16,128]{3,2,1,0:T(8,128)S(1)} %pad_maximum_fusion.c_ref), channel_id=1, source_target_pairs={{0,64},{64,128},{128,192},{192,0},{1,65},{65,129},{129,193},{193,1... | collective-permute-start | bytes 884744 | tf_op jit(solution)/shard_map/ppermute | solution.py:534
  12.0 6.9 %collective-permute-start.3 = (f32[18,2,16,128]{3,2,1,0:T(8,128)S(1)}, f32[18,2,16,128]{3,2,1,0:T(8,128)S(1)}, u32[]{:S(2)}, u32[]{:S(2)}) collective-permute-start(f32[18,2,16,128]{3,2,1,0:T(8,128)S(1)} %pad_maximum_fusion.1.b_ref), channel_id=1, source_target_pairs={{0,192},{64,0},{128,64},{192,128},{1,193},{65,1},{129,65},{193,129... | collective-permute-start | bytes 884744 | tf_op jit(solution)/shard_map/ppermute | solution.py:534
  19.4 7.4 %collective-permute-start.4 = (f32[72,8,128]{2,1,0:T(8,128)S(1)}, f32[72,8,128]{2,1,0:T(8,128)S(1)}, u32[]{:S(2)}, u32[]{:S(2)}) collective-permute-start(f32[72,8,128]{2,1,0:T(8,128)S(1)} %get-tuple-element.29), channel_id=1, source_target_pairs={{0,8},{8,16},{16,24},{24,32},{32,40},{40,48},{48,56},{56,0},{1,9},... | collective-permute-start | bytes 884744 | tf_op jit(solution)/shard_map/ppermute | solution.py:534
  23.2 6.1 %collective-permute-start.5 = (f32[72,8,128]{2,1,0:T(8,128)S(1)}, f32[72,8,128]{2,1,0:T(8,128)S(1)}, u32[]{:S(2)}, u32[]{:S(2)}) collective-permute-start(f32[72,8,128]{2,1,0:T(8,128)S(1)} %get-tuple-element.30), channel_id=1, source_target_pairs={{0,56},{8,0},{16,8},{24,16},{32,24},{40,32},{48,40},{56,48},{1,57}... | collective-permute-start | bytes 884744 | tf_op jit(solution)/shard_map/ppermute | solution.py:534
  45.3 4.0 %collective-permute-start.6 = (f32[4,2,8,128]{3,2,1,0:T(8,128)S(1)}, f32[4,2,8,128]{3,2,1,0:T(8,128)S(1)}, u32[]{:S(2)}, u32[]{:S(2)}) collective-permute-start(f32[4,2,8,128]{3,2,1,0:T(8,128)S(1)} %get-tuple-element.35), channel_id=1, source_target_pairs={{0,1},{1,2},{2,3},{3,4},{4,5},{5,6},{6,7},{7,0},{8,9},{9,10},{10,1... | collective-permute-start | bytes 98312 | tf_op jit(solution)/shard_map/ppermute | solution.py:534
  45.3 4.1 %collective-permute-start.7 = (f32[4,2,8,128]{3,2,1,0:T(8,128)S(1)}, f32[4,2,8,128]{3,2,1,0:T(8,128)S(1)}, u32[]{:S(2)}, u32[]{:S(2)}) collective-permute-start(f32[4,2,8,128]{3,2,1,0:T(8,128)S(1)} %get-tuple-element.36), channel_id=1, source_target_pairs={{0,7},{1,0},{2,1},{3,2},{4,3},{5,4},{6,5},{7,6},{8,15},{9,8},{10,9... | collective-permute-start | bytes 98312 | tf_op jit(solution)/shard_map/ppermute | solution.py:534
  49.4 5.1 %collective-permute-start.8 = (f32[16,2,8,128]{3,2,1,0:T(8,128)S(1)}, f32[16,2,8,128]{3,2,1,0:T(8,128)S(1)}, u32[]{:S(2)}, u32[]{:S(2)}) collective-permute-start(f32[16,2,8,128]{3,2,1,0:T(8,128)S(1)} %get-tuple-element.47), channel_id=1, source_target_pairs={{0,64},{64,128},{128,192},{192,0},{1,65},{65,129},{129,193},{193,1... | collective-permute-start | bytes 393224 | tf_op jit(solution)/shard_map/ppermute | solution.py:534
  50.7 7.6 %collective-permute-start.9 = (f32[16,2,8,128]{3,2,1,0:T(8,128)S(1)}, f32[16,2,8,128]{3,2,1,0:T(8,128)S(1)}, u32[]{:S(2)}, u32[]{:S(2)}) collective-permute-start(f32[16,2,8,128]{3,2,1,0:T(8,128)S(1)} %get-tuple-element.47), channel_id=1, source_target_pairs={{0,128},{64,192},{128,0},{192,64},{1,129},{65,193},{129,1},{193,65... | collective-permute-start | bytes 393224 | tf_op jit(solution)/shard_map/ppermute | solution.py:534
  53.3 5.5 %collective-permute-start.10 = (f32[16,2,8,128]{3,2,1,0:T(8,128)S(1)}, f32[16,2,8,128]{3,2,1,0:T(8,128)S(1)}, u32[]{:S(2)}, u32[]{:S(2)}) collective-permute-start(f32[16,2,8,128]{3,2,1,0:T(8,128)S(1)} %get-tuple-element.47), channel_id=1, source_target_pairs={{0,192},{64,0},{128,64},{192,128},{1,193},{65,1},{129,65},{193,129... | collective-permute-start | bytes 393224 | tf_op jit(solution)/shard_map/ppermute | solution.py:534
  58.8 10.1 %collective-permute-start.12 = (f32[64,2,8,128]{3,2,1,0:T(8,128)S(1)}, f32[64,2,8,128]{3,2,1,0:T(8,128)S(1)}, u32[]{:S(2)}, u32[]{:S(2)}) collective-permute-start(f32[64,2,8,128]{3,2,1,0:T(8,128)S(1)} %constant_dynamic-update-slice_fusion.3.own_ref), channel_id=1, source_target_pairs={{0,56},{8,0},{16,8},{24,16},{32,24},{40,32},{48,40},{56,48},{1,57}... | collective-permute-start | bytes 1572872 | tf_op jit(solution)/shard_map/ppermute | solution.py:534
  60.6 8.3 %collective-permute-start.11 = (f32[64,2,8,128]{3,2,1,0:T(8,128)S(1)}, f32[64,2,8,128]{3,2,1,0:T(8,128)S(1)}, u32[]{:S(2)}, u32[]{:S(2)}) collective-permute-start(f32[64,2,8,128]{3,2,1,0:T(8,128)S(1)} %constant_dynamic-update-slice_fusion.3.own_ref), channel_id=1, source_target_pairs={{0,8},{8,16},{16,24},{24,32},{32,40},{40,48},{48,56},{56,0},{1,9},... | collective-permute-start | bytes 1572872 | tf_op jit(solution)/shard_map/ppermute | solution.py:534
  85.7 5.4 %collective-permute-start.15 = (f32[1,16,8,128]{3,2,1,0:T(8,128)S(1)}, f32[1,16,8,128]{3,2,1,0:T(8,128)S(1)}, u32[]{:S(2)}, u32[]{:S(2)}) collective-permute-start(f32[1,16,8,128]{3,2,1,0:T(8,128)S(1)} %bitcast.6), channel_id=1, source_target_pairs={{0,48},{8,56},{16,0},{24,8},{32,16},{40,24},{48,32},{56,40},{1,49}... | collective-permute-start | bytes 196616 | tf_op jit(solution)/shard_map/ppermute | solution.py:534
  89.0 4.7 %collective-permute-start.14 = (f32[1,16,8,128]{3,2,1,0:T(8,128)S(1)}, f32[1,16,8,128]{3,2,1,0:T(8,128)S(1)}, u32[]{:S(2)}, u32[]{:S(2)}) collective-permute-start(f32[1,16,8,128]{3,2,1,0:T(8,128)S(1)} %bitcast.7), channel_id=1, source_target_pairs={{0,32},{8,40},{16,48},{24,56},{32,0},{40,8},{48,16},{56,24},{1,33}... | collective-permute-start | bytes 196616 | tf_op jit(solution)/shard_map/ppermute | solution.py:534
  89.0 5.6 %collective-permute-start.13 = (f32[1,16,8,128]{3,2,1,0:T(8,128)S(1)}, f32[1,16,8,128]{3,2,1,0:T(8,128)S(1)}, u32[]{:S(2)}, u32[]{:S(2)}) collective-permute-start(f32[1,16,8,128]{3,2,1,0:T(8,128)S(1)} %bitcast.8), channel_id=1, source_target_pairs={{0,16},{8,24},{16,32},{24,40},{32,48},{40,56},{48,0},{56,8},{1,17}... | collective-permute-start | bytes 196616 | tf_op jit(solution)/shard_map/ppermute | solution.py:534
where the time goes:
time: 168 us
  Pallas kernels  87.8 us (52%)
  waiting for transfers between devices  31 us (18%)
  starting transfers between devices  27.3 us (16%)
  blocking collectives  19.7 us (12%)
  local copies, waits for them, and re-layouts  1.96 us (1%)
    pallas_call x9, Pallas kernels, call(): pl.pallas_call(kernel, out_shape=outs, in_specs=specs, out_specs=jax.tree...  87.8 us
    ppermute x16, waiting for transfers between devices, ring(): lax.ppermute(values, axis, [(i, (i + step) % count) for i in range(count)])  31 us
    ppermute x16, starting transfers between devices, ring(): lax.ppermute(values, axis, [(i, (i + step) % count) for i in range(count)])  27.3 us
    all_to_all x1, blocking collectives, on_device(): whole = lax.all_to_all(own, 'gz', 0, 0, tiled=True)  16.1 us
    all_gather x1, blocking collectives, on_device(): lax.all_gather(sheet, 'gy', axis=0, axis_index_groups=[[0, 1], [2, 3], [4...  3.62 us
  transfers between devices with their start and end apart: 16, of which 12 were waited for; matrix products, arithmetic and copies ran while one was open for 0% of the time, Pallas kernels for 0%

commit v1 on v0

v1 whole, which is shorter than its diff:
```python
import functools

import jax
import jax.numpy as jnp
from jax import lax
from jax.experimental import pallas as pl
from jax.experimental.pallas import tpu as pltpu
from jax.sharding import PartitionSpec as P

SWEEPS = 2
ITERS = 20
F32 = jnp.float32
OFF = 1e30
VMEM = pl.BlockSpec(memory_space=pltpu.VMEM)
SMEM = pl.BlockSpec(memory_space=pltpu.SMEM)


class Level:
    def __init__(self, count, rows, group, fold):
        self.count, self.rows, self.group, self.fold = count, rows, group, fold

    def wide(self):
        return (self.count + 2, 2, self.rows, 128)

    def own(self):
        return (self.count, 2, self.rows, 128)


L0 = Level(32, 24, 128, None)
L1 = Level(16, 24, 64, "x")
L2 = Level(16, 8, 32, "y")
L3 = Level(8, 8, 64, "y")
L4 = Level(4, 8, 128, None)


def lanes(rows):
    return lax.broadcasted_iota(jnp.int32, (rows, 128), 1)


def rows_of(rows):
    return lax.broadcasted_iota(jnp.int32, (rows, 128), 0)


def pick(values, index):
    return jnp.take_along_axis(values, index, axis=1, mode="promise_in_bounds")


def turn(values, shift):
    shift = shift % 128
    return pltpu.roll(values, shift, 1) if shift else values


def inverse_of(values):
    guess = pl.reciprocal(values, approx=True)
    guess = guess * (2.0 - values * guess)
    return guess * (2.0 - values * guess)


def up(level, values):
    rolled = pltpu.roll(values, level.rows - 1, 0)
    if level.fold == "y":
        rolled = jnp.where(rows_of(level.rows) == level.rows - 1, turn(rolled, -level.group), rolled)
    return rolled


def down(level, values):
    rolled = pltpu.roll(values, 1, 0)
    if level.fold == "y":
        rolled = jnp.where(rows_of(level.rows) == 0, turn(rolled, level.group), rolled)
    return rolled


def goes_back(colour, a, q):
    return (colour == 0) == ((a + q) % 2 == 0)


def beside(level, other, x, q, colour, a):
    mid = other[x + 1, q]
    across = other[x + 1, 1 - q]
    return [
        other[x + 2, q],
        other[x, q],
        across if q == 0 else up(level, across),
        down(level, across) if q == 0 else across,
        mid,
        turn(mid, 1 if goes_back(colour, a, q) else -1),
    ]


def planes(first, last, unroll, body):
    pairs = (last - first) // 2
    unroll = min(unroll, pairs)
    while pairs % unroll:
        unroll -= 1

    def step(i, carry):
        for u in range(unroll):
            for a in (0, 1):
                for q in (0, 1):
                    body(first + 2 * (unroll * i + u) + a, a, q)
        return carry

    if pairs == unroll:
        step(0, 0)
    else:
        lax.fori_loop(0, pairs // unroll, step, 0)


def fill_ends(level, values, rest=0.0):
    lane = lanes(level.rows)
    for q in (0, 1):
        if level.fold == "x":
            values[0, q] = jnp.where(lane < 64, rest, turn(values[level.count, q], 64))
            values[level.count + 1, q] = jnp.where(lane < 64, turn(values[1, q], 64), rest)
        else:
            values[0, q] = jnp.full((level.rows, 128), rest, F32)
            values[level.count + 1, q] = jnp.full((level.rows, 128), rest, F32)


def set_up(level, cond, rec, wd, fd, dd):
    rows = level.rows
    row, lane = rows_of(rows), lanes(rows)
    for colour in (0, 1):
        fill_ends(level, rec[colour], OFF)

    def body(x, a, q):
        for colour in (0, 1):
            own = cond[colour][x, q]
            own_rec = rec[colour][x + 1, q]
            near = beside(level, rec[1 - colour], x, q, colour, a)
            if level.fold == "y":
                if q == 0:
                    near[3] = jnp.where((row == 0) & (lane < level.group), OFF, near[3])
                else:
                    near[2] = jnp.where((row == rows - 1) & (lane >= 128 - level.group), OFF, near[2])
            elif level is L4:
                if q == 0:
                    near[3] = jnp.where(row == 0, OFF, near[3])
                else:
                    near[2] = jnp.where(row == rows - 1, OFF, near[2])
            if level.group < 128:
                end = 0 if goes_back(colour, a, q) else level.group - 1
                near[5] = jnp.where(lane % level.group == end, OFF, near[5])
            total = None
            faces = []
            for value in near:
                off = value > 0.5 * OFF
                face = inverse_of(own_rec + value)
                faces.append(jnp.where(off, 0.0, face))
                part = jnp.where(off, own, face)
                total = part if total is None else total + part
            total = jnp.where(own_rec > 0.5 * OFF, 1.0, total)
            inverse = inverse_of(total)
            for i, face in enumerate(faces):
                wd[colour][i, x, q] = face * inverse
            fd[colour][x, q] = fd[colour][x, q] * (0.5 * inverse)
            if colour == 0:
                dd[x, q] = total

    planes(0, level.count, 1, body)


def relaxed(level, colour, x, a, q, v, wd, fd):
    near = beside(level, v[1 - colour], x, q, colour, a)
    weight = wd[colour]
    one = fd[colour][x, q] + weight[0, x, q] * near[0]
    two = weight[4, x, q] * near[4] + weight[1, x, q] * near[1]
    one = one + weight[2, x, q] * near[2]
    two = two + weight[3, x, q] * near[3]
    return one + (two + weight[5, x, q] * near[5])


def half_sweep(level, colour, v, wd, fd, first=0, last=None):
    def body(x, a, q):
        v[colour][x + 1, q] = relaxed(level, colour, x, a, q, v, wd, fd)

    planes(first, level.count if last is None else last, 8 if level.rows == 8 else 4, body)
    if level.fold == "x":
        fill_ends(level, v[colour])


def first_half(level, v, fd):
    for colour in (0, 1):
        fill_ends(level, v[colour])

    def body(x, a, q):
        v[0][x + 1, q] = fd[0][x, q]

    planes(0, level.count, 4, body)
    if level.fold == "x":
        fill_ends(level, v[0])


def descend(level, v, wd, fd, dd, cond, out_f, out_b, ranges=None):
    ranges = ranges or [(0, level.count)] * 4
    first_half(level, v, fd)
    half_sweep(level, 1, v, wd, fd, *ranges[0])
    half_sweep(level, 0, v, wd, fd, *ranges[1])
    half_sweep(level, 1, v, wd, fd, *ranges[2])
    first, last = ranges[3]

    def body(i, carry):
        for u in (0, 1):
            left = jnp.zeros((level.rows, 128), F32)
            mean = jnp.zeros((level.rows, 128), F32)
            for a in (0, 1):
                for q in (0, 1):
                    x = first + 4 * i + 2 * u + a
                    left = left + dd[x, q] * (relaxed(level, 0, x, a, q, v, wd, fd) - v[0][x + 1, q])
                    mean = mean + (cond[0][x, q] + cond[1][x, q])
            out_f[2 * i + u] = left
            out_b[2 * i + u] = 0.125 * mean
        return carry

    lax.fori_loop(0, (last - first) // 4, body, 0)


def ascend(level, v, wd, fd, ranges=None):
    ranges = ranges or [(0, level.count)] * 4
    for step in range(2 * SWEEPS):
        half_sweep(level, step % 2, v, wd, fd, *ranges[step])


def correct(level, v, black, add):
    for colour in (0, 1):
        fill_ends(level, v[colour])

    def body(x, a, q):
        v[1][x + 1, q] = black[x, q] + add[x // 2]

    planes(0, level.count, 4, body)
    if level.fold == "x":
        fill_ends(level, v[1])


def keep_black(level, v, black):
    def body(x, a, q):
        black[x, q] = v[1][x + 1, q]

    planes(0, level.count, 4, body)


def even_odd(v, x, a, q):
    red, black = v[0][x + 1, q], v[1][x + 1, q]
    return (red, black) if (a + q) % 2 == 0 else (black, red)


def split_kernel(f_ref, b_ref, lo_ref, hi_ref, zl_ref, zr_ref):
    lane = lanes(16)
    whole = 2 * (lane % 64) + lane // 64
    slot = lane // 8
    within = lane % 8
    first = 2 * (within % 4) + within // 4
    last = 120 + first
    for half, out in enumerate((lo_ref, hi_ref)):
        for q in (0, 1):
            left = jnp.zeros((16, 128), F32)
            right = jnp.zeros((16, 128), F32)
            for x in range(8):
                for arr, ref in enumerate((f_ref, b_ref)):
                    cells = ref[8 * half + x, pl.ds(q, 16, stride=2), :]
                    out[8 * arr + x, q] = pick(cells, whole)
                    here = slot == 2 * x + arr
                    left = jnp.where(here, pick(cells, first), left)
                    right = jnp.where(here, pick(cells, last), right)
            zl_ref[half, q] = left
            zr_ref[half, q] = turn(right, 60)


def edge_kernel(a_ref, b_ref, c_ref, d_ref, lo_ref, hi_ref):
    for t, ref in enumerate((a_ref, b_ref, c_ref, d_ref)):
        for i in range(18):
            for q in (0, 1):
                cells = ref[i, q]
                lo_ref[18 * t + i, 4 * q : 4 * q + 4] = cells[0:4]
                hi_ref[18 * t + i, 4 - 4 * q : 8 - 4 * q] = cells[12:16]


def level0_down_kernel(
    scal, a_ref, b_ref, c_ref, d_ref, yl_ref, yr_ref,
    own_ref, zl_ref, zr_ref, black_ref, wd0, wd1, fd0, fd1,
    cond0, cond1, rec0, rec1, v0, v1, dd, nat_f, nat_b,
):
    cond, rec, v, wd, fd = (cond0, cond1), (rec0, rec1), (v0, v1), (wd0, wd1), (fd0, fd1)
    gx, gy, gz = scal[0], scal[1], scal[2]
    lane, row = lanes(24), rows_of(24)
    inside = (lane < 68) | (lane >= 124)
    inside = inside & ((gz > 0) | (lane < 124)) & ((gz < 7) | (lane < 64) | (lane >= 124))
    inside = inside & ((gy > 0) | (row < 20)) & ((gy < 7) | (row < 16) | (row >= 20))
    keep = jnp.where(inside, 1.0, 0.0)
    low = rows_of(8) < 4
    for t, ref in enumerate((a_ref, b_ref, c_ref, d_ref)):
        here = keep
        if t == 0:
            here = keep * jnp.where(gx > 0, 1.0, 0.0)
        if t == 3:
            here = keep * jnp.where(gx < 3, 1.0, 0.0)

        def wide(i, q):
            right, left = yr_ref[18 * t + i], yl_ref[18 * t + i]
            edge = jnp.where(low, right, left) if q == 0 else pltpu.roll(jnp.where(low, left, right), 4, 0)
            return jnp.concatenate([ref[i, q], edge], axis=0)

        ends = [(wide(16, q), wide(17, q)) for q in (0, 1)]
        for x in range(8):
            for q in (0, 1):
                from_left, from_right = ends[q]
                for arr in (0, 1):
                    s = 2 * x + arr
                    main = wide(8 * arr + x, q)
                    edge = jnp.where(lane // 8 == s, from_right, from_left)
                    even = jnp.where(lane < 64, main, turn(edge, 64 - 8 * s))
                    odd = jnp.where(lane < 64, turn(main, 64), turn(edge, 60 - 8 * s))
                    cells = (even, odd) if (x + q) % 2 == 0 else (odd, even)
                    for colour in (0, 1):
                        if arr == 0:
                            fd[colour][8 * t + x, q] = cells[colour]
                        else:
                            on_grid = cells[colour] * here
                            cond[colour][8 * t + x, q] = on_grid
                            rec[colour][8 * t + x + 1, q] = jnp.where(
                                here > 0.0, inverse_of(cells[colour]), OFF
                            )
    set_up(L0, cond, rec, wd, fd, dd)
    descend(L0, v, wd, fd, dd, cond, nat_f, nat_b, [(2, 30), (2, 30), (4, 28), (8, 24)])
    keep_black(L0, v, black_ref)
    lane8 = lanes(8)
    index = 2 * (lane8 % 32) + (lane8 // 32) % 2
    group = 32 * ((lane8 % 64) // 16) + lane8 % 16
    for x in range(0, 8, 2):
        for q in (0, 1):
            own = []
            for a in (0, 1):
                f = nat_f[x + a, pl.ds(q, 8, stride=2), :]
                b = nat_b[x + a, pl.ds(q, 8, stride=2), :]
                cells = jnp.where(lane8 < 64, pick(f, index), pick(b, index))
                own_ref[x + a, q] = cells
                own.append(cells)
            left = jnp.where(lane8 < 64, pick(own[0], group), pick(own[1], group))
            zl_ref[x // 2, q] = turn(left, 48)
            zr_ref[x // 2, q] = jnp.where(lane8 < 64, pick(own[0], group + 16), pick(own[1], group + 16))


def level1_down_kernel(
    scal, own_ref, yl_ref, yr_ref,
    out_ref, black_ref, wd0, wd1, fd0, fd1,
    cond0, cond1, rec0, rec1, v0, v1, dd, nat_f, nat_b,
):
    cond, rec, v, wd, fd = (cond0, cond1), (rec0, rec1), (v0, v1), (wd0, wd1), (fd0, fd1)
    gx, gy, gz = scal[0], scal[1], scal[2]
    lane = lanes(8)
    k = lane % 64
    inside = ((gz > 0) | (k >= 16)) & ((gz < 7) | (k < 48))
    keep = jnp.where(inside, 1.0, 0.0)
    for block, ref in enumerate((yl_ref, own_ref, yr_ref)):
        here = keep
        if block == 0:
            here = keep * jnp.where(gy > 0, 1.0, 0.0)
        if block == 2:
            here = keep * jnp.where(gy < 7, 1.0, 0.0)
        rows = pl.ds(8 * block, 8)

        def body(j, carry):
            slots = [16 * ((gx + 4 - j) % 4), 16 * ((gx + 6 - j) % 4)]
            for x in range(8):
                for q in (0, 1):
                    parts = []
                    for g in range(4):
                        far = 64 * (x % 2) + 16 * g
                        made = []
                        for h, slot in enumerate(slots):
                            main = ref[slot + x, q]
                            from_left = ref[slot + 8 + x // 2, q]
                            from_right = ref[slot + 12 + x // 2, q]
                            edge = jnp.where(lane // 16 == far // 16, from_left, from_right)
                            made.append((turn(main, 64 * h + 16 - 32 * g), turn(edge, 64 * h - far)))
                        main = jnp.where(lane < 64, made[0][0], made[1][0])
                        edge = jnp.where(lane < 64, made[0][1], made[1][1])
                        parts.append(jnp.where((k >= 16) & (k < 48), main, edge))
                    for colour in (0, 1):
                        odd = (x + q + colour) % 2
                        fd[colour][8 * j + x, q, rows] = parts[odd]
                        cond[colour][8 * j + x, q, rows] = parts[2 + odd] * here
                        rec[colour][8 * j + x + 1, q, rows] = jnp.where(
                            here > 0.0, inverse_of(parts[2 + odd]), OFF
                        )
            return carry

        lax.fori_loop(0, 2, body, 0)
    set_up(L1, cond, rec, wd, fd, dd)
    descend(L1, v, wd, fd, dd, cond, nat_f, nat_b)
    keep_black(L1, v, black_ref)
    for h in (0, 1):
        index = 64 * h + 2 * (lane % 32) + (lane // 32) % 2
        for x in range(8):
            f = pick(nat_f[x, 8:16], index)
            b = pick(nat_b[x, 8:16], index)
            nat_f[x, 0:8] = jnp.where(lane < 64, f, b)
            for q in (0, 1):
                out_ref[8 * h + x, 4 * q : 4 * q + 4] = nat_f[x, pl.ds(q, 4, stride=2), :]


def level2_down_kernel(
    scal, in_ref,
    out_ref, black_ref, wd0, wd1, fd0, fd1,
    cond0, cond1, rec0, rec1, v0, v1, dd, nat_f, nat_b,
):
    cond, rec, v, wd, fd = (cond0, cond1), (rec0, rec1), (v0, v1), (wd0, wd1), (fd0, fd1)
    gy, gz = scal[1], scal[2]
    chip = gy // 2
    lane = lanes(8)
    k = lane % 32
    inside = ((gz > 0) | (k >= 8)) & ((gz < 7) | (k < 24))
    slots = [(chip + 4 - j) % 4 for j in range(4)]

    def body(x, a, q):
        mains = []
        for slot in slots:
            both = [in_ref[c, slot, x, 4 * q : 4 * q + 4] for c in (0, 1)]
            mains.append(jnp.concatenate(both, axis=0))
        parts = []
        for g in range(4):
            part = turn(mains[0], -32 * g)
            for j in (1, 2, 3):
                part = jnp.where(lane // 32 == j, turn(mains[j], 32 * (j - g)), part)
            parts.append(part)
        for colour in (0, 1):
            odd = (a + q + colour) % 2
            fd[colour][x, q] = parts[odd]
            cond[colour][x, q] = jnp.where(inside, parts[2 + odd], 0.0)
            rec[colour][x + 1, q] = jnp.where(inside, inverse_of(parts[2 + odd]), OFF)

    planes(0, 16, 2, body)
    set_up(L2, cond, rec, wd, fd, dd)
    descend(L2, v, wd, fd, dd, cond, nat_f, nat_b)
    keep_black(L2, v, black_ref)
    index = 32 * (lane // 32) + 8 + 2 * (lane % 8) + (lane // 8) % 2
    for x in range(8):
        packed = jnp.where(lane % 32 < 16, pick(nat_f[x], index), pick(nat_b[x], index))
        for r in range(8):
            out_ref[r, x] = packed


def unfold(ref, x, q, group):
    cells = ref[x, pl.ds(q, 8, stride=2), :]
    for j in range(1, 128 // group):
        more = ref[x, pl.ds(16 * j + q, 8, stride=2), :]
        cells = jnp.where(lanes(8) // group == j, turn(more, group * j), cells)
    return cells


def coarse_kernel(
    scal, in_ref, out_ref,
    cond30, cond31, rec30, rec31, v30, v31, dd3, wd30, wd31, fd30, fd31, nat_f, nat_b,
    cond40, cond41, rec40, rec41, v40, v41, dd4, wd40, wd41, fd40, fd41, whole, nat4, nat3,
):
    cond3, rec3, v3, wd3, fd3 = (cond30, cond31), (rec30, rec31), (v30, v31), (wd30, wd31), (fd30, fd31)
    cond4, rec4, v4, wd4, fd4 = (cond40, cond41), (rec40, rec41), (v40, v41), (wd40, wd41), (fd40, fd41)
    gz = scal[2]
    lane = lanes(8)

    def collect(x, carry):
        for g in range(4):
            for mq in range(4):
                cells = turn(in_ref[0, x], -32 * mq - 8 * g)
                for r in range(1, 8):
                    cells = jnp.where(lane // 8 == r, turn(in_ref[r, x], 8 * r - 32 * mq - 8 * g), cells)
                whole[g, x, 8 * mq : 8 * mq + 8] = cells
        return carry

    lax.fori_loop(0, 8, collect, 0)

    def place3(x, a, q):
        for colour in (0, 1):
            odd = (a + q + colour) % 2
            fd3[colour][x, q] = unfold(whole.at[odd], x, q, 64)
            cells = unfold(whole.at[2 + odd], x, q, 64)
            cond3[colour][x, q] = cells
            rec3[colour][x + 1, q] = inverse_of(cells)

    planes(0, 8, 2, place3)
    set_up(L3, cond3, rec3, wd3, fd3, dd3)
    descend(L3, v3, wd3, fd3, dd3, cond3, nat_f, nat_b)
    on_grid = lane < 32
    for x in range(4):
        f_plane, b_plane = nat_f[x], nat_b[x]
        for half in (0, 1):
            nat4[x, 8 * half : 8 * half + 8] = turn(f_plane, 64 * half)
            whole[0, x, 8 * half : 8 * half + 8] = turn(b_plane, 64 * half)
        for q in (0, 1):
            f = nat4[x, pl.ds(q, 8, stride=2), :]
            b = whole[0, x, pl.ds(q, 8, stride=2), :]
            for e in (0, 1):
                colour = (x + q + e) % 2
                index = 2 * (lane % 32) + e
                fd4[colour][x, q] = pick(f, index)
                cells = pick(b, index)
                cond4[colour][x, q] = jnp.where(on_grid, cells, 0.0)
                rec4[colour][x + 1, q] = jnp.where(on_grid, inverse_of(cells), OFF)
    set_up(L4, cond4, rec4, wd4, fd4, dd4)

    def half(colour, other):
        made = {}
        for x in range(4):
            for q in (0, 1):
                mid, across = other[x, q], other[x, 1 - q]
                weight = lambda i: wd4[colour][i, x, q]
                total = fd4[colour][x, q] + weight(4) * mid
                total = total + weight(2) * (across if q == 0 else up(L4, across))
                total = total + weight(3) * (down(L4, across) if q == 0 else across)
                rest = weight(5) * turn(mid, 1 if goes_back(colour, x, q) else -1)
                if x < 3:
                    rest = rest + weight(0) * other[x + 1, q]
                if x > 0:
                    rest = rest + weight(1) * other[x - 1, q]
                made[x, q] = total + rest
        return made

    keys = [(x, q) for x in range(4) for q in (0, 1)]
    black = half(1, {key: fd4[0][key] for key in keys})

    def step(_, carry):
        after = half(1, half(0, dict(zip(keys, carry))))
        return tuple(after[key] for key in keys)

    final = lax.fori_loop(0, ITERS - 2, step, tuple(black[key] for key in keys))
    red = half(0, dict(zip(keys, final)))
    black = half(1, red)
    index = (lane % 2) * 32 + (lane // 2) % 32
    for x, q in keys:
        even, odd = (red[x, q], black[x, q]) if (x + q) % 2 == 0 else (black[x, q], red[x, q])
        nat4[x, pl.ds(q, 8, stride=2), :] = pick(jnp.where(lane < 32, even, turn(odd, 32)), index)
    for x in range(4):
        nat_f[x] = jnp.where(lane < 64, nat4[x, 0:8], turn(nat4[x, 8:16], 64))

    def add(x, a, q):
        v3[1][x + 1, q] = v3[1][x + 1, q] + nat_f[x // 2]

    planes(0, 8, 4, add)
    ascend(L3, v3, wd3, fd3)
    z = jnp.clip(16 * gz - 8 + lane % 32, 0, 127)
    index = (z % 2) * 64 + z // 2
    for x in range(8):
        for q in (0, 1):
            even, odd = even_odd(v3, x, x, q)
            first = pick(jnp.where(lane < 64, even, turn(odd, 64)), index)
            second = pick(jnp.where(lane < 64, turn(even, 64), odd), index)
            nat3[x, pl.ds(q, 8, stride=2), :] = first
            nat3[x, pl.ds(16 + q, 8, stride=2), :] = second
        cells = nat3[x, 0:8]
        for j in (1, 2, 3):
            cells = jnp.where(lane // 32 == j, nat3[x, 8 * j : 8 * j + 8], cells)
        out_ref[x] = cells


def level2_up_kernel(scal, black_ref, wd0, wd1, fd0, fd1, add_ref, out_ref, v0, v1, nat):
    v, wd, fd = (v0, v1), (wd0, wd1), (fd0, fd1)
    gy = scal[1]
    correct(L2, v, black_ref, add_ref)
    ascend(L2, v, wd, fd)
    lane = lanes(8)
    k = lane % 64
    start = pl.multiple_of(8 * gy, 8)
    for x in range(16):
        nat[x, 0:8] = jnp.zeros((8, 128), F32)
        nat[x, 72:80] = jnp.zeros((8, 128), F32)

    def store(x, a, q):
        even, odd = even_odd(v, x, a, q)
        for mq in range(4):
            packed = jnp.where(lane < 32, turn(even, -32 * mq), turn(odd, 32 - 32 * mq))
            nat[x, pl.ds(8 + 16 * mq + q, 8, stride=2), :] = pick(packed, (k % 2) * 32 + k // 2)

    planes(0, 16, 2, store)
    side = lanes(24) < 64
    for x in range(8):
        out_ref[x] = jnp.where(side, nat[x, pl.ds(start, 24), :], nat[8 + x, pl.ds(start, 24), :])


def level1_up_kernel(scal, black_ref, wd0, wd1, fd0, fd1, add_ref, out_ref, v0, v1, nat):
    v, wd, fd = (v0, v1), (wd0, wd1), (fd0, fd1)
    gx = scal[0]
    correct(L1, v, black_ref, add_ref)
    ascend(L1, v, wd, fd)
    lane = lanes(24)
    z = jnp.where(lane < 96, lane, lane - 128) + 32
    index = (z % 2) * 64 + jnp.clip(z // 2, 0, 63)
    for x in range(4):
        nat[x] = jnp.zeros((48, 128), F32)
        nat[36 + x] = jnp.zeros((48, 128), F32)

    def store(x, a, q):
        even, odd = even_odd(v, x, a, q)
        first = jnp.where(lane < 64, even, turn(odd, 64))
        second = jnp.where(lane < 64, turn(even, 64), odd)
        nat[x + 4, pl.ds(q, 24, stride=2), :] = pick(first, index)
        nat[x + 20, pl.ds(q, 24, stride=2), :] = pick(second, index)

    planes(0, 16, 2, store)

    def hand_on(x, carry):
        out_ref[x, 0:16] = nat[8 * gx + x, 16:32]
        out_ref[x, 16:20] = nat[8 * gx + x, 32:36]
        out_ref[x, 20:24] = nat[8 * gx + x, 12:16]
        return carry

    lax.fori_loop(0, 16, hand_on, 0)


def level0_up_kernel(black_ref, wd0, wd1, fd0, fd1, add_ref, out_ref, v0, v1):
    v, wd, fd = (v0, v1), (wd0, wd1), (fd0, fd1)
    correct(L0, v, black_ref, add_ref)
    ascend(L0, v, wd, fd, [(4, 28), (6, 26), (6, 26), (8, 24)])
    lane = lanes(16)
    index = (lane % 2) * 64 + lane // 2

    def store(x, a, q):
        even, odd = even_odd(v, x, a, q)
        packed = jnp.where(lane < 64, even[0:16], turn(odd[0:16], 64))
        out_ref[x - 8, pl.ds(q, 16, stride=2), :] = pick(packed, index)

    planes(8, 24, 4, store)


def arr(*shape):
    return jax.ShapeDtypeStruct(shape, F32)


def scratch(*shape):
    return pltpu.VMEM(shape, F32)


def level_scratch(level):
    shapes = [level.own()] * 2 + [level.wide()] * 4 + [level.own()]
    return [scratch(*s) for s in shapes]


def nat_scratch(level, count=None):
    return [scratch(count or level.count // 2, level.rows, 128)] * 2


def weights(level):
    return [(6,) + level.own()] * 2 + [level.own()] * 2


def call(kernel, outs, temps, *args, scal=None, limit=28):
    specs = [VMEM] * len(args)
    if scal is not None:
        specs = [SMEM] + specs
        args = (scal,) + args
    return pl.pallas_call(
        kernel,
        out_shape=outs,
        in_specs=specs,
        out_specs=jax.tree.map(lambda _: VMEM, outs),
        scratch_shapes=temps,
        compiler_params=pltpu.CompilerParams(vmem_limit_bytes=limit * 1024 * 1024),
    )(*args)


def ring(values, axis, step):
    count = lax.axis_size(axis)
    return lax.ppermute(values, axis, [(i, (i + step) % count) for i in range(count)])


def on_device(right_side, coefficient):
    scal = jnp.stack([lax.axis_index("gx"), lax.axis_index("gy"), lax.axis_index("gz")]).astype(jnp.int32)
    half = arr(16, 2, 16, 128)
    strip = arr(2, 2, 16, 128)
    lo, hi, zl, zr = call(split_kernel, [half, half, strip, strip], [], right_side, coefficient)
    from_left, from_right = ring(zr, "gz", 1), ring(zl, "gz", -1)
    lo = jnp.concatenate([lo, from_left[0:1], from_right[0:1]])
    hi = jnp.concatenate([hi, from_left[1:2], from_right[1:2]])
    before, after = ring(hi, "gx", 1), ring(lo, "gx", -1)
    bundles = (before, lo, hi, after)
    yl, yr = call(edge_kernel, [arr(72, 8, 128)] * 2, [], *bundles)
    from_left, from_right = ring(yr, "gy", 1), ring(yl, "gy", -1)
    own, zl, zr, black0, *set0 = call(
        level0_down_kernel,
        [arr(8, 2, 8, 128), arr(4, 2, 8, 128), arr(4, 2, 8, 128), arr(*L0.own())]
        + [arr(*s) for s in weights(L0)],
        level_scratch(L0) + nat_scratch(L0, 8),
        *bundles, from_left, from_right, scal=scal,
    )
    from_left, from_right = ring(zr, "gz", 1), ring(zl, "gz", -1)
    bundle = jnp.concatenate([own, from_left, from_right])
    column = jnp.concatenate([bundle] + [ring(bundle, "gx", s) for s in (1, 2, 3)])
    from_left, from_right = ring(column, "gy", 1), ring(column, "gy", -1)
    own, black1, *set1 = call(
        level1_down_kernel,
        [arr(16, 8, 128), arr(*L1.own())] + [arr(*s) for s in weights(L1)],
        level_scratch(L1) + nat_scratch(L1),
        column, from_left, from_right, scal=scal,
    )
    own = own[None]
    sheet = jnp.concatenate([own] + [ring(own, "gy", 2 * s) for s in (1, 2, 3)])
    sheet = lax.all_gather(sheet, "gy", axis=0, axis_index_groups=[[0, 1], [2, 3], [4, 5], [6, 7]])
    own, black2, *set2 = call(
        level2_down_kernel,
        [arr(8, 8, 8, 128), arr(*L2.own())] + [arr(*s) for s in weights(L2)],
        level_scratch(L2) + nat_scratch(L2),
        sheet, scal=scal,
    )
    whole = lax.all_to_all(own, "gz", 0, 0, tiled=True)
    correction = call(
        coarse_kernel,
        arr(8, 8, 128),
        level_scratch(L3) + [scratch(*s) for s in weights(L3)] + nat_scratch(L3)
        + level_scratch(L4) + [scratch(*s) for s in weights(L4)]
        + [scratch(4, 8, 32, 128), scratch(4, 16, 128), scratch(8, 32, 128)],
        whole, scal=scal,
    )
    correction = call(
        level2_up_kernel, arr(8, 24, 128),
        [scratch(*L2.wide())] * 2 + [scratch(16, 80, 128)],
        black2, *set2, correction, scal=scal,
    )
    correction = call(
        level1_up_kernel, arr(16, 24, 128),
        [scratch(*L1.wide())] * 2 + [scratch(40, 48, 128)],
        black1, *set1, correction, scal=scal,
    )
    return call(
        level0_up_kernel, arr(16, 32, 128),
        [scratch(*L0.wide())] * 2,
        black0, *set0, correction,
    )


def solution(mesh):
    spec = P("gx", "gy", "gz")
    return jax.shard_map(on_device, mesh=mesh, in_specs=(spec, spec), out_specs=spec, check_vma=False)
```

time: 168 us -> 118 us (0.70)
  Pallas kernels: 87.8 us -> 37.2 us
    pallas_call x9, Pallas kernels: 87.8 us -> 37.2 us  [call(): pl.pallas_call(kernel, out_shape=outs, in_specs=specs, out_specs=jax.tree...]
where the time goes in v1:
time: 118 us
  Pallas kernels  37.2 us (32%)
  waiting for transfers between devices  30.7 us (26%)
  starting transfers between devices  27.8 us (24%)
  blocking collectives  19.8 us (17%)
  local copies, waits for them, and re-layouts  1.96 us (2%)
    pallas_call x9, Pallas kernels, call(): pl.pallas_call(kernel, out_shape=outs, in_specs=specs, out_specs=jax.tree...  37.2 us
    ppermute x16, waiting for transfers between devices, ring(): lax.ppermute(values, axis, [(i, (i + step) % count) for i in range(count)])  30.7 us
    ppermute x16, starting transfers between devices, ring(): lax.ppermute(values, axis, [(i, (i + step) % count) for i in range(count)])  27.8 us
    all_to_all x1, blocking collectives, on_device(): whole = lax.all_to_all(own, 'gz', 0, 0, tiled=True)  16.1 us
    all_gather x1, blocking collectives, on_device(): lax.all_gather(sheet, 'gy', axis=0, axis_index_groups=[[0, 1], [2, 3], [4...  3.73 us
  transfers between devices with their start and end apart: 16, of which 12 were waited for; matrix products, arithmetic and copies ran while one was open for 0% of the time, Pallas kernels for 0%

profile of v1, /device:TPU:1, one launch (start us, length us, event | category | flops | bytes accessed | tf_op | source)
XLA Modules:
  0.0 117.6 jit_solution(16377861391014366824)
XLA Ops:
  0.0 0.0 copy-start
  0.0 0.9 copy-done
  1.0 0.0 copy-start.1
  1.0 0.9 copy-done.1
  1.9 1.0 shard_map.28
  2.9 2.5 %collective-permute-start = (f32[2,2,16,128]{3,2,1,0:T(8,128)S(1)}, f32[2,2,16,128]{3,2,1,0:T(8,128)S(1)}, u32[]{:S(2)}, u32[]{:S(2)}) collective-permute-start(f32[2,2,16,128]{3,2,1,0:T(8,128)S(1)} %get-tuple-element.32), channel_id=1, source_target_pairs={{0,1},{1,2},{2,3},{3,4},{4,5},{5,6},{6,7},{7,0},{8,9},{9,10},{10,1... | collective-permute-start | bytes 98312 | tf_op jit(solution)/shard_map/ppermute | solution.py:663
  5.5 4.0 %collective-permute-start.1 = (f32[2,2,16,128]{3,2,1,0:T(8,128)S(1)}, f32[2,2,16,128]{3,2,1,0:T(8,128)S(1)}, u32[]{:S(2)}, u32[]{:S(2)}) collective-permute-start(f32[2,2,16,128]{3,2,1,0:T(8,128)S(1)} %get-tuple-element.33), channel_id=1, source_target_pairs={{0,7},{1,0},{2,1},{3,2},{4,3},{5,4},{6,5},{7,6},{8,15},{9,8},{10,9... | collective-permute-start | bytes 98312 | tf_op jit(solution)/shard_map/ppermute | solution.py:663
  9.5 1.2 %collective-permute-done = f32[2,2,16,128]{3,2,1,0:T(8,128)S(1)} collective-permute-done((f32[2,2,16,128]{3,2,1,0:T(8,128)S(1)}, f32[2,2,16,128]{3,2,1,0:T(8,128)S(1)}, u32[]{:S(2)}, u32[]{:S(2)}) %collective-permute-start) | collective-permute-done | bytes 32800 | tf_op jit(solution)/shard_map/ppermute | solution.py:663
  10.7 0.0 collective-permute-done.1
  10.8 1.3 %collective-permute-start.2 = (f32[18,2,16,128]{3,2,1,0:T(8,128)S(1)}, f32[18,2,16,128]{3,2,1,0:T(8,128)S(1)}, u32[]{:S(2)}, u32[]{:S(2)}) collective-permute-start(f32[18,2,16,128]{3,2,1,0:T(8,128)S(1)} %pad_maximum_fusion.c_ref), channel_id=1, source_target_pairs={{0,64},{64,128},{128,192},{192,0},{1,65},{65,129},{129,193},{193,1... | collective-permute-start | bytes 884744 | tf_op jit(solution)/shard_map/ppermute | solution.py:663
  12.1 1.5 %collective-permute-start.3 = (f32[18,2,16,128]{3,2,1,0:T(8,128)S(1)}, f32[18,2,16,128]{3,2,1,0:T(8,128)S(1)}, u32[]{:S(2)}, u32[]{:S(2)}) collective-permute-start(f32[18,2,16,128]{3,2,1,0:T(8,128)S(1)} %pad_maximum_fusion.1.b_ref), channel_id=1, source_target_pairs={{0,192},{64,0},{128,64},{192,128},{1,193},{65,1},{129,65},{193,129... | collective-permute-start | bytes 884744 | tf_op jit(solution)/shard_map/ppermute | solution.py:663
  13.6 5.4 %collective-permute-done.2.a_ref = f32[18,2,16,128]{3,2,1,0:T(8,128)S(1)} collective-permute-done((f32[18,2,16,128]{3,2,1,0:T(8,128)S(1)}, f32[18,2,16,128]{3,2,1,0:T(8,128)S(1)}, u32[]{:S(2)}, u32[]{:S(2)}) %collective-permute-start.2) | collective-permute-done | bytes 294944 | tf_op jit(solution)/shard_map/ppermute | solution.py:663
  19.0 0.0 collective-permute-done.3.d_ref
  19.0 0.1 shard_map.29
  19.1 3.8 %collective-permute-start.4 = (f32[72,8,128]{2,1,0:T(8,128)S(1)}, f32[72,8,128]{2,1,0:T(8,128)S(1)}, u32[]{:S(2)}, u32[]{:S(2)}) collective-permute-start(f32[72,8,128]{2,1,0:T(8,128)S(1)} %get-tuple-element.35), channel_id=1, source_target_pairs={{0,8},{8,16},{16,24},{24,32},{32,40},{40,48},{48,56},{56,0},{1,9},... | collective-permute-start | bytes 884744 | tf_op jit(solution)/shard_map/ppermute | solution.py:663
  22.8 0.0 collective-permute-start.5
  22.9 0.1 pad_add_fusion.scal
  22.9 3.6 %collective-permute-done.4.yl_ref = f32[72,8,128]{2,1,0:T(8,128)S(1)} collective-permute-done((f32[72,8,128]{2,1,0:T(8,128)S(1)}, f32[72,8,128]{2,1,0:T(8,128)S(1)}, u32[]{:S(2)}, u32[]{:S(2)}) %collective-permute-start.4) | collective-permute-done | bytes 294944 | tf_op jit(solution)/shard_map/ppermute | solution.py:663
  26.5 2.5 %collective-permute-done.5.yr_ref = f32[72,8,128]{2,1,0:T(8,128)S(1)} collective-permute-done((f32[72,8,128]{2,1,0:T(8,128)S(1)}, f32[72,8,128]{2,1,0:T(8,128)S(1)}, u32[]{:S(2)}, u32[]{:S(2)}) %collective-permute-start.5) | collective-permute-done | bytes 294944 | tf_op jit(solution)/shard_map/ppermute | solution.py:663
  29.0 9.8 %shard_map.30 = (f32[8,2,8,128]{3,2,1,0:T(8,128)S(1)}, f32[4,2,8,128]{3,2,1,0:T(8,128)S(1)}, f32[4,2,8,128]{3,2,1,0:T(8,128)S(1)}, f32[32,2,24,128]{3,2,1,0:T(8,...) custom-call(s32[3]{0:T(128)S(1)} %pad_add_fusion.scal, ...), custom_call_target="tpu_custom_call" | custom-call | tf_op jit(solution)/shard_map/pallas_call | solution.py:651
  38.7 0.1 collective-permute-start.6
  38.8 2.8 %collective-permute-start.7 = (f32[4,2,8,128]{3,2,1,0:T(8,128)S(1)}, f32[4,2,8,128]{3,2,1,0:T(8,128)S(1)}, u32[]{:S(2)}, u32[]{:S(2)}) collective-permute-start(f32[4,2,8,128]{3,2,1,0:T(8,128)S(1)} %get-tuple-element.44), channel_id=1, source_target_pairs={{0,7},{1,0},{2,1},{3,2},{4,3},{5,4},{6,5},{7,6},{8,15},{9,8},{10,9... | collective-permute-start | bytes 98312 | tf_op jit(solution)/shard_map/ppermute | solution.py:663
  41.6 1.2 %collective-permute-done.6 = f32[4,2,8,128]{3,2,1,0:T(8,128)S(1)} collective-permute-done((f32[4,2,8,128]{3,2,1,0:T(8,128)S(1)}, f32[4,2,8,128]{3,2,1,0:T(8,128)S(1)}, u32[]{:S(2)}, u32[]{:S(2)}) %collective-permute-start.6) | collective-permute-done | bytes 32800 | tf_op jit(solution)/shard_map/ppermute | solution.py:663
  42.9 0.0 collective-permute-done.7
  42.9 1.3 %collective-permute-start.8 = (f32[16,2,8,128]{3,2,1,0:T(8,128)S(1)}, f32[16,2,8,128]{3,2,1,0:T(8,128)S(1)}, u32[]{:S(2)}, u32[]{:S(2)}) collective-permute-start(f32[16,2,8,128]{3,2,1,0:T(8,128)S(1)} %get-tuple-element.59), channel_id=1, source_target_pairs={{0,64},{64,128},{128,192},{192,0},{1,65},{65,129},{129,193},{193,1... | collective-permute-start | bytes 393224 | tf_op jit(solution)/shard_map/ppermute | solution.py:663
  44.2 2.6 %collective-permute-start.9 = (f32[16,2,8,128]{3,2,1,0:T(8,128)S(1)}, f32[16,2,8,128]{3,2,1,0:T(8,128)S(1)}, u32[]{:S(2)}, u32[]{:S(2)}) collective-permute-start(f32[16,2,8,128]{3,2,1,0:T(8,128)S(1)} %get-tuple-element.59), channel_id=1, source_target_pairs={{0,128},{64,192},{128,0},{192,64},{1,129},{65,193},{129,1},{193,65... | collective-permute-start | bytes 393224 | tf_op jit(solution)/shard_map/ppermute | solution.py:663
  46.8 0.7 collective-permute-start.10
  47.5 0.5 collective-permute-done.8
  48.0 3.7 %collective-permute-done.9 = f32[16,2,8,128]{3,2,1,0:T(8,128)S(1)} collective-permute-done((f32[16,2,8,128]{3,2,1,0:T(8,128)S(1)}, f32[16,2,8,128]{3,2,1,0:T(8,128)S(1)}, u32[]{:S(2)}, u32[]{:S(2)}) %collective-permute-start.9) | collective-permute-done | bytes 131104 | tf_op jit(solution)/shard_map/ppermute | solution.py:663
  51.8 0.6 collective-permute-done.10
  52.3 1.8 %collective-permute-start.12 = (f32[64,2,8,128]{3,2,1,0:T(8,128)S(1)}, f32[64,2,8,128]{3,2,1,0:T(8,128)S(1)}, u32[]{:S(2)}, u32[]{:S(2)}) collective-permute-start(f32[64,2,8,128]{3,2,1,0:T(8,128)S(1)} %constant_dynamic-update-slice_fusion.3.own_ref), channel_id=1, source_target_pairs={{0,56},{8,0},{16,8},{24,16},{32,24},{40,32},{48,40},{56,48},{1,57}... | collective-permute-start | bytes 1572872 | tf_op jit(solution)/shard_map/ppermute | solution.py:663
  54.1 1.2 %collective-permute-start.11 = (f32[64,2,8,128]{3,2,1,0:T(8,128)S(1)}, f32[64,2,8,128]{3,2,1,0:T(8,128)S(1)}, u32[]{:S(2)}, u32[]{:S(2)}) collective-permute-start(f32[64,2,8,128]{3,2,1,0:T(8,128)S(1)} %constant_dynamic-update-slice_fusion.3.own_ref), channel_id=1, source_target_pairs={{0,8},{8,16},{16,24},{24,32},{32,40},{40,48},{48,56},{56,0},{1,9},... | collective-permute-start | bytes 1572872 | tf_op jit(solution)/shard_map/ppermute | solution.py:663
  55.3 7.1 %collective-permute-done.12.yr_ref = f32[64,2,8,128]{3,2,1,0:T(8,128)S(1)} collective-permute-done((f32[64,2,8,128]{3,2,1,0:T(8,128)S(1)}, f32[64,2,8,128]{3,2,1,0:T(8,128)S(1)}, u32[]{:S(2)}, u32[]{:S(2)}) %collective-permute-start.12) | collective-permute-done | bytes 524320 | tf_op jit(solution)/shard_map/ppermute | solution.py:663
  62.5 0.0 collective-permute-done.11.yl_ref
  62.5 7.1 %shard_map.31 = (f32[16,8,128]{2,1,0:T(8,128)S(1)}, f32[16,2,24,128]{3,2,1,0:T(8,128)S(1)}, f32[6,16,2,24,128]{4,3,2,1,0:T(8,128)S(1)}, f32[6,16,2,24,128]{4,3,2...) custom-call(s32[3]{0:T(128)S(1)} %pad_add_fusion.scal, ...), custom_call_target="tpu_custom_call" | custom-call | tf_op jit(solution)/shard_map/pallas_call | solution.py:651
  69.6 3.5 %collective-permute-start.15 = (f32[1,16,8,128]{3,2,1,0:T(8,128)S(1)}, f32[1,16,8,128]{3,2,1,0:T(8,128)S(1)}, u32[]{:S(2)}, u32[]{:S(2)}) collective-permute-start(f32[1,16,8,128]{3,2,1,0:T(8,128)S(1)} %bitcast.6), channel_id=1, source_target_pairs={{0,48},{8,56},{16,0},{24,8},{32,16},{40,24},{48,32},{56,40},{1,49}... | collective-permute-start | bytes 196616 | tf_op jit(solution)/shard_map/ppermute | solution.py:663
  73.1 0.0 collective-permute-start.14
  73.1 0.7 collective-permute-start.13
  73.7 0.7 collective-permute-done.15
  74.4 3.4 %collective-permute-done.14 = f32[1,16,8,128]{3,2,1,0:T(8,128)S(1)} collective-permute-done((f32[1,16,8,128]{3,2,1,0:T(8,128)S(1)}, f32[1,16,8,128]{3,2,1,0:T(8,128)S(1)}, u32[]{:S(2)}, u32[]{:S(2)}) %collective-permute-start.14) | collective-permute-done | bytes 65568 | tf_op jit(solution)/shard_map/ppermute | solution.py:663
  77.8 0.8 collective-permute-done.13
  78.6 3.7 %all-gather = f32[8,16,8,128]{3,2,1,0:T(8,128)S(1)} all-gather(f32[4,16,8,128]{3,2,1,0:T(8,128)S(1)} %pad_maximum_fusion.2), channel_id=2, replica_groups={{0,8},{16,24},{32,40},{48,56},{1,9},{17,25},{33,41},{49,57},{2,10},{18,..., dimensions={0}, use_global_device_ids=true | all-gather | bytes 786432 | tf_op jit(solution)/shard_map/all_gather | solution.py:697
  82.3 3.3 %shard_map.32 = (f32[8,8,8,128]{3,2,1,0:T(8,128)S(1)}, f32[16,2,8,128]{3,2,1,0:T(8,128)S(1)}, f32[6,16,2,8,128]{4,3,2,1,0:T(8,128)S(1)}, f32[6,16,2,8,128]{4,3,2...) custom-call(s32[3]{0:T(128)S(1)} %pad_add_fusion.scal, f32[2,4,16,8,128]{4,3,2,1,0:T(8,128)S(1)} %bitcast.5), custom_call_target="tpu_custom_call" | custom-call | tf_op jit(solution)/shard_map/pallas_call | solution.py:651
  85.6 16.1 %all_to_all.5.in_ref = f32[8,8,8,128]{3,2,1,0:T(8,128)S(1)} all-to-all(f32[8,8,8,128]{3,2,1,0:T(8,128)S(1)} %get-tuple-element.56), channel_id=1, replica_groups=mesh['gx'=4,'gy'=8,'gz'=8] {'gz'}, dimensions={0} | all-to-all | bytes 524288 | tf_op jit(solution)/shard_map/all_to_all | solution.py:704
  101.7 7.6 %shard_map.33.add_ref = f32[8,8,128]{2,1,0:T(8,128)S(1)} custom-call(s32[3]{0:T(128)S(1)} %pad_add_fusion.scal, f32[8,8,8,128]{3,2,1,0:T(8,128)S(1)} %all_to_all.5.in_ref), custom_call_target="tpu_custom_call" | custom-call | tf_op jit(solution)/shard_map/pallas_call | solution.py:651
  109.2 1.9 %shard_map.34.add_ref = f32[8,24,128]{2,1,0:T(8,128)S(1)} custom-call(s32[3]{0:T(128)S(1)} %pad_add_fusion.scal, f32[16,2,8,128]{3,2,1,0:T(8,128)S(1)} %get-tuple-element.51.black_ref, f32[6,16,2,8,128]{4,3,2,1,0:T(8,128)S(1)} %get-tuple-element.52.wd0, f32[6,16,2,8,128]{4,3,2,1,0:T(8,128)S(1)} %get-tuple-element.53.wd1, ...), custom_call_target="tpu_custom_call" | custom-call | tf_op jit(solution)/shard_map/pallas_call | solution.py:651
  111.2 3.4 %shard_map.35.add_ref = f32[16,24,128]{2,1,0:T(8,128)S(1)} custom-call(s32[3]{0:T(128)S(1)} %pad_add_fusion.scal, f32[16,2,24,128]{3,2,1,0:T(8,128)S(1)} %get-tuple-element.45.black_ref, f32[6,16,2,24,128]{4,3,2,1,0:T(8,128)S(1)} %get-tuple-element.46.wd0, f32[6,16,2,24,128]{4,3,2,1,0:T(8,128)S(1)} %get-tuple-element.47.wd1, ...), custom_call_target="tpu_custom_call" | custom-call | tf_op jit(solution)/shard_map/pallas_call | solution.py:651
  114.6 3.1 %shard_map.36 = f32[16,32,128]{2,1,0:T(8,128)} custom-call(f32[32,2,24,128]{3,2,1,0:T(8,128)S(1)} %get-tuple-element.37.black_ref, f32[6,32,2,24,128]{4,3,2,1,0:T(8,128)S(1)} %get-tuple-element.38.wd0, f32[6,32,2,24,128]{4,3,2,1,0:T(8,128)S(1)} %get-tuple-element.39.wd1, f32[32,2,24,128]{3,2,1,0:T(8,128)S(1)} %get-tuple-element.40.fd0, ...), custom_call_target="tpu_custom_call" | custom-call | tf_op jit(solution)/shard_map/pallas_call | solution.py:651
  (11 shorter events, 0.1 us)
Async XLA Ops:
  0.0 0.9 copy-start
  1.0 0.9 copy-start.1
  2.9 7.8 %collective-permute-start = (f32[2,2,16,128]{3,2,1,0:T(8,128)S(1)}, f32[2,2,16,128]{3,2,1,0:T(8,128)S(1)}, u32[]{:S(2)}, u32[]{:S(2)}) collective-permute-start(f32[2,2,16,128]{3,2,1,0:T(8,128)S(1)} %get-tuple-element.32), channel_id=1, source_target_pairs={{0,1},{1,2},{2,3},{3,4},{4,5},{5,6},{6,7},{7,0},{8,9},{9,10},{10,1... | collective-permute-start | bytes 98312 | tf_op jit(solution)/shard_map/ppermute | solution.py:663
  5.5 5.2 %collective-permute-start.1 = (f32[2,2,16,128]{3,2,1,0:T(8,128)S(1)}, f32[2,2,16,128]{3,2,1,0:T(8,128)S(1)}, u32[]{:S(2)}, u32[]{:S(2)}) collective-permute-start(f32[2,2,16,128]{3,2,1,0:T(8,128)S(1)} %get-tuple-element.33), channel_id=1, source_target_pairs={{0,7},{1,0},{2,1},{3,2},{4,3},{5,4},{6,5},{7,6},{8,15},{9,8},{10,9... | collective-permute-start | bytes 98312 | tf_op jit(solution)/shard_map/ppermute | solution.py:663
  10.8 8.2 %collective-permute-start.2 = (f32[18,2,16,128]{3,2,1,0:T(8,128)S(1)}, f32[18,2,16,128]{3,2,1,0:T(8,128)S(1)}, u32[]{:S(2)}, u32[]{:S(2)}) collective-permute-start(f32[18,2,16,128]{3,2,1,0:T(8,128)S(1)} %pad_maximum_fusion.c_ref), channel_id=1, source_target_pairs={{0,64},{64,128},{128,192},{192,0},{1,65},{65,129},{129,193},{193,1... | collective-permute-start | bytes 884744 | tf_op jit(solution)/shard_map/ppermute | solution.py:663
  12.1 6.9 %collective-permute-start.3 = (f32[18,2,16,128]{3,2,1,0:T(8,128)S(1)}, f32[18,2,16,128]{3,2,1,0:T(8,128)S(1)}, u32[]{:S(2)}, u32[]{:S(2)}) collective-permute-start(f32[18,2,16,128]{3,2,1,0:T(8,128)S(1)} %pad_maximum_fusion.1.b_ref), channel_id=1, source_target_pairs={{0,192},{64,0},{128,64},{192,128},{1,193},{65,1},{129,65},{193,129... | collective-permute-start | bytes 884744 | tf_op jit(solution)/shard_map/ppermute | solution.py:663
  19.1 7.4 %collective-permute-start.4 = (f32[72,8,128]{2,1,0:T(8,128)S(1)}, f32[72,8,128]{2,1,0:T(8,128)S(1)}, u32[]{:S(2)}, u32[]{:S(2)}) collective-permute-start(f32[72,8,128]{2,1,0:T(8,128)S(1)} %get-tuple-element.35), channel_id=1, source_target_pairs={{0,8},{8,16},{16,24},{24,32},{32,40},{40,48},{48,56},{56,0},{1,9},... | collective-permute-start | bytes 884744 | tf_op jit(solution)/shard_map/ppermute | solution.py:663
  22.8 6.1 %collective-permute-start.5 = (f32[72,8,128]{2,1,0:T(8,128)S(1)}, f32[72,8,128]{2,1,0:T(8,128)S(1)}, u32[]{:S(2)}, u32[]{:S(2)}) collective-permute-start(f32[72,8,128]{2,1,0:T(8,128)S(1)} %get-tuple-element.36), channel_id=1, source_target_pairs={{0,56},{8,0},{16,8},{24,16},{32,24},{40,32},{48,40},{56,48},{1,57}... | collective-permute-start | bytes 884744 | tf_op jit(solution)/shard_map/ppermute | solution.py:663
  38.7 4.1 %collective-permute-start.6 = (f32[4,2,8,128]{3,2,1,0:T(8,128)S(1)}, f32[4,2,8,128]{3,2,1,0:T(8,128)S(1)}, u32[]{:S(2)}, u32[]{:S(2)}) collective-permute-start(f32[4,2,8,128]{3,2,1,0:T(8,128)S(1)} %get-tuple-element.43), channel_id=1, source_target_pairs={{0,1},{1,2},{2,3},{3,4},{4,5},{5,6},{6,7},{7,0},{8,9},{9,10},{10,1... | collective-permute-start | bytes 98312 | tf_op jit(solution)/shard_map/ppermute | solution.py:663
  38.8 4.0 %collective-permute-start.7 = (f32[4,2,8,128]{3,2,1,0:T(8,128)S(1)}, f32[4,2,8,128]{3,2,1,0:T(8,128)S(1)}, u32[]{:S(2)}, u32[]{:S(2)}) collective-permute-start(f32[4,2,8,128]{3,2,1,0:T(8,128)S(1)} %get-tuple-element.44), channel_id=1, source_target_pairs={{0,7},{1,0},{2,1},{3,2},{4,3},{5,4},{6,5},{7,6},{8,15},{9,8},{10,9... | collective-permute-start | bytes 98312 | tf_op jit(solution)/shard_map/ppermute | solution.py:663
  42.9 5.1 %collective-permute-start.8 = (f32[16,2,8,128]{3,2,1,0:T(8,128)S(1)}, f32[16,2,8,128]{3,2,1,0:T(8,128)S(1)}, u32[]{:S(2)}, u32[]{:S(2)}) collective-permute-start(f32[16,2,8,128]{3,2,1,0:T(8,128)S(1)} %get-tuple-element.59), channel_id=1, source_target_pairs={{0,64},{64,128},{128,192},{192,0},{1,65},{65,129},{129,193},{193,1... | collective-permute-start | bytes 393224 | tf_op jit(solution)/shard_map/ppermute | solution.py:663
  44.2 7.6 %collective-permute-start.9 = (f32[16,2,8,128]{3,2,1,0:T(8,128)S(1)}, f32[16,2,8,128]{3,2,1,0:T(8,128)S(1)}, u32[]{:S(2)}, u32[]{:S(2)}) collective-permute-start(f32[16,2,8,128]{3,2,1,0:T(8,128)S(1)} %get-tuple-element.59), channel_id=1, source_target_pairs={{0,128},{64,192},{128,0},{192,64},{1,129},{65,193},{129,1},{193,65... | collective-permute-start | bytes 393224 | tf_op jit(solution)/shard_map/ppermute | solution.py:663
  46.8 5.5 %collective-permute-start.10 = (f32[16,2,8,128]{3,2,1,0:T(8,128)S(1)}, f32[16,2,8,128]{3,2,1,0:T(8,128)S(1)}, u32[]{:S(2)}, u32[]{:S(2)}) collective-permute-start(f32[16,2,8,128]{3,2,1,0:T(8,128)S(1)} %get-tuple-element.59), channel_id=1, source_target_pairs={{0,192},{64,0},{128,64},{192,128},{1,193},{65,1},{129,65},{193,129... | collective-permute-start | bytes 393224 | tf_op jit(solution)/shard_map/ppermute | solution.py:663
  52.3 10.1 %collective-permute-start.12 = (f32[64,2,8,128]{3,2,1,0:T(8,128)S(1)}, f32[64,2,8,128]{3,2,1,0:T(8,128)S(1)}, u32[]{:S(2)}, u32[]{:S(2)}) collective-permute-start(f32[64,2,8,128]{3,2,1,0:T(8,128)S(1)} %constant_dynamic-update-slice_fusion.3.own_ref), channel_id=1, source_target_pairs={{0,56},{8,0},{16,8},{24,16},{32,24},{40,32},{48,40},{56,48},{1,57}... | collective-permute-start | bytes 1572872 | tf_op jit(solution)/shard_map/ppermute | solution.py:663
  54.1 8.3 %collective-permute-start.11 = (f32[64,2,8,128]{3,2,1,0:T(8,128)S(1)}, f32[64,2,8,128]{3,2,1,0:T(8,128)S(1)}, u32[]{:S(2)}, u32[]{:S(2)}) collective-permute-start(f32[64,2,8,128]{3,2,1,0:T(8,128)S(1)} %constant_dynamic-update-slice_fusion.3.own_ref), channel_id=1, source_target_pairs={{0,8},{8,16},{16,24},{24,32},{32,40},{40,48},{48,56},{56,0},{1,9},... | collective-permute-start | bytes 1572872 | tf_op jit(solution)/shard_map/ppermute | solution.py:663
  69.6 4.8 %collective-permute-start.15 = (f32[1,16,8,128]{3,2,1,0:T(8,128)S(1)}, f32[1,16,8,128]{3,2,1,0:T(8,128)S(1)}, u32[]{:S(2)}, u32[]{:S(2)}) collective-permute-start(f32[1,16,8,128]{3,2,1,0:T(8,128)S(1)} %bitcast.6), channel_id=1, source_target_pairs={{0,48},{8,56},{16,0},{24,8},{32,16},{40,24},{48,32},{56,40},{1,49}... | collective-permute-start | bytes 196616 | tf_op jit(solution)/shard_map/ppermute | solution.py:663
  73.1 4.7 %collective-permute-start.14 = (f32[1,16,8,128]{3,2,1,0:T(8,128)S(1)}, f32[1,16,8,128]{3,2,1,0:T(8,128)S(1)}, u32[]{:S(2)}, u32[]{:S(2)}) collective-permute-start(f32[1,16,8,128]{3,2,1,0:T(8,128)S(1)} %bitcast.7), channel_id=1, source_target_pairs={{0,32},{8,40},{16,48},{24,56},{32,0},{40,8},{48,16},{56,24},{1,33}... | collective-permute-start | bytes 196616 | tf_op jit(solution)/shard_map/ppermute | solution.py:663
  73.1 5.5 %collective-permute-start.13 = (f32[1,16,8,128]{3,2,1,0:T(8,128)S(1)}, f32[1,16,8,128]{3,2,1,0:T(8,128)S(1)}, u32[]{:S(2)}, u32[]{:S(2)}) collective-permute-start(f32[1,16,8,128]{3,2,1,0:T(8,128)S(1)} %bitcast.8), channel_id=1, source_target_pairs={{0,16},{8,24},{16,32},{24,40},{32,48},{40,56},{48,0},{56,8},{1,17}... | collective-permute-start | bytes 196616 | tf_op jit(solution)/shard_map/ppermute | solution.py:663

commit v2 on v1

--- a/solution.py
+++ b/solution.py
@@ -10,7 +10,7 @@
 SWEEPS = 2
 ITERS = 20
 F32 = jnp.float32
-OFF = 1e30
+OFF = 1e-20
 VMEM = pl.BlockSpec(memory_space=pltpu.VMEM)
 SMEM = pl.BlockSpec(memory_space=pltpu.SMEM)
 
@@ -51,9 +51,7 @@
 
 
 def inverse_of(values):
-    guess = pl.reciprocal(values, approx=True)
-    guess = guess * (2.0 - values * guess)
-    return guess * (2.0 - values * guess)
+    return pl.reciprocal(values, approx=True)
 
 
 def up(level, values):
@@ -125,39 +123,35 @@
 
     def body(x, a, q):
         for colour in (0, 1):
-            own = cond[colour][x, q]
             own_rec = rec[colour][x + 1, q]
             near = beside(level, rec[1 - colour], x, q, colour, a)
-            if level.fold == "y":
+            walls = {}
+            if level.fold == "y" or level is L4:
+                width = level.group if level.fold == "y" else 128
                 if q == 0:
-                    near[3] = jnp.where((row == 0) & (lane < level.group), OFF, near[3])
+                    walls[3] = (row == 0) & (lane < width)
                 else:
-                    near[2] = jnp.where((row == rows - 1) & (lane >= 128 - level.group), OFF, near[2])
-            elif level is L4:
-                if q == 0:
-                    near[3] = jnp.where(row == 0, OFF, near[3])
-                else:
-                    near[2] = jnp.where(row == rows - 1, OFF, near[2])
+                    walls[2] = (row == rows - 1) & (lane >= 128 - width)
             if level.group < 128:
                 end = 0 if goes_back(colour, a, q) else level.group - 1
-                near[5] = jnp.where(lane % level.group == end, OFF, near[5])
+                walls[5] = lane % level.group == end
             total = None
             faces = []
-            for value in near:
-                off = value > 0.5 * OFF
+            for i, value in enumerate(near):
+                if i in walls:
+                    value = jnp.where(walls[i], OFF, value)
                 face = inverse_of(own_rec + value)
-                faces.append(jnp.where(off, 0.0, face))
-                part = jnp.where(off, own, face)
-                total = part if total is None else total + part
-            total = jnp.where(own_rec > 0.5 * OFF, 1.0, total)
-            inverse = inverse_of(total)
+                faces.append(face)
+                total = face if total is None else total + face
+            inverse = jnp.where(own_rec > 1e-10, inverse_of(total), 0.0)
             for i, face in enumerate(faces):
-                wd[colour][i, x, q] = face * inverse
+                weight = face * inverse
+                wd[colour][i, x, q] = jnp.where(walls[i], 0.0, weight) if i in walls else weight
             fd[colour][x, q] = fd[colour][x, q] * (0.5 * inverse)
             if colour == 0:
                 dd[x, q] = total
 
-    planes(0, level.count, 1, body)
+    planes(0, level.count, 4 if level.rows == 8 else 1, body)
 
 
 def relaxed(level, colour, x, a, q, v, wd, fd):
@@ -243,6 +237,22 @@
 def even_odd(v, x, a, q):
     red, black = v[0][x + 1, q], v[1][x + 1, q]
     return (red, black) if (a + q) % 2 == 0 else (black, red)
+
+
+def exchange(blocks, width):
+    group = lanes(8) // width
+    step = len(blocks) // 2
+    while step:
+        swapped = list(blocks)
+        for i in range(len(blocks)):
+            if not i & step:
+                a, b = blocks[i], blocks[i + step]
+                low = group & step == 0
+                swapped[i] = jnp.where(low, a, turn(b, width * step))
+                swapped[i + step] = jnp.where(low, turn(a, -width * step), b)
+        blocks = swapped
+        step //= 2
+    return blocks
 
 
 def split_kernel(f_ref, b_ref, lo_ref, hi_ref, zl_ref, zr_ref):
@@ -268,12 +278,11 @@
 
 
 def edge_kernel(a_ref, b_ref, c_ref, d_ref, lo_ref, hi_ref):
+    low = rows_of(8) < 4
     for t, ref in enumerate((a_ref, b_ref, c_ref, d_ref)):
         for i in range(18):
-            for q in (0, 1):
-                cells = ref[i, q]
-                lo_ref[18 * t + i, 4 * q : 4 * q + 4] = cells[0:4]
-                hi_ref[18 * t + i, 4 - 4 * q : 8 - 4 * q] = cells[12:16]
+            lo_ref[18 * t + i] = jnp.where(low, ref[i, 0, 0:8], pltpu.roll(ref[i, 1, 0:8], 4, 0))
+            hi_ref[18 * t + i] = jnp.where(low, pltpu.roll(ref[i, 1, 8:16], 4, 0), ref[i, 0, 8:16])
 
 
 def level0_down_kernel(
@@ -325,26 +334,53 @@
     descend(L0, v, wd, fd, dd, cond, nat_f, nat_b, [(2, 30), (2, 30), (4, 28), (8, 24)])
     keep_black(L0, v, black_ref)
     lane8 = lanes(8)
-    index = 2 * (lane8 % 32) + (lane8 // 32) % 2
-    group = 32 * ((lane8 % 64) // 16) + lane8 % 16
+    k = lane8 % 64
+    spread = 2 * jnp.clip(k - 16, 0, 31) + lane8 // 64
+    near = 2 * (lane8 % 16) + (lane8 // 16) % 2
     for x in range(0, 8, 2):
         for q in (0, 1):
-            own = []
+            left, right = [], []
             for a in (0, 1):
                 f = nat_f[x + a, pl.ds(q, 8, stride=2), :]
                 b = nat_b[x + a, pl.ds(q, 8, stride=2), :]
-                cells = jnp.where(lane8 < 64, pick(f, index), pick(b, index))
-                own_ref[x + a, q] = cells
-                own.append(cells)
-            left = jnp.where(lane8 < 64, pick(own[0], group), pick(own[1], group))
-            zl_ref[x // 2, q] = turn(left, 48)
-            zr_ref[x // 2, q] = jnp.where(lane8 < 64, pick(own[0], group + 16), pick(own[1], group + 16))
+                own_ref[x + a, q] = pick(f, spread)
+                own_ref[8 + x + a, q] = pick(b, spread)
+                here = lane8 % 64 < 32
+                left.append(jnp.where(here, pick(f, near), pick(b, near)))
+                right.append(jnp.where(here, pick(f, near + 32), pick(b, near + 32)))
+            zl_ref[x // 2, q] = jnp.where(lane8 < 64, left[0], left[1])
+            zr_ref[x // 2, q] = jnp.where(lane8 < 64, right[0], right[1])
+
+
+def widen_kernel(own_ref, left_ref, right_ref, out_ref):
+    lane = lanes(8)
+    k = lane % 64
+    index = lane % 16 + 16 * (lane // 64)
+    for x in range(8):
+        for q in (0, 1):
+            for arr in (0, 1):
+                there = index + 64 * (x % 2) + 32 * arr
+                edge = jnp.where(k < 16, pick(left_ref[x // 2, q], there), pick(right_ref[x // 2, q], there))
+                out_ref[8 * arr + x, q] = jnp.where((k >= 16) & (k < 48), own_ref[8 * arr + x, q], edge)
+
+
+def strip_kernel(a_ref, b_ref, c_ref, d_ref, lo_ref, hi_ref):
+    low = rows_of(8) < 4
+    for t, ref in enumerate((a_ref, b_ref, c_ref, d_ref)):
+        for i in range(16):
+            zero, one = ref[i, 0], ref[i, 1]
+            lo_ref[20 * t + i] = jnp.where(low, zero, pltpu.roll(one, 4, 0))
+            hi_ref[20 * t + i] = jnp.where(low, pltpu.roll(zero, 4, 0), one)
+            for q in (0, 1):
+                row = 2 * (i % 4) + q
+                lo_ref[20 * t + 16 + i // 4, row : row + 1] = ref[i, q, 4:5]
+                hi_ref[20 * t + 16 + i // 4, row : row + 1] = ref[i, q, 3:4]
 
 
 def level1_down_kernel(
-    scal, own_ref, yl_ref, yr_ref,
+    scal, a_ref, b_ref, c_ref, d_ref, yl_ref, yr_ref,
     out_ref, black_ref, wd0, wd1, fd0, fd1,
-    cond0, cond1, rec0, rec1, v0, v1, dd, nat_f, nat_b,
+    cond0, cond1, rec0, rec1, v0, v1, dd, nat_f, nat_b, own,
 ):
     cond, rec, v, wd, fd = (cond0, cond1), (rec0, rec1), (v0, v1), (wd0, wd1), (fd0, fd1)
     gx, gy, gz = scal[0], scal[1], scal[2]
@@ -352,31 +388,37 @@
     k = lane % 64
     inside = ((gz > 0) | (k >= 16)) & ((gz < 7) | (k < 48))
     keep = jnp.where(inside, 1.0, 0.0)
-    for block, ref in enumerate((yl_ref, own_ref, yr_ref)):
+    row = rows_of(8)
+    for i, ref in enumerate((a_ref, b_ref, c_ref, d_ref)):
+        own[i] = ref[...]
+    for block in range(3):
         here = keep
         if block == 0:
-            here = keep * jnp.where(gy > 0, 1.0, 0.0)
+            here = jnp.where(row >= 3, keep, 0.0) * jnp.where(gy > 0, 1.0, 0.0)
         if block == 2:
-            here = keep * jnp.where(gy < 7, 1.0, 0.0)
+            here = jnp.where(row < 5, keep, 0.0) * jnp.where(gy < 7, 1.0, 0.0)
         rows = pl.ds(8 * block, 8)
 
+        def cells_of(slot, i, q):
+            if block == 1:
+                return own[slot, i, q]
+            ref = yl_ref if block == 0 else yr_ref
+            cells = ref[20 * slot + i]
+            if (block == 0) == (q == 0):
+                cells = pltpu.roll(cells, 4, 0)
+            at = 2 * (i % 4) + q
+            single = ref[20 * slot + 16 + i // 4, at : at + 1]
+            return jnp.where(row == (3 if block == 0 else 4), single, cells)
+
         def body(j, carry):
-            slots = [16 * ((gx + 4 - j) % 4), 16 * ((gx + 6 - j) % 4)]
+            slots = [(gx + 4 - j) % 4, (gx + 6 - j) % 4]
             for x in range(8):
                 for q in (0, 1):
                     parts = []
-                    for g in range(4):
-                        far = 64 * (x % 2) + 16 * g
-                        made = []
-                        for h, slot in enumerate(slots):
-                            main = ref[slot + x, q]
-                            from_left = ref[slot + 8 + x // 2, q]
-                            from_right = ref[slot + 12 + x // 2, q]
-                            edge = jnp.where(lane // 16 == far // 16, from_left, from_right)
-                            made.append((turn(main, 64 * h + 16 - 32 * g), turn(edge, 64 * h - far)))
-                        main = jnp.where(lane < 64, made[0][0], made[1][0])
-                        edge = jnp.where(lane < 64, made[0][1], made[1][1])
-                        parts.append(jnp.where((k >= 16) & (k < 48), main, edge))
+                    for arr in (0, 8):
+                        first, second = [cells_of(slot, arr + x, q) for slot in slots]
+                        parts.append(jnp.where(lane < 64, first, turn(second, 64)))
+                        parts.append(jnp.where(lane < 64, turn(first, 64), second))
                     for colour in (0, 1):
                         odd = (x + q + colour) % 2
                         fd[colour][8 * j + x, q, rows] = parts[odd]
@@ -418,67 +460,52 @@
         for slot in slots:
             both = [in_ref[c, slot, x, 4 * q : 4 * q + 4] for c in (0, 1)]
             mains.append(jnp.concatenate(both, axis=0))
-        parts = []
-        for g in range(4):
-            part = turn(mains[0], -32 * g)
-            for j in (1, 2, 3):
-                part = jnp.where(lane // 32 == j, turn(mains[j], 32 * (j - g)), part)
-            parts.append(part)
+        parts = exchange(mains, 32)
         for colour in (0, 1):
             odd = (a + q + colour) % 2
             fd[colour][x, q] = parts[odd]
             cond[colour][x, q] = jnp.where(inside, parts[2 + odd], 0.0)
             rec[colour][x + 1, q] = jnp.where(inside, inverse_of(parts[2 + odd]), OFF)
 
-    planes(0, 16, 2, body)
+    planes(0, 16, 4, body)
     set_up(L2, cond, rec, wd, fd, dd)
     descend(L2, v, wd, fd, dd, cond, nat_f, nat_b)
     keep_black(L2, v, black_ref)
     index = 32 * (lane // 32) + 8 + 2 * (lane % 8) + (lane // 8) % 2
     for x in range(8):
         packed = jnp.where(lane % 32 < 16, pick(nat_f[x], index), pick(nat_b[x], index))
-        for r in range(8):
-            out_ref[r, x] = packed
-
-
-def unfold(ref, x, q, group):
-    cells = ref[x, pl.ds(q, 8, stride=2), :]
-    for j in range(1, 128 // group):
-        more = ref[x, pl.ds(16 * j + q, 8, stride=2), :]
-        cells = jnp.where(lanes(8) // group == j, turn(more, group * j), cells)
-    return cells
+        out_ref[x] = packed
 
 
 def coarse_kernel(
-    scal, in_ref, out_ref,
+    scal, own_ref, pair_ref, far_ref, out_ref,
     cond30, cond31, rec30, rec31, v30, v31, dd3, wd30, wd31, fd30, fd31, nat_f, nat_b,
-    cond40, cond41, rec40, rec41, v40, v41, dd4, wd40, wd41, fd40, fd41, whole, nat4, nat3,
+    cond40, cond41, rec40, rec41, v40, v41, dd4, wd40, wd41, fd40, fd41, slabs, whole, nat4, nat3,
 ):
     cond3, rec3, v3, wd3, fd3 = (cond30, cond31), (rec30, rec31), (v30, v31), (wd30, wd31), (fd30, fd31)
     cond4, rec4, v4, wd4, fd4 = (cond40, cond41), (rec40, rec41), (v40, v41), (wd40, wd41), (fd40, fd41)
     gz = scal[2]
     lane = lanes(8)
 
-    def collect(x, carry):
-        for g in range(4):
-            for mq in range(4):
-                cells = turn(in_ref[0, x], -32 * mq - 8 * g)
-                for r in range(1, 8):
-                    cells = jnp.where(lane // 8 == r, turn(in_ref[r, x], 8 * r - 32 * mq - 8 * g), cells)
-                whole[g, x, 8 * mq : 8 * mq + 8] = cells
-        return carry
-
-    lax.fori_loop(0, 8, collect, 0)
+    slabs[gz] = own_ref[...]
+    slabs[(gz + 4) % 8] = far_ref[...]
+    for j in range(3):
+        slabs[(gz + 7 - j) % 8] = pair_ref[0, j]
+        slabs[(gz + 1 + j) % 8] = pair_ref[1, j]
+
+    for x in range(8):
+        for c, cells in enumerate(exchange([slabs[r, x] for r in range(8)], 8)):
+            whole[c % 4, x, 8 * (c // 4) : 8 * (c // 4) + 8] = cells
 
     def place3(x, a, q):
         for colour in (0, 1):
             odd = (a + q + colour) % 2
-            fd3[colour][x, q] = unfold(whole.at[odd], x, q, 64)
-            cells = unfold(whole.at[2 + odd], x, q, 64)
+            fd3[colour][x, q] = whole[odd, x, pl.ds(q, 8, stride=2), :]
+            cells = whole[2 + odd, x, pl.ds(q, 8, stride=2), :]
             cond3[colour][x, q] = cells
             rec3[colour][x + 1, q] = inverse_of(cells)
 
-    planes(0, 8, 2, place3)
+    planes(0, 8, 4, place3)
     set_up(L3, cond3, rec3, wd3, fd3, dd3)
     descend(L3, v3, wd3, fd3, dd3, cond3, nat_f, nat_b)
     on_grid = lane < 32
@@ -538,7 +565,8 @@
 
     planes(0, 8, 4, add)
     ascend(L3, v3, wd3, fd3)
-    z = jnp.clip(16 * gz - 8 + lane % 32, 0, 127)
+    place = 16 * gz - 8 + lane % 32
+    z = jnp.clip(place, 0, 127)
     index = (z % 2) * 64 + z // 2
     for x in range(8):
         for q in (0, 1):
@@ -550,7 +578,7 @@
         cells = nat3[x, 0:8]
         for j in (1, 2, 3):
             cells = jnp.where(lane // 32 == j, nat3[x, 8 * j : 8 * j + 8], cells)
-        out_ref[x] = cells
+        out_ref[x] = jnp.where(place == z, cells, 0.0)
 
 
 def level2_up_kernel(scal, black_ref, wd0, wd1, fd0, fd1, add_ref, out_ref, v0, v1, nat):
@@ -560,18 +588,18 @@
     ascend(L2, v, wd, fd)
     lane = lanes(8)
     k = lane % 64
-    start = pl.multiple_of(8 * gy, 8)
-    for x in range(16):
-        nat[x, 0:8] = jnp.zeros((8, 128), F32)
-        nat[x, 72:80] = jnp.zeros((8, 128), F32)
+    base = (gy + 1) // 2 - 1
+    groups = [base, base + 1]
 
     def store(x, a, q):
         even, odd = even_odd(v, x, a, q)
-        for mq in range(4):
-            packed = jnp.where(lane < 32, turn(even, -32 * mq), turn(odd, 32 - 32 * mq))
-            nat[x, pl.ds(8 + 16 * mq + q, 8, stride=2), :] = pick(packed, (k % 2) * 32 + k // 2)
-
-    planes(0, 16, 2, store)
+        for i, mq in enumerate(groups):
+            index = 32 * jnp.clip(mq, 0, 3) + k // 2
+            cells = jnp.where(lane % 2 == 0, pick(even, index), pick(odd, index))
+            nat[x, pl.ds(16 * i + q, 8, stride=2), :] = jnp.where((mq >= 0) & (mq < 4), cells, 0.0)
+
+    planes(0, 16, 4, store)
+    start = pl.multiple_of(8 - 8 * (gy % 2), 8)
     side = lanes(24) < 64
     for x in range(8):
         out_ref[x] = jnp.where(side, nat[x, pl.ds(start, 24), :], nat[8 + x, pl.ds(start, 24), :])
@@ -584,27 +612,25 @@
     ascend(L1, v, wd, fd)
     lane = lanes(24)
     z = jnp.where(lane < 96, lane, lane - 128) + 32
-    index = (z % 2) * 64 + jnp.clip(z // 2, 0, 63)
-    for x in range(4):
-        nat[x] = jnp.zeros((48, 128), F32)
-        nat[36 + x] = jnp.zeros((48, 128), F32)
-
-    def store(x, a, q):
-        even, odd = even_odd(v, x, a, q)
-        first = jnp.where(lane < 64, even, turn(odd, 64))
-        second = jnp.where(lane < 64, turn(even, 64), odd)
-        nat[x + 4, pl.ds(q, 24, stride=2), :] = pick(first, index)
-        nat[x + 20, pl.ds(q, 24, stride=2), :] = pick(second, index)
-
-    planes(0, 16, 2, store)
-
-    def hand_on(x, carry):
-        out_ref[x, 0:16] = nat[8 * gx + x, 16:32]
-        out_ref[x, 16:20] = nat[8 * gx + x, 32:36]
-        out_ref[x, 20:24] = nat[8 * gx + x, 12:16]
+    index = jnp.clip(z // 2, 0, 63)
+
+    def store(i, carry):
+        for u in range(4):
+            x = 8 * gx - 4 + 4 * i + u
+            inside = (x >= 0) & (x < 32)
+            x = jnp.clip(x, 0, 31)
+            there = 64 * (x // 16) + index
+            for q in (0, 1):
+                even, odd = even_odd(v, x % 16, u, q)
+                cells = jnp.where(lane % 2 == 0, pick(even, there), pick(odd, there))
+                nat[4 * i + u, pl.ds(q, 24, stride=2), :] = jnp.where(inside, cells, 0.0)
         return carry
 
-    lax.fori_loop(0, 16, hand_on, 0)
+    lax.fori_loop(0, 4, store, 0)
+    for x in range(16):
+        out_ref[x, 0:16] = nat[x, 16:32]
+        out_ref[x, 16:20] = nat[x, 32:36]
+        out_ref[x, 20:24] = nat[x, 12:16]
 
 
 def level0_up_kernel(black_ref, wd0, wd1, fd0, fd1, add_ref, out_ref, v0, v1):
@@ -661,6 +687,20 @@
 def ring(values, axis, step):
     count = lax.axis_size(axis)
     return lax.ppermute(values, axis, [(i, (i + step) % count) for i in range(count)])
+
+
+def both_cores(values):
+    count = lax.axis_size("gy")
+    return lax.all_gather(values, "gy", axis=0, axis_index_groups=[[i, i + 1] for i in range(0, count, 2)])
+
+
+def along_z(values, step):
+    rows, count = lax.axis_size("gy"), lax.axis_size("gz")
+    pairs = []
+    for i in range(rows):
+        for k in range(count):
+            pairs.append((i * count + k, i * count + (k + (-step if i % 2 else step)) % count))
+    return lax.ppermute(values, ("gy", "gz"), pairs)
 
 
 def on_device(right_side, coefficient):
@@ -677,47 +717,48 @@
     from_left, from_right = ring(yr, "gy", 1), ring(yl, "gy", -1)
     own, zl, zr, black0, *set0 = call(
         level0_down_kernel,
-        [arr(8, 2, 8, 128), arr(4, 2, 8, 128), arr(4, 2, 8, 128), arr(*L0.own())]
+        [arr(16, 2, 8, 128), arr(4, 2, 8, 128), arr(4, 2, 8, 128), arr(*L0.own())]
         + [arr(*s) for s in weights(L0)],
         level_scratch(L0) + nat_scratch(L0, 8),
         *bundles, from_left, from_right, scal=scal,
     )
     from_left, from_right = ring(zr, "gz", 1), ring(zl, "gz", -1)
-    bundle = jnp.concatenate([own, from_left, from_right])
-    column = jnp.concatenate([bundle] + [ring(bundle, "gx", s) for s in (1, 2, 3)])
-    from_left, from_right = ring(column, "gy", 1), ring(column, "gy", -1)
+    bundle = call(widen_kernel, arr(16, 2, 8, 128), [], own, from_left, from_right)
+    column = [bundle] + [ring(bundle, "gx", s) for s in (1, 2, 3)]
+    yl, yr = call(strip_kernel, [arr(80, 8, 128)] * 2, [], *column)
     own, black1, *set1 = call(
         level1_down_kernel,
         [arr(16, 8, 128), arr(*L1.own())] + [arr(*s) for s in weights(L1)],
-        level_scratch(L1) + nat_scratch(L1),
-        column, from_left, from_right, scal=scal,
+        level_scratch(L1) + nat_scratch(L1) + [scratch(4, 16, 2, 8, 128)],
+        *column, ring(yr, "gy", 1), ring(yl, "gy", -1), scal=scal,
     )
     own = own[None]
     sheet = jnp.concatenate([own] + [ring(own, "gy", 2 * s) for s in (1, 2, 3)])
-    sheet = lax.all_gather(sheet, "gy", axis=0, axis_index_groups=[[0, 1], [2, 3], [4, 5], [6, 7]])
+    sheet = both_cores(sheet)
     own, black2, *set2 = call(
         level2_down_kernel,
-        [arr(8, 8, 8, 128), arr(*L2.own())] + [arr(*s) for s in weights(L2)],
+        [arr(8, 8, 128), arr(*L2.own())] + [arr(*s) for s in weights(L2)],
         level_scratch(L2) + nat_scratch(L2),
         sheet, scal=scal,
     )
-    whole = lax.all_to_all(own, "gz", 0, 0, tiled=True)
+    far = along_z(own, 4)
+    near = both_cores(jnp.stack([along_z(own, s) for s in (1, 2, 3)]))
     correction = call(
         coarse_kernel,
         arr(8, 8, 128),
         level_scratch(L3) + [scratch(*s) for s in weights(L3)] + nat_scratch(L3)
         + level_scratch(L4) + [scratch(*s) for s in weights(L4)]
-        + [scratch(4, 8, 32, 128), scratch(4, 16, 128), scratch(8, 32, 128)],
-        whole, scal=scal,
+        + [scratch(8, 8, 8, 128), scratch(4, 8, 16, 128), scratch(4, 16, 128), scratch(8, 32, 128)],
+        own, near, far, scal=scal,
     )
     correction = call(
         level2_up_kernel, arr(8, 24, 128),
-        [scratch(*L2.wide())] * 2 + [scratch(16, 80, 128)],
+        [scratch(*L2.wide())] * 2 + [scratch(16, 32, 128)],
         black2, *set2, correction, scal=scal,
     )
     correction = call(
         level1_up_kernel, arr(16, 24, 128),
-        [scratch(*L1.wide())] * 2 + [scratch(40, 48, 128)],
+        [scratch(*L1.wide())] * 2 + [scratch(16, 48, 128)],
         black1, *set1, correction, scal=scal,
     )
     return call(

time: 118 us -> 107 us (0.907)
  blocking collectives: 19.8 us -> 5.41 us
  Pallas kernels: 37.2 us -> 28.3 us
  waiting for transfers between devices: 30.7 us -> 37.3 us
  starting transfers between devices: 27.8 us -> 33.7 us
    all_to_all x1 -> x0, blocking collectives: 16.1 us -> none  [on_device(): whole = lax.all_to_all(own, 'gz', 0, 0, tiled=True)]
    pallas_call x9 -> x11, Pallas kernels: 37.2 us -> 28.3 us  [call(): pl.pallas_call(kernel, out_shape=outs, in_specs=specs, out_specs=jax.tree...]
    ppermute x0 -> x4, starting transfers between devices: none -> 8.41 us  [along_z(): return lax.ppermute(values, ('gy', 'gz'), pairs)]
    ppermute x16, waiting for transfers between devices: 30.7 us -> 34.6 us  [ring(): lax.ppermute(values, axis, [(i, (i + step) % count) for i in range(count)])]
    ppermute x0 -> x4, waiting for transfers between devices: none -> 2.7 us  [along_z(): return lax.ppermute(values, ('gy', 'gz'), pairs)]
    ppermute x16, starting transfers between devices: 27.8 us -> 25.3 us  [ring(): lax.ppermute(values, axis, [(i, (i + step) % count) for i in range(count)])]
    all_gather x1 -> x2, blocking collectives: 3.73 us -> 5.41 us  [both_cores(): lax.all_gather(values, 'gy', axis=0, axis_index_groups=[[i, i + 1] for i...]
  transfers between devices with their start and end apart: 16 -> 20, of which waited for: 12 -> 15; matrix products, arithmetic and copies ran while one was open for 0% -> 0% of each run, Pallas kernels for 0% -> 0%
where the time goes in v2:
time: 107 us
  waiting for transfers between devices  37.3 us (35%)
  starting transfers between devices  33.7 us (31%)
  Pallas kernels  28.3 us (26%)
  blocking collectives  5.41 us (5%)
  local copies, waits for them, and re-layouts  1.91 us (2%)
    ppermute x16, waiting for transfers between devices, ring(): lax.ppermute(values, axis, [(i, (i + step) % count) for i in range(count)])  34.6 us
    pallas_call x11, Pallas kernels, call(): pl.pallas_call(kernel, out_shape=outs, in_specs=specs, out_specs=jax.tree...  28.3 us
    ppermute x16, starting transfers between devices, ring(): lax.ppermute(values, axis, [(i, (i + step) % count) for i in range(count)])  25.3 us
    ppermute x4, starting transfers between devices, along_z(): return lax.ppermute(values, ('gy', 'gz'), pairs)  8.41 us
    all_gather x2, blocking collectives, both_cores(): lax.all_gather(values, 'gy', axis=0, axis_index_groups=[[i, i + 1] for i...  5.41 us
    ppermute x4, waiting for transfers between devices, along_z(): return lax.ppermute(values, ('gy', 'gz'), pairs)  2.7 us
  transfers between devices with their start and end apart: 20, of which 15 were waited for; matrix products, arithmetic and copies ran while one was open for 0% of the time, Pallas kernels for 0%

profile of v2, /device:TPU:1, one launch (start us, length us, event | category | flops | bytes accessed | tf_op | source)
XLA Modules:
  0.0 106.9 jit_solution(2134937374377016248)
XLA Ops:
  0.0 0.0 copy-start
  0.0 0.9 copy-done
  1.0 0.0 copy-start.1
  1.0 0.9 copy-done.1
  1.9 1.0 shard_map.28
  2.9 2.5 %collective-permute-start = (f32[2,2,16,128]{3,2,1,0:T(8,128)S(1)}, f32[2,2,16,128]{3,2,1,0:T(8,128)S(1)}, u32[]{:S(2)}, u32[]{:S(2)}) collective-permute-start(f32[2,2,16,128]{3,2,1,0:T(8,128)S(1)} %get-tuple-element.34), channel_id=1, source_target_pairs={{0,1},{1,2},{2,3},{3,4},{4,5},{5,6},{6,7},{7,0},{8,9},{9,10},{10,1... | collective-permute-start | bytes 98312 | tf_op jit(solution)/shard_map/ppermute | solution.py:689
  5.5 4.0 %collective-permute-start.1 = (f32[2,2,16,128]{3,2,1,0:T(8,128)S(1)}, f32[2,2,16,128]{3,2,1,0:T(8,128)S(1)}, u32[]{:S(2)}, u32[]{:S(2)}) collective-permute-start(f32[2,2,16,128]{3,2,1,0:T(8,128)S(1)} %get-tuple-element.35), channel_id=1, source_target_pairs={{0,7},{1,0},{2,1},{3,2},{4,3},{5,4},{6,5},{7,6},{8,15},{9,8},{10,9... | collective-permute-start | bytes 98312 | tf_op jit(solution)/shard_map/ppermute | solution.py:689
  9.5 1.2 %collective-permute-done = f32[2,2,16,128]{3,2,1,0:T(8,128)S(1)} collective-permute-done((f32[2,2,16,128]{3,2,1,0:T(8,128)S(1)}, f32[2,2,16,128]{3,2,1,0:T(8,128)S(1)}, u32[]{:S(2)}, u32[]{:S(2)}) %collective-permute-start) | collective-permute-done | bytes 32800 | tf_op jit(solution)/shard_map/ppermute | solution.py:689
  10.7 0.0 collective-permute-done.1
  10.8 1.3 %collective-permute-start.2 = (f32[18,2,16,128]{3,2,1,0:T(8,128)S(1)}, f32[18,2,16,128]{3,2,1,0:T(8,128)S(1)}, u32[]{:S(2)}, u32[]{:S(2)}) collective-permute-start(f32[18,2,16,128]{3,2,1,0:T(8,128)S(1)} %pad_maximum_fusion.c_ref), channel_id=1, source_target_pairs={{0,64},{64,128},{128,192},{192,0},{1,65},{65,129},{129,193},{193,1... | collective-permute-start | bytes 884744 | tf_op jit(solution)/shard_map/ppermute | solution.py:689
  12.1 1.5 %collective-permute-start.3 = (f32[18,2,16,128]{3,2,1,0:T(8,128)S(1)}, f32[18,2,16,128]{3,2,1,0:T(8,128)S(1)}, u32[]{:S(2)}, u32[]{:S(2)}) collective-permute-start(f32[18,2,16,128]{3,2,1,0:T(8,128)S(1)} %pad_maximum_fusion.1.b_ref), channel_id=1, source_target_pairs={{0,192},{64,0},{128,64},{192,128},{1,193},{65,1},{129,65},{193,129... | collective-permute-start | bytes 884744 | tf_op jit(solution)/shard_map/ppermute | solution.py:689
  13.6 5.4 %collective-permute-done.2.a_ref = f32[18,2,16,128]{3,2,1,0:T(8,128)S(1)} collective-permute-done((f32[18,2,16,128]{3,2,1,0:T(8,128)S(1)}, f32[18,2,16,128]{3,2,1,0:T(8,128)S(1)}, u32[]{:S(2)}, u32[]{:S(2)}) %collective-permute-start.2) | collective-permute-done | bytes 294944 | tf_op jit(solution)/shard_map/ppermute | solution.py:689
  19.0 0.0 collective-permute-done.3.d_ref
  19.0 0.1 shard_map.29
  19.1 3.8 %collective-permute-start.4 = (f32[72,8,128]{2,1,0:T(8,128)S(1)}, f32[72,8,128]{2,1,0:T(8,128)S(1)}, u32[]{:S(2)}, u32[]{:S(2)}) collective-permute-start(f32[72,8,128]{2,1,0:T(8,128)S(1)} %get-tuple-element.37), channel_id=1, source_target_pairs={{0,8},{8,16},{16,24},{24,32},{32,40},{40,48},{48,56},{56,0},{1,9},... | collective-permute-start | bytes 884744 | tf_op jit(solution)/shard_map/ppermute | solution.py:689
  22.8 0.0 collective-permute-start.5
  22.8 0.1 pad_add_fusion.scal
  22.9 3.6 %collective-permute-done.4.yl_ref = f32[72,8,128]{2,1,0:T(8,128)S(1)} collective-permute-done((f32[72,8,128]{2,1,0:T(8,128)S(1)}, f32[72,8,128]{2,1,0:T(8,128)S(1)}, u32[]{:S(2)}, u32[]{:S(2)}) %collective-permute-start.4) | collective-permute-done | bytes 294944 | tf_op jit(solution)/shard_map/ppermute | solution.py:689
  26.5 2.5 %collective-permute-done.5.yr_ref = f32[72,8,128]{2,1,0:T(8,128)S(1)} collective-permute-done((f32[72,8,128]{2,1,0:T(8,128)S(1)}, f32[72,8,128]{2,1,0:T(8,128)S(1)}, u32[]{:S(2)}, u32[]{:S(2)}) %collective-permute-start.5) | collective-permute-done | bytes 294944 | tf_op jit(solution)/shard_map/ppermute | solution.py:689
  29.0 6.8 %shard_map.30 = (f32[16,2,8,128]{3,2,1,0:T(8,128)S(1)}, f32[4,2,8,128]{3,2,1,0:T(8,128)S(1)}, f32[4,2,8,128]{3,2,1,0:T(8,128)S(1)}, f32[32,2,24,128]{3,2,1,0:T(8...) custom-call(s32[3]{0:T(128)S(1)} %pad_add_fusion.scal, ...), custom_call_target="tpu_custom_call" | custom-call | tf_op jit(solution)/shard_map/pallas_call | solution.py:677
  35.8 0.1 collective-permute-start.6
  35.9 2.8 %collective-permute-start.7 = (f32[4,2,8,128]{3,2,1,0:T(8,128)S(1)}, f32[4,2,8,128]{3,2,1,0:T(8,128)S(1)}, u32[]{:S(2)}, u32[]{:S(2)}) collective-permute-start(f32[4,2,8,128]{3,2,1,0:T(8,128)S(1)} %get-tuple-element.46), channel_id=1, source_target_pairs={{0,7},{1,0},{2,1},{3,2},{4,3},{5,4},{6,5},{7,6},{8,15},{9,8},{10,9... | collective-permute-start | bytes 98312 | tf_op jit(solution)/shard_map/ppermute | solution.py:689
  38.7 1.2 %collective-permute-done.6.left_ref = f32[4,2,8,128]{3,2,1,0:T(8,128)S(1)} collective-permute-done((f32[4,2,8,128]{3,2,1,0:T(8,128)S(1)}, f32[4,2,8,128]{3,2,1,0:T(8,128)S(1)}, u32[]{:S(2)}, u32[]{:S(2)}) %collective-permute-start.6) | collective-permute-done | bytes 32800 | tf_op jit(solution)/shard_map/ppermute | solution.py:689
  40.0 0.0 collective-permute-done.7.right_ref
  40.0 0.2 shard_map.31.a_ref
  40.2 2.8 %collective-permute-start.10 = (f32[16,2,8,128]{3,2,1,0:T(8,128)S(1)}, f32[16,2,8,128]{3,2,1,0:T(8,128)S(1)}, u32[]{:S(2)}, u32[]{:S(2)}) collective-permute-start(f32[16,2,8,128]{3,2,1,0:T(8,128)S(1)} %shard_map.31.a_ref), channel_id=1, source_target_pairs={{0,192},{64,0},{128,64},{192,128},{1,193},{65,1},{129,65},{193,129... | collective-permute-start | bytes 393224 | tf_op jit(solution)/shard_map/ppermute | solution.py:689
  42.9 0.3 collective-permute-start.9
  43.3 0.4 collective-permute-start.8
  43.6 2.5 %collective-permute-done.10.d_ref = f32[16,2,8,128]{3,2,1,0:T(8,128)S(1)} collective-permute-done((f32[16,2,8,128]{3,2,1,0:T(8,128)S(1)}, f32[16,2,8,128]{3,2,1,0:T(8,128)S(1)}, u32[]{:S(2)}, u32[]{:S(2)}) %collective-permute-start.10) | collective-permute-done | bytes 131104 | tf_op jit(solution)/shard_map/ppermute | solution.py:689
  46.1 2.3 %collective-permute-done.9.c_ref = f32[16,2,8,128]{3,2,1,0:T(8,128)S(1)} collective-permute-done((f32[16,2,8,128]{3,2,1,0:T(8,128)S(1)}, f32[16,2,8,128]{3,2,1,0:T(8,128)S(1)}, u32[]{:S(2)}, u32[]{:S(2)}) %collective-permute-start.9) | collective-permute-done | bytes 131104 | tf_op jit(solution)/shard_map/ppermute | solution.py:689
  48.4 3.7 %collective-permute-done.8.b_ref = f32[16,2,8,128]{3,2,1,0:T(8,128)S(1)} collective-permute-done((f32[16,2,8,128]{3,2,1,0:T(8,128)S(1)}, f32[16,2,8,128]{3,2,1,0:T(8,128)S(1)}, u32[]{:S(2)}, u32[]{:S(2)}) %collective-permute-start.8) | collective-permute-done | bytes 131104 | tf_op jit(solution)/shard_map/ppermute | solution.py:689
  52.1 0.1 shard_map.32
  52.2 2.3 %collective-permute-start.11 = (f32[80,8,128]{2,1,0:T(8,128)S(1)}, f32[80,8,128]{2,1,0:T(8,128)S(1)}, u32[]{:S(2)}, u32[]{:S(2)}) collective-permute-start(f32[80,8,128]{2,1,0:T(8,128)S(1)} %get-tuple-element.47), channel_id=1, source_target_pairs={{0,8},{8,16},{16,24},{24,32},{32,40},{40,48},{48,56},{56,0},{1,9},... | collective-permute-start | bytes 983048 | tf_op jit(solution)/shard_map/ppermute | solution.py:689
  54.5 0.0 collective-permute-start.12
  54.5 4.0 %collective-permute-done.11.yl_ref = f32[80,8,128]{2,1,0:T(8,128)S(1)} collective-permute-done((f32[80,8,128]{2,1,0:T(8,128)S(1)}, f32[80,8,128]{2,1,0:T(8,128)S(1)}, u32[]{:S(2)}, u32[]{:S(2)}) %collective-permute-start.11) | collective-permute-done | bytes 327712 | tf_op jit(solution)/shard_map/ppermute | solution.py:689
  58.5 2.5 %collective-permute-done.12.yr_ref = f32[80,8,128]{2,1,0:T(8,128)S(1)} collective-permute-done((f32[80,8,128]{2,1,0:T(8,128)S(1)}, f32[80,8,128]{2,1,0:T(8,128)S(1)}, u32[]{:S(2)}, u32[]{:S(2)}) %collective-permute-start.12) | collective-permute-done | bytes 327712 | tf_op jit(solution)/shard_map/ppermute | solution.py:689
  61.0 4.6 %shard_map.33 = (f32[16,8,128]{2,1,0:T(8,128)S(1)}, f32[16,2,24,128]{3,2,1,0:T(8,128)S(1)}, f32[6,16,2,24,128]{4,3,2,1,0:T(8,128)S(1)}, f32[6,16,2,24,128]{4,3,2...) custom-call(s32[3]{0:T(128)S(1)} %pad_add_fusion.scal, ...), custom_call_target="tpu_custom_call" | custom-call | tf_op jit(solution)/shard_map/pallas_call | solution.py:677
  65.6 2.7 %collective-permute-start.15 = (f32[1,16,8,128]{3,2,1,0:T(8,128)S(1)}, f32[1,16,8,128]{3,2,1,0:T(8,128)S(1)}, u32[]{:S(2)}, u32[]{:S(2)}) collective-permute-start(f32[1,16,8,128]{3,2,1,0:T(8,128)S(1)} %bitcast.11), channel_id=1, source_target_pairs={{0,48},{8,56},{16,0},{24,8},{32,16},{40,24},{48,32},{56,40},{1,49}... | collective-permute-start | bytes 196616 | tf_op jit(solution)/shard_map/ppermute | solution.py:689
  68.3 0.2 collective-permute-start.14
  68.5 0.7 collective-permute-start.13
  69.1 1.8 %collective-permute-done.15 = f32[1,16,8,128]{3,2,1,0:T(8,128)S(1)} collective-permute-done((f32[1,16,8,128]{3,2,1,0:T(8,128)S(1)}, f32[1,16,8,128]{3,2,1,0:T(8,128)S(1)}, u32[]{:S(2)}, u32[]{:S(2)}) %collective-permute-start.15) | collective-permute-done | bytes 65568 | tf_op jit(solution)/shard_map/ppermute | solution.py:689
  70.9 2.6 %collective-permute-done.14 = f32[1,16,8,128]{3,2,1,0:T(8,128)S(1)} collective-permute-done((f32[1,16,8,128]{3,2,1,0:T(8,128)S(1)}, f32[1,16,8,128]{3,2,1,0:T(8,128)S(1)}, u32[]{:S(2)}, u32[]{:S(2)}) %collective-permute-start.14) | collective-permute-done | bytes 65568 | tf_op jit(solution)/shard_map/ppermute | solution.py:689
  73.5 1.3 %collective-permute-done.13 = f32[1,16,8,128]{3,2,1,0:T(8,128)S(1)} collective-permute-done((f32[1,16,8,128]{3,2,1,0:T(8,128)S(1)}, f32[1,16,8,128]{3,2,1,0:T(8,128)S(1)}, u32[]{:S(2)}, u32[]{:S(2)}) %collective-permute-start.13) | collective-permute-done | bytes 65568 | tf_op jit(solution)/shard_map/ppermute | solution.py:689
  74.9 2.2 %all-gather = f32[8,16,8,128]{3,2,1,0:T(8,128)S(1)} all-gather(f32[4,16,8,128]{3,2,1,0:T(8,128)S(1)} %pad_maximum_fusion.2), channel_id=2, replica_groups={{0,8},{16,24},{32,40},{48,56},{1,9},{17,25},{33,41},{49,57},{2,10},{18,..., dimensions={0}, use_global_device_ids=true | all-gather | bytes 786432 | tf_op jit(solution)/shard_map/all_gather | solution.py:694
  77.1 2.4 %shard_map.34 = (f32[8,8,128]{2,1,0:T(8,128)S(1)}, f32[16,2,8,128]{3,2,1,0:T(8,128)S(1)}, f32[6,16,2,8,128]{4,3,2,1,0:T(8,128)S(1)}, f32[6,16,2,8,128]{4,3,2,1,0...) custom-call(s32[3]{0:T(128)S(1)} %pad_add_fusion.scal, f32[2,4,16,8,128]{4,3,2,1,0:T(8,128)S(1)} %bitcast.9), custom_call_target="tpu_custom_call" | custom-call | tf_op jit(solution)/shard_map/pallas_call | solution.py:677
  79.5 2.6 %collective-permute-start.18 = (f32[8,8,128]{2,1,0:T(8,128)S(1)}, f32[8,8,128]{2,1,0:T(8,128)S(1)}, u32[]{:S(2)}, u32[]{:S(2)}) collective-permute-start(f32[8,8,128]{2,1,0:T(8,128)S(1)} %get-tuple-element.60.own_ref), channel_id=1, source_target_pairs={{0,3},{1,4},{2,5},{3,6},{4,7},{5,0},{6,1},{7,2},{8,13},{9,14},{10,... | collective-permute-start | bytes 98312 | tf_op jit(solution)/shard_map/ppermute | solution.py:703
  82.1 4.1 %collective-permute-start.17 = (f32[8,8,128]{2,1,0:T(8,128)S(1)}, f32[8,8,128]{2,1,0:T(8,128)S(1)}, u32[]{:S(2)}, u32[]{:S(2)}) collective-permute-start(f32[8,8,128]{2,1,0:T(8,128)S(1)} %get-tuple-element.60.own_ref), channel_id=1, source_target_pairs={{0,2},{1,3},{2,4},{3,5},{4,6},{5,7},{6,0},{7,1},{8,14},{9,15},{10,... | collective-permute-start | bytes 98312 | tf_op jit(solution)/shard_map/ppermute | solution.py:703
  86.2 0.2 collective-permute-start.16
  86.4 1.5 %collective-permute-start.19 = (f32[8,8,128]{2,1,0:T(8,128)S(1)}, f32[8,8,128]{2,1,0:T(8,128)S(1)}, u32[]{:S(2)}, u32[]{:S(2)}) collective-permute-start(f32[8,8,128]{2,1,0:T(8,128)S(1)} %get-tuple-element.60.own_ref), channel_id=1, source_target_pairs={{0,4},{1,5},{2,6},{3,7},{4,0},{5,1},{6,2},{7,3},{8,12},{9,13},{10,... | collective-permute-start | bytes 98312 | tf_op jit(solution)/shard_map/ppermute | solution.py:703
  87.9 0.0 collective-permute-done.18
  87.9 0.0 collective-permute-done.17
  87.9 1.4 %collective-permute-done.16 = f32[8,8,128]{2,1,0:T(8,128)S(1)} collective-permute-done((f32[8,8,128]{2,1,0:T(8,128)S(1)}, f32[8,8,128]{2,1,0:T(8,128)S(1)}, u32[]{:S(2)}, u32[]{:S(2)}) %collective-permute-start.16) | collective-permute-done | bytes 32800 | tf_op jit(solution)/shard_map/ppermute | solution.py:703
  89.3 3.2 %all-gather.1 = f32[6,8,8,128]{3,2,1,0:T(8,128)S(1)} all-gather(f32[3,8,8,128]{3,2,1,0:T(8,128)S(1)} %pad_maximum_fusion.3), channel_id=3, replica_groups={{0,8},{16,24},{32,40},{48,56},{1,9},{17,25},{33,41},{49,57},{2,10},{18,..., dimensions={0}, use_global_device_ids=true | all-gather | bytes 294912 | tf_op jit(solution)/shard_map/all_gather | solution.py:694
  92.5 1.3 %collective-permute-done.19.far_ref = f32[8,8,128]{2,1,0:T(8,128)S(1)} collective-permute-done((f32[8,8,128]{2,1,0:T(8,128)S(1)}, f32[8,8,128]{2,1,0:T(8,128)S(1)}, u32[]{:S(2)}, u32[]{:S(2)}) %collective-permute-start.19) | collective-permute-done | bytes 32800 | tf_op jit(solution)/shard_map/ppermute | solution.py:703
  93.8 5.5 %shard_map.35.add_ref = f32[8,8,128]{2,1,0:T(8,128)S(1)} custom-call(s32[3]{0:T(128)S(1)} %pad_add_fusion.scal, f32[8,8,128]{2,1,0:T(8,128)S(1)} %get-tuple-element.60.own_ref, f32[2,3,8,8,128]{4,3,2,1,0:T(8,128)S(1)} %bitcast.10, f32[8,8,128]{2,1,0:T(8,128)S(1)} %collective-permute-done.19.far_ref), custom_call_target="tpu_custom_call" | custom-call | tf_op jit(solution)/shard_map/pallas_call | solution.py:677
  99.3 1.6 %shard_map.36.add_ref = f32[8,24,128]{2,1,0:T(8,128)S(1)} custom-call(s32[3]{0:T(128)S(1)} %pad_add_fusion.scal, f32[16,2,8,128]{3,2,1,0:T(8,128)S(1)} %get-tuple-element.55.black_ref, f32[6,16,2,8,128]{4,3,2,1,0:T(8,128)S(1)} %get-tuple-element.56.wd0, f32[6,16,2,8,128]{4,3,2,1,0:T(8,128)S(1)} %get-tuple-element.57.wd1, ...), custom_call_target="tpu_custom_call" | custom-call | tf_op jit(solution)/shard_map/pallas_call | solution.py:677
  100.9 2.9 %shard_map.37.add_ref = f32[16,24,128]{2,1,0:T(8,128)S(1)} custom-call(s32[3]{0:T(128)S(1)} %pad_add_fusion.scal, f32[16,2,24,128]{3,2,1,0:T(8,128)S(1)} %get-tuple-element.49.black_ref, f32[6,16,2,24,128]{4,3,2,1,0:T(8,128)S(1)} %get-tuple-element.50.wd0, f32[6,16,2,24,128]{4,3,2,1,0:T(8,128)S(1)} %get-tuple-element.51.wd1, ...), custom_call_target="tpu_custom_call" | custom-call | tf_op jit(solution)/shard_map/pallas_call | solution.py:677
  103.8 3.1 %shard_map.38 = f32[16,32,128]{2,1,0:T(8,128)} custom-call(f32[32,2,24,128]{3,2,1,0:T(8,128)S(1)} %get-tuple-element.39.black_ref, f32[6,32,2,24,128]{4,3,2,1,0:T(8,128)S(1)} %get-tuple-element.40.wd0, f32[6,32,2,24,128]{4,3,2,1,0:T(8,128)S(1)} %get-tuple-element.41.wd1, f32[32,2,24,128]{3,2,1,0:T(8,128)S(1)} %get-tuple-element.42.fd0, ...), custom_call_target="tpu_custom_call" | custom-call | tf_op jit(solution)/shard_map/pallas_call | solution.py:677
  (6 shorter events, 0.1 us)
Async XLA Ops:
  0.0 0.9 copy-start
  1.0 0.9 copy-start.1
  2.9 7.8 %collective-permute-start = (f32[2,2,16,128]{3,2,1,0:T(8,128)S(1)}, f32[2,2,16,128]{3,2,1,0:T(8,128)S(1)}, u32[]{:S(2)}, u32[]{:S(2)}) collective-permute-start(f32[2,2,16,128]{3,2,1,0:T(8,128)S(1)} %get-tuple-element.34), channel_id=1, source_target_pairs={{0,1},{1,2},{2,3},{3,4},{4,5},{5,6},{6,7},{7,0},{8,9},{9,10},{10,1... | collective-permute-start | bytes 98312 | tf_op jit(solution)/shard_map/ppermute | solution.py:689
  5.5 5.2 %collective-permute-start.1 = (f32[2,2,16,128]{3,2,1,0:T(8,128)S(1)}, f32[2,2,16,128]{3,2,1,0:T(8,128)S(1)}, u32[]{:S(2)}, u32[]{:S(2)}) collective-permute-start(f32[2,2,16,128]{3,2,1,0:T(8,128)S(1)} %get-tuple-element.35), channel_id=1, source_target_pairs={{0,7},{1,0},{2,1},{3,2},{4,3},{5,4},{6,5},{7,6},{8,15},{9,8},{10,9... | collective-permute-start | bytes 98312 | tf_op jit(solution)/shard_map/ppermute | solution.py:689
  10.8 8.2 %collective-permute-start.2 = (f32[18,2,16,128]{3,2,1,0:T(8,128)S(1)}, f32[18,2,16,128]{3,2,1,0:T(8,128)S(1)}, u32[]{:S(2)}, u32[]{:S(2)}) collective-permute-start(f32[18,2,16,128]{3,2,1,0:T(8,128)S(1)} %pad_maximum_fusion.c_ref), channel_id=1, source_target_pairs={{0,64},{64,128},{128,192},{192,0},{1,65},{65,129},{129,193},{193,1... | collective-permute-start | bytes 884744 | tf_op jit(solution)/shard_map/ppermute | solution.py:689
  12.1 6.9 %collective-permute-start.3 = (f32[18,2,16,128]{3,2,1,0:T(8,128)S(1)}, f32[18,2,16,128]{3,2,1,0:T(8,128)S(1)}, u32[]{:S(2)}, u32[]{:S(2)}) collective-permute-start(f32[18,2,16,128]{3,2,1,0:T(8,128)S(1)} %pad_maximum_fusion.1.b_ref), channel_id=1, source_target_pairs={{0,192},{64,0},{128,64},{192,128},{1,193},{65,1},{129,65},{193,129... | collective-permute-start | bytes 884744 | tf_op jit(solution)/shard_map/ppermute | solution.py:689
  19.1 7.4 %collective-permute-start.4 = (f32[72,8,128]{2,1,0:T(8,128)S(1)}, f32[72,8,128]{2,1,0:T(8,128)S(1)}, u32[]{:S(2)}, u32[]{:S(2)}) collective-permute-start(f32[72,8,128]{2,1,0:T(8,128)S(1)} %get-tuple-element.37), channel_id=1, source_target_pairs={{0,8},{8,16},{16,24},{24,32},{32,40},{40,48},{48,56},{56,0},{1,9},... | collective-permute-start | bytes 884744 | tf_op jit(solution)/shard_map/ppermute | solution.py:689
  22.8 6.1 %collective-permute-start.5 = (f32[72,8,128]{2,1,0:T(8,128)S(1)}, f32[72,8,128]{2,1,0:T(8,128)S(1)}, u32[]{:S(2)}, u32[]{:S(2)}) collective-permute-start(f32[72,8,128]{2,1,0:T(8,128)S(1)} %get-tuple-element.38), channel_id=1, source_target_pairs={{0,56},{8,0},{16,8},{24,16},{32,24},{40,32},{48,40},{56,48},{1,57}... | collective-permute-start | bytes 884744 | tf_op jit(solution)/shard_map/ppermute | solution.py:689
  35.8 4.1 %collective-permute-start.6 = (f32[4,2,8,128]{3,2,1,0:T(8,128)S(1)}, f32[4,2,8,128]{3,2,1,0:T(8,128)S(1)}, u32[]{:S(2)}, u32[]{:S(2)}) collective-permute-start(f32[4,2,8,128]{3,2,1,0:T(8,128)S(1)} %get-tuple-element.45), channel_id=1, source_target_pairs={{0,1},{1,2},{2,3},{3,4},{4,5},{5,6},{6,7},{7,0},{8,9},{9,10},{10,1... | collective-permute-start | bytes 98312 | tf_op jit(solution)/shard_map/ppermute | solution.py:689
  35.9 4.0 %collective-permute-start.7 = (f32[4,2,8,128]{3,2,1,0:T(8,128)S(1)}, f32[4,2,8,128]{3,2,1,0:T(8,128)S(1)}, u32[]{:S(2)}, u32[]{:S(2)}) collective-permute-start(f32[4,2,8,128]{3,2,1,0:T(8,128)S(1)} %get-tuple-element.46), channel_id=1, source_target_pairs={{0,7},{1,0},{2,1},{3,2},{4,3},{5,4},{6,5},{7,6},{8,15},{9,8},{10,9... | collective-permute-start | bytes 98312 | tf_op jit(solution)/shard_map/ppermute | solution.py:689
  40.2 5.9 %collective-permute-start.10 = (f32[16,2,8,128]{3,2,1,0:T(8,128)S(1)}, f32[16,2,8,128]{3,2,1,0:T(8,128)S(1)}, u32[]{:S(2)}, u32[]{:S(2)}) collective-permute-start(f32[16,2,8,128]{3,2,1,0:T(8,128)S(1)} %shard_map.31.a_ref), channel_id=1, source_target_pairs={{0,192},{64,0},{128,64},{192,128},{1,193},{65,1},{129,65},{193,129... | collective-permute-start | bytes 393224 | tf_op jit(solution)/shard_map/ppermute | solution.py:689
  42.9 5.4 %collective-permute-start.9 = (f32[16,2,8,128]{3,2,1,0:T(8,128)S(1)}, f32[16,2,8,128]{3,2,1,0:T(8,128)S(1)}, u32[]{:S(2)}, u32[]{:S(2)}) collective-permute-start(f32[16,2,8,128]{3,2,1,0:T(8,128)S(1)} %shard_map.31.a_ref), channel_id=1, source_target_pairs={{0,128},{64,192},{128,0},{192,64},{1,129},{65,193},{129,1},{193,65... | collective-permute-start | bytes 393224 | tf_op jit(solution)/shard_map/ppermute | solution.py:689
  43.3 8.8 %collective-permute-start.8 = (f32[16,2,8,128]{3,2,1,0:T(8,128)S(1)}, f32[16,2,8,128]{3,2,1,0:T(8,128)S(1)}, u32[]{:S(2)}, u32[]{:S(2)}) collective-permute-start(f32[16,2,8,128]{3,2,1,0:T(8,128)S(1)} %shard_map.31.a_ref), channel_id=1, source_target_pairs={{0,64},{64,128},{128,192},{192,0},{1,65},{65,129},{129,193},{193,1... | collective-permute-start | bytes 393224 | tf_op jit(solution)/shard_map/ppermute | solution.py:689
  52.2 6.3 %collective-permute-start.11 = (f32[80,8,128]{2,1,0:T(8,128)S(1)}, f32[80,8,128]{2,1,0:T(8,128)S(1)}, u32[]{:S(2)}, u32[]{:S(2)}) collective-permute-start(f32[80,8,128]{2,1,0:T(8,128)S(1)} %get-tuple-element.47), channel_id=1, source_target_pairs={{0,8},{8,16},{16,24},{24,32},{32,40},{40,48},{48,56},{56,0},{1,9},... | collective-permute-start | bytes 983048 | tf_op jit(solution)/shard_map/ppermute | solution.py:689
  54.5 6.5 %collective-permute-start.12 = (f32[80,8,128]{2,1,0:T(8,128)S(1)}, f32[80,8,128]{2,1,0:T(8,128)S(1)}, u32[]{:S(2)}, u32[]{:S(2)}) collective-permute-start(f32[80,8,128]{2,1,0:T(8,128)S(1)} %get-tuple-element.48), channel_id=1, source_target_pairs={{0,56},{8,0},{16,8},{24,16},{32,24},{40,32},{48,40},{56,48},{1,57}... | collective-permute-start | bytes 983048 | tf_op jit(solution)/shard_map/ppermute | solution.py:689
  65.6 5.3 %collective-permute-start.15 = (f32[1,16,8,128]{3,2,1,0:T(8,128)S(1)}, f32[1,16,8,128]{3,2,1,0:T(8,128)S(1)}, u32[]{:S(2)}, u32[]{:S(2)}) collective-permute-start(f32[1,16,8,128]{3,2,1,0:T(8,128)S(1)} %bitcast.11), channel_id=1, source_target_pairs={{0,48},{8,56},{16,0},{24,8},{32,16},{40,24},{48,32},{56,40},{1,49}... | collective-permute-start | bytes 196616 | tf_op jit(solution)/shard_map/ppermute | solution.py:689
  68.3 5.2 %collective-permute-start.14 = (f32[1,16,8,128]{3,2,1,0:T(8,128)S(1)}, f32[1,16,8,128]{3,2,1,0:T(8,128)S(1)}, u32[]{:S(2)}, u32[]{:S(2)}) collective-permute-start(f32[1,16,8,128]{3,2,1,0:T(8,128)S(1)} %bitcast.12), channel_id=1, source_target_pairs={{0,32},{8,40},{16,48},{24,56},{32,0},{40,8},{48,16},{56,24},{1,33}... | collective-permute-start | bytes 196616 | tf_op jit(solution)/shard_map/ppermute | solution.py:689
  68.5 6.4 %collective-permute-start.13 = (f32[1,16,8,128]{3,2,1,0:T(8,128)S(1)}, f32[1,16,8,128]{3,2,1,0:T(8,128)S(1)}, u32[]{:S(2)}, u32[]{:S(2)}) collective-permute-start(f32[1,16,8,128]{3,2,1,0:T(8,128)S(1)} %bitcast.13), channel_id=1, source_target_pairs={{0,16},{8,24},{16,32},{24,40},{32,48},{40,56},{48,0},{56,8},{1,17}... | collective-permute-start | bytes 196616 | tf_op jit(solution)/shard_map/ppermute | solution.py:689
  79.5 8.4 %collective-permute-start.18 = (f32[8,8,128]{2,1,0:T(8,128)S(1)}, f32[8,8,128]{2,1,0:T(8,128)S(1)}, u32[]{:S(2)}, u32[]{:S(2)}) collective-permute-start(f32[8,8,128]{2,1,0:T(8,128)S(1)} %get-tuple-element.60.own_ref), channel_id=1, source_target_pairs={{0,3},{1,4},{2,5},{3,6},{4,7},{5,0},{6,1},{7,2},{8,13},{9,14},{10,... | collective-permute-start | bytes 98312 | tf_op jit(solution)/shard_map/ppermute | solution.py:703
  82.1 5.8 %collective-permute-start.17 = (f32[8,8,128]{2,1,0:T(8,128)S(1)}, f32[8,8,128]{2,1,0:T(8,128)S(1)}, u32[]{:S(2)}, u32[]{:S(2)}) collective-permute-start(f32[8,8,128]{2,1,0:T(8,128)S(1)} %get-tuple-element.60.own_ref), channel_id=1, source_target_pairs={{0,2},{1,3},{2,4},{3,5},{4,6},{5,7},{6,0},{7,1},{8,14},{9,15},{10,... | collective-permute-start | bytes 98312 | tf_op jit(solution)/shard_map/ppermute | solution.py:703
  86.2 3.0 %collective-permute-start.16 = (f32[8,8,128]{2,1,0:T(8,128)S(1)}, f32[8,8,128]{2,1,0:T(8,128)S(1)}, u32[]{:S(2)}, u32[]{:S(2)}) collective-permute-start(f32[8,8,128]{2,1,0:T(8,128)S(1)} %get-tuple-element.60.own_ref), channel_id=1, source_target_pairs={{0,1},{1,2},{2,3},{3,4},{4,5},{5,6},{6,7},{7,0},{8,15},{9,8},{10,9... | collective-permute-start | bytes 98312 | tf_op jit(solution)/shard_map/ppermute | solution.py:703
  86.4 7.4 %collective-permute-start.19 = (f32[8,8,128]{2,1,0:T(8,128)S(1)}, f32[8,8,128]{2,1,0:T(8,128)S(1)}, u32[]{:S(2)}, u32[]{:S(2)}) collective-permute-start(f32[8,8,128]{2,1,0:T(8,128)S(1)} %get-tuple-element.60.own_ref), channel_id=1, source_target_pairs={{0,4},{1,5},{2,6},{3,7},{4,0},{5,1},{6,2},{7,3},{8,12},{9,13},{10,... | collective-permute-start | bytes 98312 | tf_op jit(solution)/shard_map/ppermute | solution.py:703

commit v3 on v2

--- a/solution.py
+++ b/solution.py
@@ -30,7 +30,6 @@
 L1 = Level(16, 24, 64, "x")
 L2 = Level(16, 8, 32, "y")
 L3 = Level(8, 8, 64, "y")
-L4 = Level(4, 8, 128, None)
 
 
 def lanes(rows):
@@ -126,12 +125,11 @@
             own_rec = rec[colour][x + 1, q]
             near = beside(level, rec[1 - colour], x, q, colour, a)
             walls = {}
-            if level.fold == "y" or level is L4:
-                width = level.group if level.fold == "y" else 128
+            if level.fold == "y":
                 if q == 0:
-                    walls[3] = (row == 0) & (lane < width)
+                    walls[3] = (row == 0) & (lane < level.group)
                 else:
-                    walls[2] = (row == rows - 1) & (lane >= 128 - width)
+                    walls[2] = (row == rows - 1) & (lane >= 128 - level.group)
             if level.group < 128:
                 end = 0 if goes_back(colour, a, q) else level.group - 1
                 walls[5] = lane % level.group == end
@@ -277,16 +275,18 @@
             zr_ref[half, q] = turn(right, 60)
 
 
-def edge_kernel(a_ref, b_ref, c_ref, d_ref, lo_ref, hi_ref):
+def edge_kernel(*refs):
+    mains, strips, lo_ref, hi_ref = refs[0:4], refs[4:8], refs[8], refs[9]
     low = rows_of(8) < 4
-    for t, ref in enumerate((a_ref, b_ref, c_ref, d_ref)):
+    for t in range(4):
         for i in range(18):
-            lo_ref[18 * t + i] = jnp.where(low, ref[i, 0, 0:8], pltpu.roll(ref[i, 1, 0:8], 4, 0))
-            hi_ref[18 * t + i] = jnp.where(low, pltpu.roll(ref[i, 1, 8:16], 4, 0), ref[i, 0, 8:16])
+            ref, at = (mains[t], i) if i < 16 else (strips[t], i - 16)
+            lo_ref[18 * t + i] = jnp.where(low, ref[at, 0, 0:8], pltpu.roll(ref[at, 1, 0:8], 4, 0))
+            hi_ref[18 * t + i] = jnp.where(low, pltpu.roll(ref[at, 1, 8:16], 4, 0), ref[at, 0, 8:16])
 
 
 def level0_down_kernel(
-    scal, a_ref, b_ref, c_ref, d_ref, yl_ref, yr_ref,
+    scal, m0, m1, m2, m3, s0, s1, s2, s3, yl_ref, yr_ref,
     own_ref, zl_ref, zr_ref, black_ref, wd0, wd1, fd0, fd1,
     cond0, cond1, rec0, rec1, v0, v1, dd, nat_f, nat_b,
 ):
@@ -298,7 +298,7 @@
     inside = inside & ((gy > 0) | (row < 20)) & ((gy < 7) | (row < 16) | (row >= 20))
     keep = jnp.where(inside, 1.0, 0.0)
     low = rows_of(8) < 4
-    for t, ref in enumerate((a_ref, b_ref, c_ref, d_ref)):
+    for t, (main_ref, strip_ref) in enumerate(((m0, s0), (m1, s1), (m2, s2), (m3, s3))):
         here = keep
         if t == 0:
             here = keep * jnp.where(gx > 0, 1.0, 0.0)
@@ -308,7 +308,8 @@
         def wide(i, q):
             right, left = yr_ref[18 * t + i], yl_ref[18 * t + i]
             edge = jnp.where(low, right, left) if q == 0 else pltpu.roll(jnp.where(low, left, right), 4, 0)
-            return jnp.concatenate([ref[i, q], edge], axis=0)
+            own = main_ref[i, q] if i < 16 else strip_ref[i - 16, q]
+            return jnp.concatenate([own, edge], axis=0)
 
         ends = [(wide(16, q), wide(17, q)) for q in (0, 1)]
         for x in range(8):
@@ -477,21 +478,74 @@
         out_ref[x] = packed
 
 
+def coarsest(f, b):
+    lane, row = lanes(8), rows_of(8)
+    x, k = lane // 32, lane % 32
+
+    def near(values, colour, q):
+        back = (x + q + colour) % 2 == 0
+        across = values[1 - q]
+        return [
+            values[q],
+            across,
+            turn(values[q], -32),
+            turn(values[q], 32),
+            pltpu.roll(across, 1 if q == 0 else 7, 0),
+            pick(values[q], (lane + jnp.where(back, 127, 1)) % 128),
+        ]
+
+    rec = [[inverse_of(cells) for cells in pair] for pair in b]
+    weights, sources = [], []
+    for colour in (0, 1):
+        weights.append([])
+        sources.append([])
+        for q in (0, 1):
+            back = (x + q + colour) % 2 == 0
+            walls = [
+                None, None, x == 3, x == 0, row == (0 if q == 0 else 7), k == jnp.where(back, 0, 31),
+            ]
+            faces, total = [], None
+            for value, wall in zip(near(rec[1 - colour], colour, q), walls):
+                if wall is not None:
+                    value = jnp.where(wall, OFF, value)
+                face = inverse_of(rec[colour][q] + value)
+                total = face if total is None else total + face
+                faces.append(face if wall is None else jnp.where(wall, 0.0, face))
+            inverse = inverse_of(total)
+            weights[-1].append([face * inverse for face in faces])
+            sources[-1].append(f[colour][q] * (0.5 * inverse))
+
+    def half(colour, other):
+        made = []
+        for q in (0, 1):
+            total = sources[colour][q]
+            for weight, value in zip(weights[colour][q], near(other, colour, q)):
+                total = total + weight * value
+            made.append(total)
+        return made
+
+    black = half(1, sources[0])
+
+    def step(_, carry):
+        return tuple(half(1, half(0, list(carry))))
+
+    black = lax.fori_loop(0, ITERS - 2, step, tuple(black))
+    red = half(0, list(black))
+    return red, half(1, red)
+
+
 def coarse_kernel(
-    scal, own_ref, pair_ref, far_ref, out_ref,
+    scal, own_ref, all_ref, out_ref,
     cond30, cond31, rec30, rec31, v30, v31, dd3, wd30, wd31, fd30, fd31, nat_f, nat_b,
-    cond40, cond41, rec40, rec41, v40, v41, dd4, wd40, wd41, fd40, fd41, slabs, whole, nat4, nat3,
+    slabs, whole, nat4, nat3,
 ):
     cond3, rec3, v3, wd3, fd3 = (cond30, cond31), (rec30, rec31), (v30, v31), (wd30, wd31), (fd30, fd31)
-    cond4, rec4, v4, wd4, fd4 = (cond40, cond41), (rec40, rec41), (v40, v41), (wd40, wd41), (fd40, fd41)
     gz = scal[2]
     lane = lanes(8)
-
     slabs[gz] = own_ref[...]
-    slabs[(gz + 4) % 8] = far_ref[...]
-    for j in range(3):
-        slabs[(gz + 7 - j) % 8] = pair_ref[0, j]
-        slabs[(gz + 1 + j) % 8] = pair_ref[1, j]
+    for j in range(4):
+        slabs[(gz + 7 - j) % 8] = all_ref[0, j]
+        slabs[(gz + 1 + j) % 8] = all_ref[1, j]
 
     for x in range(8):
         for c, cells in enumerate(exchange([slabs[r, x] for r in range(8)], 8)):
@@ -508,55 +562,25 @@
     planes(0, 8, 4, place3)
     set_up(L3, cond3, rec3, wd3, fd3, dd3)
     descend(L3, v3, wd3, fd3, dd3, cond3, nat_f, nat_b)
-    on_grid = lane < 32
+    f4 = [[None, None], [None, None]]
+    b4 = [[None, None], [None, None]]
     for x in range(4):
-        f_plane, b_plane = nat_f[x], nat_b[x]
-        for half in (0, 1):
-            nat4[x, 8 * half : 8 * half + 8] = turn(f_plane, 64 * half)
-            whole[0, x, 8 * half : 8 * half + 8] = turn(b_plane, 64 * half)
+        for arr, plane in enumerate((nat_f[x], nat_b[x])):
+            for part in (0, 1):
+                whole[arr, x, 8 * part : 8 * part + 8] = turn(plane, 64 * part)
+        for made, arr in ((f4, 0), (b4, 1)):
+            for q in (0, 1):
+                cells = whole[arr, x, pl.ds(q, 8, stride=2), :]
+                for colour in (0, 1):
+                    mine = pick(cells, 2 * (lane % 32) + (x + q + colour) % 2)
+                    before = made[colour][q]
+                    made[colour][q] = mine if x == 0 else jnp.where(lane // 32 == x, mine, before)
+    red, black = coarsest(f4, b4)
+    for x in range(4):
         for q in (0, 1):
-            f = nat4[x, pl.ds(q, 8, stride=2), :]
-            b = whole[0, x, pl.ds(q, 8, stride=2), :]
-            for e in (0, 1):
-                colour = (x + q + e) % 2
-                index = 2 * (lane % 32) + e
-                fd4[colour][x, q] = pick(f, index)
-                cells = pick(b, index)
-                cond4[colour][x, q] = jnp.where(on_grid, cells, 0.0)
-                rec4[colour][x + 1, q] = jnp.where(on_grid, inverse_of(cells), OFF)
-    set_up(L4, cond4, rec4, wd4, fd4, dd4)
-
-    def half(colour, other):
-        made = {}
-        for x in range(4):
-            for q in (0, 1):
-                mid, across = other[x, q], other[x, 1 - q]
-                weight = lambda i: wd4[colour][i, x, q]
-                total = fd4[colour][x, q] + weight(4) * mid
-                total = total + weight(2) * (across if q == 0 else up(L4, across))
-                total = total + weight(3) * (down(L4, across) if q == 0 else across)
-                rest = weight(5) * turn(mid, 1 if goes_back(colour, x, q) else -1)
-                if x < 3:
-                    rest = rest + weight(0) * other[x + 1, q]
-                if x > 0:
-                    rest = rest + weight(1) * other[x - 1, q]
-                made[x, q] = total + rest
-        return made
-
-    keys = [(x, q) for x in range(4) for q in (0, 1)]
-    black = half(1, {key: fd4[0][key] for key in keys})
-
-    def step(_, carry):
-        after = half(1, half(0, dict(zip(keys, carry))))
-        return tuple(after[key] for key in keys)
-
-    final = lax.fori_loop(0, ITERS - 2, step, tuple(black[key] for key in keys))
-    red = half(0, dict(zip(keys, final)))
-    black = half(1, red)
-    index = (lane % 2) * 32 + (lane // 2) % 32
-    for x, q in keys:
-        even, odd = (red[x, q], black[x, q]) if (x + q) % 2 == 0 else (black[x, q], red[x, q])
-        nat4[x, pl.ds(q, 8, stride=2), :] = pick(jnp.where(lane < 32, even, turn(odd, 32)), index)
+            even, odd = (red[q], black[q]) if (x + q) % 2 == 0 else (black[q], red[q])
+            index = 32 * x + (lane % 64) // 2
+            nat4[x, pl.ds(q, 8, stride=2), :] = jnp.where(lane % 2 == 0, pick(even, index), pick(odd, index))
     for x in range(4):
         nat_f[x] = jnp.where(lane < 64, nat4[x, 0:8], turn(nat4[x, 8:16], 64))
 
@@ -648,6 +672,15 @@
     planes(8, 24, 4, store)
 
 
+def up_kernel(scal, own_ref, all_ref, *refs):
+    set2, set1, set0 = refs[0:5], refs[5:10], refs[10:15]
+    out_ref, add2, add1, add0, v0, v1, w0, w1, x0, x1, nat2, nat1, *rest = refs[15:]
+    coarse_kernel(scal, own_ref, all_ref, add2, *rest)
+    level2_up_kernel(scal, *set2, add2, add1, v0, v1, nat2)
+    level1_up_kernel(scal, *set1, add1, add0, w0, w1, nat1)
+    level0_up_kernel(*set0, add0, out_ref, x0, x1)
+
+
 def arr(*shape):
     return jax.ShapeDtypeStruct(shape, F32)
 
@@ -709,18 +742,17 @@
     strip = arr(2, 2, 16, 128)
     lo, hi, zl, zr = call(split_kernel, [half, half, strip, strip], [], right_side, coefficient)
     from_left, from_right = ring(zr, "gz", 1), ring(zl, "gz", -1)
-    lo = jnp.concatenate([lo, from_left[0:1], from_right[0:1]])
-    hi = jnp.concatenate([hi, from_left[1:2], from_right[1:2]])
-    before, after = ring(hi, "gx", 1), ring(lo, "gx", -1)
-    bundles = (before, lo, hi, after)
-    yl, yr = call(edge_kernel, [arr(72, 8, 128)] * 2, [], *bundles)
+    mains = (ring(hi, "gx", 1), lo, hi, ring(lo, "gx", -1))
+    low, high = [jnp.concatenate([from_left[i : i + 1], from_right[i : i + 1]]) for i in (0, 1)]
+    strips = (ring(high, "gx", 1), low, high, ring(low, "gx", -1))
+    yl, yr = call(edge_kernel, [arr(72, 8, 128)] * 2, [], *mains, *strips)
     from_left, from_right = ring(yr, "gy", 1), ring(yl, "gy", -1)
     own, zl, zr, black0, *set0 = call(
         level0_down_kernel,
         [arr(16, 2, 8, 128), arr(4, 2, 8, 128), arr(4, 2, 8, 128), arr(*L0.own())]
         + [arr(*s) for s in weights(L0)],
         level_scratch(L0) + nat_scratch(L0, 8),
-        *bundles, from_left, from_right, scal=scal,
+        *mains, *strips, from_left, from_right, scal=scal,
     )
     from_left, from_right = ring(zr, "gz", 1), ring(zl, "gz", -1)
     bundle = call(widen_kernel, arr(16, 2, 8, 128), [], own, from_left, from_right)
@@ -741,30 +773,15 @@
         level_scratch(L2) + nat_scratch(L2),
         sheet, scal=scal,
     )
-    far = along_z(own, 4)
-    near = both_cores(jnp.stack([along_z(own, s) for s in (1, 2, 3)]))
-    correction = call(
-        coarse_kernel,
-        arr(8, 8, 128),
-        level_scratch(L3) + [scratch(*s) for s in weights(L3)] + nat_scratch(L3)
-        + level_scratch(L4) + [scratch(*s) for s in weights(L4)]
+    slabs = both_cores(jnp.stack([along_z(own, s) for s in (1, 2, 3, 4)]))
+    return call(
+        up_kernel, arr(16, 32, 128),
+        [scratch(8, 8, 128), scratch(8, 24, 128), scratch(16, 24, 128)]
+        + [scratch(*level.wide()) for level in (L2, L2, L1, L1, L0, L0)]
+        + [scratch(16, 32, 128), scratch(16, 48, 128)]
+        + level_scratch(L3) + [scratch(*s) for s in weights(L3)] + nat_scratch(L3)
         + [scratch(8, 8, 8, 128), scratch(4, 8, 16, 128), scratch(4, 16, 128), scratch(8, 32, 128)],
-        own, near, far, scal=scal,
-    )
-    correction = call(
-        level2_up_kernel, arr(8, 24, 128),
-        [scratch(*L2.wide())] * 2 + [scratch(16, 32, 128)],
-        black2, *set2, correction, scal=scal,
-    )
-    correction = call(
-        level1_up_kernel, arr(16, 24, 128),
-        [scratch(*L1.wide())] * 2 + [scratch(16, 48, 128)],
-        black1, *set1, correction, scal=scal,
-    )
-    return call(
-        level0_up_kernel, arr(16, 32, 128),
-        [scratch(*L0.wide())] * 2,
-        black0, *set0, correction,
+        own, slabs, black2, *set2, black1, *set1, black0, *set0, scal=scal,
     )
 
 

time: 107 us -> 105 us (0.981)
  waiting for transfers between devices: 37.3 us -> 34.4 us
  starting transfers between devices: 33.7 us -> 35.2 us
  Pallas kernels: 28.3 us -> 27.2 us
    ppermute x16 -> x18, waiting for transfers between devices: 34.6 us -> 31.4 us  [ring(): lax.ppermute(values, axis, [(i, (i + step) % count) for i in range(count)])]
    ppermute x16 -> x18, starting transfers between devices: 25.3 us -> 27 us  [ring(): lax.ppermute(values, axis, [(i, (i + step) % count) for i in range(count)])]
    pallas_call x11 -> x8, Pallas kernels: 28.3 us -> 27.2 us  [call(): pl.pallas_call(kernel, out_shape=outs, in_specs=specs, out_specs=jax.tree...]
  transfers between devices with their start and end apart: 20 -> 22, of which waited for: 15 -> 15; matrix products, arithmetic and copies ran while one was open for 0% -> 0% of each run, Pallas kernels for 0% -> 0%
where the time goes in v3:
time: 105 us
  starting transfers between devices  35.2 us (34%)
  waiting for transfers between devices  34.4 us (33%)
  Pallas kernels  27.2 us (26%)
  blocking collectives  5.71 us (5%)
  local copies, waits for them, and re-layouts  1.91 us (2%)
    ppermute x18, waiting for transfers between devices, ring(): lax.ppermute(values, axis, [(i, (i + step) % count) for i in range(count)])  31.4 us
    pallas_call x8, Pallas kernels, call(): pl.pallas_call(kernel, out_shape=outs, in_specs=specs, out_specs=jax.tree...  27.2 us
    ppermute x18, starting transfers between devices, ring(): lax.ppermute(values, axis, [(i, (i + step) % count) for i in range(count)])  27 us
    ppermute x4, starting transfers between devices, along_z(): return lax.ppermute(values, ('gy', 'gz'), pairs)  8.17 us
    all_gather x2, blocking collectives, both_cores(): lax.all_gather(values, 'gy', axis=0, axis_index_groups=[[i, i + 1] for i...  5.71 us
    ppermute x4, waiting for transfers between devices, along_z(): return lax.ppermute(values, ('gy', 'gz'), pairs)  3.06 us
  transfers between devices with their start and end apart: 22, of which 15 were waited for; matrix products, arithmetic and copies ran while one was open for 0% of the time, Pallas kernels for 0%

profile of v3, /device:TPU:1, one launch (start us, length us, event | category | flops | bytes accessed | tf_op | source)
XLA Modules:
  0.0 104.6 jit_solution(2400673905726226217)
XLA Ops:
  0.0 0.0 copy-start
  0.0 0.9 copy-done
  1.0 0.0 copy-start.1
  1.0 0.9 copy-done.1
  1.9 1.0 shard_map.28
  2.9 2.5 %collective-permute-start.2 = (f32[2,2,16,128]{3,2,1,0:T(8,128)S(1)}, f32[2,2,16,128]{3,2,1,0:T(8,128)S(1)}, u32[]{:S(2)}, u32[]{:S(2)}) collective-permute-start(f32[2,2,16,128]{3,2,1,0:T(8,128)S(1)} %get-tuple-element.35), channel_id=1, source_target_pairs={{0,1},{1,2},{2,3},{3,4},{4,5},{5,6},{6,7},{7,0},{8,9},{9,10},{10,1... | collective-permute-start | bytes 98312 | tf_op jit(solution)/shard_map/ppermute | solution.py:722
  5.5 4.0 %collective-permute-start.3 = (f32[2,2,16,128]{3,2,1,0:T(8,128)S(1)}, f32[2,2,16,128]{3,2,1,0:T(8,128)S(1)}, u32[]{:S(2)}, u32[]{:S(2)}) collective-permute-start(f32[2,2,16,128]{3,2,1,0:T(8,128)S(1)} %get-tuple-element.36), channel_id=1, source_target_pairs={{0,7},{1,0},{2,1},{3,2},{4,3},{5,4},{6,5},{7,6},{8,15},{9,8},{10,9... | collective-permute-start | bytes 98312 | tf_op jit(solution)/shard_map/ppermute | solution.py:722
  9.5 1.2 %collective-permute-start = (f32[16,2,16,128]{3,2,1,0:T(8,128)S(1)}, f32[16,2,16,128]{3,2,1,0:T(8,128)S(1)}, u32[]{:S(2)}, u32[]{:S(2)}) collective-permute-start(f32[16,2,16,128]{3,2,1,0:T(8,128)S(1)} %get-tuple-element.33.refs_2_.m2), channel_id=1, source_target_pairs={{0,64},{64,128},{128,192},{192,0},{1,65},{65,129},{129,193},{193,1... | collective-permute-start | bytes 786440 | tf_op jit(solution)/shard_map/ppermute | solution.py:722
  10.7 1.5 %collective-permute-start.1 = (f32[16,2,16,128]{3,2,1,0:T(8,128)S(1)}, f32[16,2,16,128]{3,2,1,0:T(8,128)S(1)}, u32[]{:S(2)}, u32[]{:S(2)}) collective-permute-start(f32[16,2,16,128]{3,2,1,0:T(8,128)S(1)} %get-tuple-element.34.refs_1_.m1), channel_id=1, source_target_pairs={{0,192},{64,0},{128,64},{192,128},{1,193},{65,1},{129,65},{193,129... | collective-permute-start | bytes 786440 | tf_op jit(solution)/shard_map/ppermute | solution.py:722
  12.2 0.0 collective-permute-done.2
  12.2 0.0 collective-permute-done.3
  12.2 0.1 collective-permute-start.4
  12.3 2.7 %collective-permute-start.5 = (f32[2,2,16,128]{3,2,1,0:T(8,128)S(1)}, f32[2,2,16,128]{3,2,1,0:T(8,128)S(1)}, u32[]{:S(2)}, u32[]{:S(2)}) collective-permute-start(f32[2,2,16,128]{3,2,1,0:T(8,128)S(1)} %pad_maximum_fusion.3.refs_5_.s1), channel_id=1, source_target_pairs={{0,192},{64,0},{128,64},{192,128},{1,193},{65,1},{129,65},{193,129... | collective-permute-start | bytes 98312 | tf_op jit(solution)/shard_map/ppermute | solution.py:722
  15.0 3.3 %collective-permute-done.4.refs_4_.s0 = f32[2,2,16,128]{3,2,1,0:T(8,128)S(1)} collective-permute-done((f32[2,2,16,128]{3,2,1,0:T(8,128)S(1)}, f32[2,2,16,128]{3,2,1,0:T(8,128)S(1)}, u32[]{:S(2)}, u32[]{:S(2)}) %collective-permute-start.4) | collective-permute-done | bytes 32800 | tf_op jit(solution)/shard_map/ppermute | solution.py:722
  18.3 0.0 collective-permute-done.5.refs_7_.s3
  18.3 0.0 collective-permute-done.refs_0_.m0
  18.3 0.0 collective-permute-done.1.refs_3_.m3
  18.3 0.1 shard_map.29
  18.4 3.1 %collective-permute-start.6 = (f32[72,8,128]{2,1,0:T(8,128)S(1)}, f32[72,8,128]{2,1,0:T(8,128)S(1)}, u32[]{:S(2)}, u32[]{:S(2)}) collective-permute-start(f32[72,8,128]{2,1,0:T(8,128)S(1)} %get-tuple-element.37), channel_id=1, source_target_pairs={{0,8},{8,16},{16,24},{24,32},{32,40},{40,48},{48,56},{56,0},{1,9},... | collective-permute-start | bytes 884744 | tf_op jit(solution)/shard_map/ppermute | solution.py:722
  21.4 0.0 collective-permute-start.7
  21.4 0.1 pad_add_fusion.scal
  21.5 3.6 %collective-permute-done.6.yl_ref = f32[72,8,128]{2,1,0:T(8,128)S(1)} collective-permute-done((f32[72,8,128]{2,1,0:T(8,128)S(1)}, f32[72,8,128]{2,1,0:T(8,128)S(1)}, u32[]{:S(2)}, u32[]{:S(2)}) %collective-permute-start.6) | collective-permute-done | bytes 294944 | tf_op jit(solution)/shard_map/ppermute | solution.py:722
  25.1 2.5 %collective-permute-done.7.yr_ref = f32[72,8,128]{2,1,0:T(8,128)S(1)} collective-permute-done((f32[72,8,128]{2,1,0:T(8,128)S(1)}, f32[72,8,128]{2,1,0:T(8,128)S(1)}, u32[]{:S(2)}, u32[]{:S(2)}) %collective-permute-start.7) | collective-permute-done | bytes 294944 | tf_op jit(solution)/shard_map/ppermute | solution.py:722
  27.6 6.9 %shard_map.30 = (f32[16,2,8,128]{3,2,1,0:T(8,128)S(1)}, f32[4,2,8,128]{3,2,1,0:T(8,128)S(1)}, f32[4,2,8,128]{3,2,1,0:T(8,128)S(1)}, f32[32,2,24,128]{3,2,1,0:T(8...) custom-call(s32[3]{0:T(128)S(1)} %pad_add_fusion.scal, ...), custom_call_target="tpu_custom_call" | custom-call | tf_op jit(solution)/shard_map/pallas_call | solution.py:710
  34.5 0.1 collective-permute-start.8
  34.6 2.7 %collective-permute-start.9 = (f32[4,2,8,128]{3,2,1,0:T(8,128)S(1)}, f32[4,2,8,128]{3,2,1,0:T(8,128)S(1)}, u32[]{:S(2)}, u32[]{:S(2)}) collective-permute-start(f32[4,2,8,128]{3,2,1,0:T(8,128)S(1)} %get-tuple-element.41), channel_id=1, source_target_pairs={{0,7},{1,0},{2,1},{3,2},{4,3},{5,4},{6,5},{7,6},{8,15},{9,8},{10,9... | collective-permute-start | bytes 98312 | tf_op jit(solution)/shard_map/ppermute | solution.py:722
  37.2 1.3 %collective-permute-done.8.left_ref = f32[4,2,8,128]{3,2,1,0:T(8,128)S(1)} collective-permute-done((f32[4,2,8,128]{3,2,1,0:T(8,128)S(1)}, f32[4,2,8,128]{3,2,1,0:T(8,128)S(1)}, u32[]{:S(2)}, u32[]{:S(2)}) %collective-permute-start.8) | collective-permute-done | bytes 32800 | tf_op jit(solution)/shard_map/ppermute | solution.py:722
  38.5 0.0 collective-permute-done.9.right_ref
  38.5 0.2 shard_map.31.a_ref
  38.8 2.7 %collective-permute-start.12 = (f32[16,2,8,128]{3,2,1,0:T(8,128)S(1)}, f32[16,2,8,128]{3,2,1,0:T(8,128)S(1)}, u32[]{:S(2)}, u32[]{:S(2)}) collective-permute-start(f32[16,2,8,128]{3,2,1,0:T(8,128)S(1)} %shard_map.31.a_ref), channel_id=1, source_target_pairs={{0,192},{64,0},{128,64},{192,128},{1,193},{65,1},{129,65},{193,129... | collective-permute-start | bytes 393224 | tf_op jit(solution)/shard_map/ppermute | solution.py:722
  41.5 0.3 collective-permute-start.11
  41.8 0.4 collective-permute-start.10
  42.2 2.4 %collective-permute-done.12.d_ref = f32[16,2,8,128]{3,2,1,0:T(8,128)S(1)} collective-permute-done((f32[16,2,8,128]{3,2,1,0:T(8,128)S(1)}, f32[16,2,8,128]{3,2,1,0:T(8,128)S(1)}, u32[]{:S(2)}, u32[]{:S(2)}) %collective-permute-start.12) | collective-permute-done | bytes 131104 | tf_op jit(solution)/shard_map/ppermute | solution.py:722
  44.6 2.4 %collective-permute-done.11.c_ref = f32[16,2,8,128]{3,2,1,0:T(8,128)S(1)} collective-permute-done((f32[16,2,8,128]{3,2,1,0:T(8,128)S(1)}, f32[16,2,8,128]{3,2,1,0:T(8,128)S(1)}, u32[]{:S(2)}, u32[]{:S(2)}) %collective-permute-start.11) | collective-permute-done | bytes 131104 | tf_op jit(solution)/shard_map/ppermute | solution.py:722
  46.9 3.6 %collective-permute-done.10.b_ref = f32[16,2,8,128]{3,2,1,0:T(8,128)S(1)} collective-permute-done((f32[16,2,8,128]{3,2,1,0:T(8,128)S(1)}, f32[16,2,8,128]{3,2,1,0:T(8,128)S(1)}, u32[]{:S(2)}, u32[]{:S(2)}) %collective-permute-start.10) | collective-permute-done | bytes 131104 | tf_op jit(solution)/shard_map/ppermute | solution.py:722
  50.6 0.1 shard_map.32
  50.7 2.4 %collective-permute-start.13 = (f32[80,8,128]{2,1,0:T(8,128)S(1)}, f32[80,8,128]{2,1,0:T(8,128)S(1)}, u32[]{:S(2)}, u32[]{:S(2)}) collective-permute-start(f32[80,8,128]{2,1,0:T(8,128)S(1)} %get-tuple-element.42), channel_id=1, source_target_pairs={{0,8},{8,16},{16,24},{24,32},{32,40},{40,48},{48,56},{56,0},{1,9},... | collective-permute-start | bytes 983048 | tf_op jit(solution)/shard_map/ppermute | solution.py:722
  53.0 0.0 collective-permute-start.14
  53.0 4.0 %collective-permute-done.13.yl_ref = f32[80,8,128]{2,1,0:T(8,128)S(1)} collective-permute-done((f32[80,8,128]{2,1,0:T(8,128)S(1)}, f32[80,8,128]{2,1,0:T(8,128)S(1)}, u32[]{:S(2)}, u32[]{:S(2)}) %collective-permute-start.13) | collective-permute-done | bytes 327712 | tf_op jit(solution)/shard_map/ppermute | solution.py:722
  57.1 2.5 %collective-permute-done.14.yr_ref = f32[80,8,128]{2,1,0:T(8,128)S(1)} collective-permute-done((f32[80,8,128]{2,1,0:T(8,128)S(1)}, f32[80,8,128]{2,1,0:T(8,128)S(1)}, u32[]{:S(2)}, u32[]{:S(2)}) %collective-permute-start.14) | collective-permute-done | bytes 327712 | tf_op jit(solution)/shard_map/ppermute | solution.py:722
  59.5 4.6 %shard_map.33 = (f32[16,8,128]{2,1,0:T(8,128)S(1)}, f32[16,2,24,128]{3,2,1,0:T(8,128)S(1)}, f32[6,16,2,24,128]{4,3,2,1,0:T(8,128)S(1)}, f32[6,16,2,24,128]{4,3,2...) custom-call(s32[3]{0:T(128)S(1)} %pad_add_fusion.scal, ...), custom_call_target="tpu_custom_call" | custom-call | tf_op jit(solution)/shard_map/pallas_call | solution.py:710
  64.2 2.7 %collective-permute-start.17 = (f32[1,16,8,128]{3,2,1,0:T(8,128)S(1)}, f32[1,16,8,128]{3,2,1,0:T(8,128)S(1)}, u32[]{:S(2)}, u32[]{:S(2)}) collective-permute-start(f32[1,16,8,128]{3,2,1,0:T(8,128)S(1)} %bitcast.12), channel_id=1, source_target_pairs={{0,48},{8,56},{16,0},{24,8},{32,16},{40,24},{48,32},{56,40},{1,49}... | collective-permute-start | bytes 196616 | tf_op jit(solution)/shard_map/ppermute | solution.py:722
  66.8 0.2 collective-permute-start.16
  67.0 0.5 collective-permute-start.15
  67.6 1.9 %collective-permute-done.17 = f32[1,16,8,128]{3,2,1,0:T(8,128)S(1)} collective-permute-done((f32[1,16,8,128]{3,2,1,0:T(8,128)S(1)}, f32[1,16,8,128]{3,2,1,0:T(8,128)S(1)}, u32[]{:S(2)}, u32[]{:S(2)}) %collective-permute-start.17) | collective-permute-done | bytes 65568 | tf_op jit(solution)/shard_map/ppermute | solution.py:722
  69.4 2.6 %collective-permute-done.16 = f32[1,16,8,128]{3,2,1,0:T(8,128)S(1)} collective-permute-done((f32[1,16,8,128]{3,2,1,0:T(8,128)S(1)}, f32[1,16,8,128]{3,2,1,0:T(8,128)S(1)}, u32[]{:S(2)}, u32[]{:S(2)}) %collective-permute-start.16) | collective-permute-done | bytes 65568 | tf_op jit(solution)/shard_map/ppermute | solution.py:722
  72.1 1.3 %collective-permute-done.15 = f32[1,16,8,128]{3,2,1,0:T(8,128)S(1)} collective-permute-done((f32[1,16,8,128]{3,2,1,0:T(8,128)S(1)}, f32[1,16,8,128]{3,2,1,0:T(8,128)S(1)}, u32[]{:S(2)}, u32[]{:S(2)}) %collective-permute-start.15) | collective-permute-done | bytes 65568 | tf_op jit(solution)/shard_map/ppermute | solution.py:722
  73.4 2.2 %all-gather = f32[8,16,8,128]{3,2,1,0:T(8,128)S(1)} all-gather(f32[4,16,8,128]{3,2,1,0:T(8,128)S(1)} %pad_maximum_fusion), channel_id=2, replica_groups={{0,8},{16,24},{32,40},{48,56},{1,9},{17,25},{33,41},{49,57},{2,10},{18,..., dimensions={0}, use_global_device_ids=true | all-gather | bytes 786432 | tf_op jit(solution)/shard_map/all_gather | solution.py:727
  75.6 2.4 %shard_map.34 = (f32[8,8,128]{2,1,0:T(8,128)S(1)}, f32[16,2,8,128]{3,2,1,0:T(8,128)S(1)}, f32[6,16,2,8,128]{4,3,2,1,0:T(8,128)S(1)}, f32[6,16,2,8,128]{4,3,2,1,0...) custom-call(s32[3]{0:T(128)S(1)} %pad_add_fusion.scal, f32[2,4,16,8,128]{4,3,2,1,0:T(8,128)S(1)} %bitcast.10), custom_call_target="tpu_custom_call" | custom-call | tf_op jit(solution)/shard_map/pallas_call | solution.py:710
  78.1 4.0 %collective-permute-start.21 = (f32[8,8,128]{2,1,0:T(8,128)S(1)}, f32[8,8,128]{2,1,0:T(8,128)S(1)}, u32[]{:S(2)}, u32[]{:S(2)}) collective-permute-start(f32[8,8,128]{2,1,0:T(8,128)S(1)} %get-tuple-element.45.own_ref), channel_id=1, source_target_pairs={{0,4},{1,5},{2,6},{3,7},{4,0},{5,1},{6,2},{7,3},{8,12},{9,13},{10,... | collective-permute-start | bytes 98312 | tf_op jit(solution)/shard_map/ppermute | solution.py:736
  82.1 0.6 collective-permute-start.20
  82.7 3.5 %collective-permute-start.19 = (f32[8,8,128]{2,1,0:T(8,128)S(1)}, f32[8,8,128]{2,1,0:T(8,128)S(1)}, u32[]{:S(2)}, u32[]{:S(2)}) collective-permute-start(f32[8,8,128]{2,1,0:T(8,128)S(1)} %get-tuple-element.45.own_ref), channel_id=1, source_target_pairs={{0,2},{1,3},{2,4},{3,5},{4,6},{5,7},{6,0},{7,1},{8,14},{9,15},{10,... | collective-permute-start | bytes 98312 | tf_op jit(solution)/shard_map/ppermute | solution.py:736
  86.2 0.0 collective-permute-start.18
  86.2 0.0 collective-permute-done.21
  86.2 1.2 %collective-permute-done.20 = f32[8,8,128]{2,1,0:T(8,128)S(1)} collective-permute-done((f32[8,8,128]{2,1,0:T(8,128)S(1)}, f32[8,8,128]{2,1,0:T(8,128)S(1)}, u32[]{:S(2)}, u32[]{:S(2)}) %collective-permute-start.20) | collective-permute-done | bytes 32800 | tf_op jit(solution)/shard_map/ppermute | solution.py:736
  87.4 1.4 %collective-permute-done.19 = f32[8,8,128]{2,1,0:T(8,128)S(1)} collective-permute-done((f32[8,8,128]{2,1,0:T(8,128)S(1)}, f32[8,8,128]{2,1,0:T(8,128)S(1)}, u32[]{:S(2)}, u32[]{:S(2)}) %collective-permute-start.19) | collective-permute-done | bytes 32800 | tf_op jit(solution)/shard_map/ppermute | solution.py:736
  88.8 0.5 collective-permute-done.18
  89.3 3.5 %all-gather.1 = f32[8,8,8,128]{3,2,1,0:T(8,128)S(1)} all-gather(f32[4,8,8,128]{3,2,1,0:T(8,128)S(1)} %pad_maximum_fusion.1), channel_id=3, replica_groups={{0,8},{16,24},{32,40},{48,56},{1,9},{17,25},{33,41},{49,57},{2,10},{18,..., dimensions={0}, use_global_device_ids=true | all-gather | bytes 393216 | tf_op jit(solution)/shard_map/all_gather | solution.py:727
  92.8 11.9 %shard_map.35 = f32[16,32,128]{2,1,0:T(8,128)} custom-call(s32[3]{0:T(128)S(1)} %pad_add_fusion.scal, f32[8,8,128]{2,1,0:T(8,128)S(1)} %get-tuple-element.45.own_ref, f32[2,4,8,8,128]{4,3,2,1,0:T(8,128)S(1)} %bitcast.11, f32[16,2,8,128]{3,2,1,0:T(8,128)S(1)} %get-tuple-element.46.refs_0_, f32[6,16,2,8,128]{4,3,2,1,0:T(8,128)S(1)} %get-tuple-element.47.refs_1_, ...), custom_call_target="tpu_custom_call" | custom-call | tf_op jit(solution)/shard_map/pallas_call | solution.py:710
  (6 shorter events, 0.0 us)
Async XLA Ops:
  0.0 0.9 copy-start
  1.0 0.9 copy-start.1
  2.9 9.3 %collective-permute-start.2 = (f32[2,2,16,128]{3,2,1,0:T(8,128)S(1)}, f32[2,2,16,128]{3,2,1,0:T(8,128)S(1)}, u32[]{:S(2)}, u32[]{:S(2)}) collective-permute-start(f32[2,2,16,128]{3,2,1,0:T(8,128)S(1)} %get-tuple-element.35), channel_id=1, source_target_pairs={{0,1},{1,2},{2,3},{3,4},{4,5},{5,6},{6,7},{7,0},{8,9},{9,10},{10,1... | collective-permute-start | bytes 98312 | tf_op jit(solution)/shard_map/ppermute | solution.py:722
  5.5 6.7 %collective-permute-start.3 = (f32[2,2,16,128]{3,2,1,0:T(8,128)S(1)}, f32[2,2,16,128]{3,2,1,0:T(8,128)S(1)}, u32[]{:S(2)}, u32[]{:S(2)}) collective-permute-start(f32[2,2,16,128]{3,2,1,0:T(8,128)S(1)} %get-tuple-element.36), channel_id=1, source_target_pairs={{0,7},{1,0},{2,1},{3,2},{4,3},{5,4},{6,5},{7,6},{8,15},{9,8},{10,9... | collective-permute-start | bytes 98312 | tf_op jit(solution)/shard_map/ppermute | solution.py:722
  9.5 8.8 %collective-permute-start = (f32[16,2,16,128]{3,2,1,0:T(8,128)S(1)}, f32[16,2,16,128]{3,2,1,0:T(8,128)S(1)}, u32[]{:S(2)}, u32[]{:S(2)}) collective-permute-start(f32[16,2,16,128]{3,2,1,0:T(8,128)S(1)} %get-tuple-element.33.refs_2_.m2), channel_id=1, source_target_pairs={{0,64},{64,128},{128,192},{192,0},{1,65},{65,129},{129,193},{193,1... | collective-permute-start | bytes 786440 | tf_op jit(solution)/shard_map/ppermute | solution.py:722
  10.7 7.6 %collective-permute-start.1 = (f32[16,2,16,128]{3,2,1,0:T(8,128)S(1)}, f32[16,2,16,128]{3,2,1,0:T(8,128)S(1)}, u32[]{:S(2)}, u32[]{:S(2)}) collective-permute-start(f32[16,2,16,128]{3,2,1,0:T(8,128)S(1)} %get-tuple-element.34.refs_1_.m1), channel_id=1, source_target_pairs={{0,192},{64,0},{128,64},{192,128},{1,193},{65,1},{129,65},{193,129... | collective-permute-start | bytes 786440 | tf_op jit(solution)/shard_map/ppermute | solution.py:722
  12.2 6.1 %collective-permute-start.4 = (f32[2,2,16,128]{3,2,1,0:T(8,128)S(1)}, f32[2,2,16,128]{3,2,1,0:T(8,128)S(1)}, u32[]{:S(2)}, u32[]{:S(2)}) collective-permute-start(f32[2,2,16,128]{3,2,1,0:T(8,128)S(1)} %pad_maximum_fusion.2.refs_6_.s2), channel_id=1, source_target_pairs={{0,64},{64,128},{128,192},{192,0},{1,65},{65,129},{129,193},{193,1... | collective-permute-start | bytes 98312 | tf_op jit(solution)/shard_map/ppermute | solution.py:722
  12.3 6.0 %collective-permute-start.5 = (f32[2,2,16,128]{3,2,1,0:T(8,128)S(1)}, f32[2,2,16,128]{3,2,1,0:T(8,128)S(1)}, u32[]{:S(2)}, u32[]{:S(2)}) collective-permute-start(f32[2,2,16,128]{3,2,1,0:T(8,128)S(1)} %pad_maximum_fusion.3.refs_5_.s1), channel_id=1, source_target_pairs={{0,192},{64,0},{128,64},{192,128},{1,193},{65,1},{129,65},{193,129... | collective-permute-start | bytes 98312 | tf_op jit(solution)/shard_map/ppermute | solution.py:722
  18.4 6.7 %collective-permute-start.6 = (f32[72,8,128]{2,1,0:T(8,128)S(1)}, f32[72,8,128]{2,1,0:T(8,128)S(1)}, u32[]{:S(2)}, u32[]{:S(2)}) collective-permute-start(f32[72,8,128]{2,1,0:T(8,128)S(1)} %get-tuple-element.37), channel_id=1, source_target_pairs={{0,8},{8,16},{16,24},{24,32},{32,40},{40,48},{48,56},{56,0},{1,9},... | collective-permute-start | bytes 884744 | tf_op jit(solution)/shard_map/ppermute | solution.py:722
  21.4 6.1 %collective-permute-start.7 = (f32[72,8,128]{2,1,0:T(8,128)S(1)}, f32[72,8,128]{2,1,0:T(8,128)S(1)}, u32[]{:S(2)}, u32[]{:S(2)}) collective-permute-start(f32[72,8,128]{2,1,0:T(8,128)S(1)} %get-tuple-element.38), channel_id=1, source_target_pairs={{0,56},{8,0},{16,8},{24,16},{32,24},{40,32},{48,40},{56,48},{1,57}... | collective-permute-start | bytes 884744 | tf_op jit(solution)/shard_map/ppermute | solution.py:722
  34.5 4.1 %collective-permute-start.8 = (f32[4,2,8,128]{3,2,1,0:T(8,128)S(1)}, f32[4,2,8,128]{3,2,1,0:T(8,128)S(1)}, u32[]{:S(2)}, u32[]{:S(2)}) collective-permute-start(f32[4,2,8,128]{3,2,1,0:T(8,128)S(1)} %get-tuple-element.40), channel_id=1, source_target_pairs={{0,1},{1,2},{2,3},{3,4},{4,5},{5,6},{6,7},{7,0},{8,9},{9,10},{10,1... | collective-permute-start | bytes 98312 | tf_op jit(solution)/shard_map/ppermute | solution.py:722
  34.6 4.0 %collective-permute-start.9 = (f32[4,2,8,128]{3,2,1,0:T(8,128)S(1)}, f32[4,2,8,128]{3,2,1,0:T(8,128)S(1)}, u32[]{:S(2)}, u32[]{:S(2)}) collective-permute-start(f32[4,2,8,128]{3,2,1,0:T(8,128)S(1)} %get-tuple-element.41), channel_id=1, source_target_pairs={{0,7},{1,0},{2,1},{3,2},{4,3},{5,4},{6,5},{7,6},{8,15},{9,8},{10,9... | collective-permute-start | bytes 98312 | tf_op jit(solution)/shard_map/ppermute | solution.py:722
  38.8 5.8 %collective-permute-start.12 = (f32[16,2,8,128]{3,2,1,0:T(8,128)S(1)}, f32[16,2,8,128]{3,2,1,0:T(8,128)S(1)}, u32[]{:S(2)}, u32[]{:S(2)}) collective-permute-start(f32[16,2,8,128]{3,2,1,0:T(8,128)S(1)} %shard_map.31.a_ref), channel_id=1, source_target_pairs={{0,192},{64,0},{128,64},{192,128},{1,193},{65,1},{129,65},{193,129... | collective-permute-start | bytes 393224 | tf_op jit(solution)/shard_map/ppermute | solution.py:722
  41.5 5.4 %collective-permute-start.11 = (f32[16,2,8,128]{3,2,1,0:T(8,128)S(1)}, f32[16,2,8,128]{3,2,1,0:T(8,128)S(1)}, u32[]{:S(2)}, u32[]{:S(2)}) collective-permute-start(f32[16,2,8,128]{3,2,1,0:T(8,128)S(1)} %shard_map.31.a_ref), channel_id=1, source_target_pairs={{0,128},{64,192},{128,0},{192,64},{1,129},{65,193},{129,1},{193,65... | collective-permute-start | bytes 393224 | tf_op jit(solution)/shard_map/ppermute | solution.py:722
  41.8 8.7 %collective-permute-start.10 = (f32[16,2,8,128]{3,2,1,0:T(8,128)S(1)}, f32[16,2,8,128]{3,2,1,0:T(8,128)S(1)}, u32[]{:S(2)}, u32[]{:S(2)}) collective-permute-start(f32[16,2,8,128]{3,2,1,0:T(8,128)S(1)} %shard_map.31.a_ref), channel_id=1, source_target_pairs={{0,64},{64,128},{128,192},{192,0},{1,65},{65,129},{129,193},{193,1... | collective-permute-start | bytes 393224 | tf_op jit(solution)/shard_map/ppermute | solution.py:722
  50.7 6.4 %collective-permute-start.13 = (f32[80,8,128]{2,1,0:T(8,128)S(1)}, f32[80,8,128]{2,1,0:T(8,128)S(1)}, u32[]{:S(2)}, u32[]{:S(2)}) collective-permute-start(f32[80,8,128]{2,1,0:T(8,128)S(1)} %get-tuple-element.42), channel_id=1, source_target_pairs={{0,8},{8,16},{16,24},{24,32},{32,40},{40,48},{48,56},{56,0},{1,9},... | collective-permute-start | bytes 983048 | tf_op jit(solution)/shard_map/ppermute | solution.py:722
  53.0 6.5 %collective-permute-start.14 = (f32[80,8,128]{2,1,0:T(8,128)S(1)}, f32[80,8,128]{2,1,0:T(8,128)S(1)}, u32[]{:S(2)}, u32[]{:S(2)}) collective-permute-start(f32[80,8,128]{2,1,0:T(8,128)S(1)} %get-tuple-element.43), channel_id=1, source_target_pairs={{0,56},{8,0},{16,8},{24,16},{32,24},{40,32},{48,40},{56,48},{1,57}... | collective-permute-start | bytes 983048 | tf_op jit(solution)/shard_map/ppermute | solution.py:722
  64.2 5.3 %collective-permute-start.17 = (f32[1,16,8,128]{3,2,1,0:T(8,128)S(1)}, f32[1,16,8,128]{3,2,1,0:T(8,128)S(1)}, u32[]{:S(2)}, u32[]{:S(2)}) collective-permute-start(f32[1,16,8,128]{3,2,1,0:T(8,128)S(1)} %bitcast.12), channel_id=1, source_target_pairs={{0,48},{8,56},{16,0},{24,8},{32,16},{40,24},{48,32},{56,40},{1,49}... | collective-permute-start | bytes 196616 | tf_op jit(solution)/shard_map/ppermute | solution.py:722
  66.8 5.2 %collective-permute-start.16 = (f32[1,16,8,128]{3,2,1,0:T(8,128)S(1)}, f32[1,16,8,128]{3,2,1,0:T(8,128)S(1)}, u32[]{:S(2)}, u32[]{:S(2)}) collective-permute-start(f32[1,16,8,128]{3,2,1,0:T(8,128)S(1)} %bitcast.13), channel_id=1, source_target_pairs={{0,32},{8,40},{16,48},{24,56},{32,0},{40,8},{48,16},{56,24},{1,33}... | collective-permute-start | bytes 196616 | tf_op jit(solution)/shard_map/ppermute | solution.py:722
  67.0 6.4 %collective-permute-start.15 = (f32[1,16,8,128]{3,2,1,0:T(8,128)S(1)}, f32[1,16,8,128]{3,2,1,0:T(8,128)S(1)}, u32[]{:S(2)}, u32[]{:S(2)}) collective-permute-start(f32[1,16,8,128]{3,2,1,0:T(8,128)S(1)} %bitcast.14), channel_id=1, source_target_pairs={{0,16},{8,24},{16,32},{24,40},{32,48},{40,56},{48,0},{56,8},{1,17}... | collective-permute-start | bytes 196616 | tf_op jit(solution)/shard_map/ppermute | solution.py:722
  78.1 8.2 %collective-permute-start.21 = (f32[8,8,128]{2,1,0:T(8,128)S(1)}, f32[8,8,128]{2,1,0:T(8,128)S(1)}, u32[]{:S(2)}, u32[]{:S(2)}) collective-permute-start(f32[8,8,128]{2,1,0:T(8,128)S(1)} %get-tuple-element.45.own_ref), channel_id=1, source_target_pairs={{0,4},{1,5},{2,6},{3,7},{4,0},{5,1},{6,2},{7,3},{8,12},{9,13},{10,... | collective-permute-start | bytes 98312 | tf_op jit(solution)/shard_map/ppermute | solution.py:736
  82.1 5.3 %collective-permute-start.20 = (f32[8,8,128]{2,1,0:T(8,128)S(1)}, f32[8,8,128]{2,1,0:T(8,128)S(1)}, u32[]{:S(2)}, u32[]{:S(2)}) collective-permute-start(f32[8,8,128]{2,1,0:T(8,128)S(1)} %get-tuple-element.45.own_ref), channel_id=1, source_target_pairs={{0,3},{1,4},{2,5},{3,6},{4,7},{5,0},{6,1},{7,2},{8,13},{9,14},{10,... | collective-permute-start | bytes 98312 | tf_op jit(solution)/shard_map/ppermute | solution.py:736
  82.7 6.1 %collective-permute-start.19 = (f32[8,8,128]{2,1,0:T(8,128)S(1)}, f32[8,8,128]{2,1,0:T(8,128)S(1)}, u32[]{:S(2)}, u32[]{:S(2)}) collective-permute-start(f32[8,8,128]{2,1,0:T(8,128)S(1)} %get-tuple-element.45.own_ref), channel_id=1, source_target_pairs={{0,2},{1,3},{2,4},{3,5},{4,6},{5,7},{6,0},{7,1},{8,14},{9,15},{10,... | collective-permute-start | bytes 98312 | tf_op jit(solution)/shard_map/ppermute | solution.py:736
  86.2 3.1 %collective-permute-start.18 = (f32[8,8,128]{2,1,0:T(8,128)S(1)}, f32[8,8,128]{2,1,0:T(8,128)S(1)}, u32[]{:S(2)}, u32[]{:S(2)}) collective-permute-start(f32[8,8,128]{2,1,0:T(8,128)S(1)} %get-tuple-element.45.own_ref), channel_id=1, source_target_pairs={{0,1},{1,2},{2,3},{3,4},{4,5},{5,6},{6,7},{7,0},{8,15},{9,8},{10,9... | collective-permute-start | bytes 98312 | tf_op jit(solution)/shard_map/ppermute | solution.py:736

commit v4 on v3

--- a/solution.py
+++ b/solution.py
@@ -71,12 +71,22 @@
     return (colour == 0) == ((a + q) % 2 == 0)
 
 
-def beside(level, other, x, q, colour, a):
-    mid = other[x + 1, q]
-    across = other[x + 1, 1 - q]
+class Window:
+    def __init__(self, ref, first):
+        self.ref, self.first, self.kept = ref, first, {}
+
+    def __call__(self, offset, q):
+        if (offset, q) not in self.kept:
+            self.kept[offset, q] = self.ref[self.first + offset, q]
+        return self.kept[offset, q]
+
+
+def beside(level, other, at, q, colour, a):
+    mid = other(at + 1, q)
+    across = other(at + 1, 1 - q)
     return [
-        other[x + 2, q],
-        other[x, q],
+        other(at + 2, q),
+        other(at, q),
         across if q == 0 else up(level, across),
         down(level, across) if q == 0 else across,
         mid,
@@ -84,17 +94,21 @@
     ]
 
 
-def planes(first, last, unroll, body):
+def planes(first, last, unroll, body, *refs):
     pairs = (last - first) // 2
     unroll = min(unroll, pairs)
     while pairs % unroll:
         unroll -= 1
 
     def step(i, carry):
-        for u in range(unroll):
-            for a in (0, 1):
-                for q in (0, 1):
-                    body(first + 2 * (unroll * i + u) + a, a, q)
+        start = first + 2 * unroll * i
+        windows = [Window(ref, start) for ref in refs]
+        for at in range(2 * unroll):
+            for q in (0, 1):
+                if refs:
+                    body(start + at, at, q, windows)
+                else:
+                    body(start + at, at % 2, q)
         return carry
 
     if pairs == unroll:
@@ -120,10 +134,11 @@
     for colour in (0, 1):
         fill_ends(level, rec[colour], OFF)
 
-    def body(x, a, q):
+    def body(x, at, q, windows):
+        a = at % 2
         for colour in (0, 1):
-            own_rec = rec[colour][x + 1, q]
-            near = beside(level, rec[1 - colour], x, q, colour, a)
+            own_rec = windows[colour](at + 1, q)
+            near = beside(level, windows[1 - colour], at, q, colour, a)
             walls = {}
             if level.fold == "y":
                 if q == 0:
@@ -149,11 +164,11 @@
             if colour == 0:
                 dd[x, q] = total
 
-    planes(0, level.count, 4 if level.rows == 8 else 1, body)
-
-
-def relaxed(level, colour, x, a, q, v, wd, fd):
-    near = beside(level, v[1 - colour], x, q, colour, a)
+    planes(0, level.count, 4 if level.rows == 8 else 1, body, *rec)
+
+
+def relaxed(level, colour, x, at, q, window, wd, fd):
+    near = beside(level, window, at, q, colour, at % 2)
     weight = wd[colour]
     one = fd[colour][x, q] + weight[0, x, q] * near[0]
     two = weight[4, x, q] * near[4] + weight[1, x, q] * near[1]
@@ -163,10 +178,10 @@
 
 
 def half_sweep(level, colour, v, wd, fd, first=0, last=None):
-    def body(x, a, q):
-        v[colour][x + 1, q] = relaxed(level, colour, x, a, q, v, wd, fd)
-
-    planes(first, level.count if last is None else last, 8 if level.rows == 8 else 4, body)
+    def body(x, at, q, windows):
+        v[colour][x + 1, q] = relaxed(level, colour, x, at, q, windows[0], wd, fd)
+
+    planes(first, level.count if last is None else last, 8 if level.rows == 8 else 4, body, v[1 - colour])
     if level.fold == "x":
         fill_ends(level, v[colour])
 
@@ -192,13 +207,15 @@
     first, last = ranges[3]
 
     def body(i, carry):
+        window = Window(v[1], first + 4 * i)
         for u in (0, 1):
             left = jnp.zeros((level.rows, 128), F32)
             mean = jnp.zeros((level.rows, 128), F32)
             for a in (0, 1):
                 for q in (0, 1):
-                    x = first + 4 * i + 2 * u + a
-                    left = left + dd[x, q] * (relaxed(level, 0, x, a, q, v, wd, fd) - v[0][x + 1, q])
+                    at = 2 * u + a
+                    x = first + 4 * i + at
+                    left = left + dd[x, q] * (relaxed(level, 0, x, at, q, window, wd, fd) - v[0][x + 1, q])
                     mean = mean + (cond[0][x, q] + cond[1][x, q])
             out_f[2 * i + u] = left
             out_b[2 * i + u] = 0.125 * mean
@@ -412,7 +429,7 @@
             return jnp.where(row == (3 if block == 0 else 4), single, cells)
 
         def body(j, carry):
-            slots = [(gx + 4 - j) % 4, (gx + 6 - j) % 4]
+            slots = [gx ^ j, gx ^ (j + 2)]
             for x in range(8):
                 for q in (0, 1):
                     parts = []
@@ -454,7 +471,7 @@
     lane = lanes(8)
     k = lane % 32
     inside = ((gz > 0) | (k >= 8)) & ((gz < 7) | (k < 24))
-    slots = [(chip + 4 - j) % 4 for j in range(4)]
+    slots = [chip ^ j for j in range(4)]
 
     def body(x, a, q):
         mains = []
@@ -722,6 +739,10 @@
     return lax.ppermute(values, axis, [(i, (i + step) % count) for i in range(count)])
 
 
+def trade(values, axis, step):
+    return lax.ppermute(values, axis, [(i, i ^ step) for i in range(lax.axis_size(axis))])
+
+
 def both_cores(values):
     count = lax.axis_size("gy")
     return lax.all_gather(values, "gy", axis=0, axis_index_groups=[[i, i + 1] for i in range(0, count, 2)])
@@ -756,7 +777,7 @@
     )
     from_left, from_right = ring(zr, "gz", 1), ring(zl, "gz", -1)
     bundle = call(widen_kernel, arr(16, 2, 8, 128), [], own, from_left, from_right)
-    column = [bundle] + [ring(bundle, "gx", s) for s in (1, 2, 3)]
+    column = [bundle] + [trade(bundle, "gx", s) for s in (1, 2, 3)]
     yl, yr = call(strip_kernel, [arr(80, 8, 128)] * 2, [], *column)
     own, black1, *set1 = call(
         level1_down_kernel,
@@ -765,7 +786,7 @@
         *column, ring(yr, "gy", 1), ring(yl, "gy", -1), scal=scal,
     )
     own = own[None]
-    sheet = jnp.concatenate([own] + [ring(own, "gy", 2 * s) for s in (1, 2, 3)])
+    sheet = jnp.concatenate([own] + [trade(own, "gy", 2 * s) for s in (1, 2, 3)])
     sheet = both_cores(sheet)
     own, black2, *set2 = call(
         level2_down_kernel,

time: 105 us -> 101 us (0.962)
  waiting for transfers between devices: 34.4 us -> 29.6 us
  starting transfers between devices: 35.2 us -> 37.3 us
    ppermute x18 -> x12, waiting for transfers between devices: 31.4 us -> 17.5 us  [ring(): lax.ppermute(values, axis, [(i, (i + step) % count) for i in range(count)])]
    ppermute x0 -> x6, waiting for transfers between devices: none -> 9.12 us  [trade(): lax.ppermute(values, axis, [(i, i ^ step) for i in range(lax.axis_size(ax...]
    ppermute x0 -> x6, starting transfers between devices: none -> 7.44 us  [trade(): lax.ppermute(values, axis, [(i, i ^ step) for i in range(lax.axis_size(ax...]
    ppermute x18 -> x12, starting transfers between devices: 27 us -> 21.6 us  [ring(): lax.ppermute(values, axis, [(i, (i + step) % count) for i in range(count)])]
  transfers between devices with their start and end apart: 22 -> 22, of which waited for: 15 -> 12; matrix products, arithmetic and copies ran while one was open for 0% -> 0% of each run, Pallas kernels for 0% -> 0%
where the time goes in v4:
time: 101 us
  starting transfers between devices  37.3 us (37%)
  waiting for transfers between devices  29.6 us (29%)
  Pallas kernels  26.7 us (26%)
  blocking collectives  5.45 us (5%)
  local copies, waits for them, and re-layouts  1.91 us (2%)
    pallas_call x8, Pallas kernels, call(): pl.pallas_call(kernel, out_shape=outs, in_specs=specs, out_specs=jax.tree...  26.7 us
    ppermute x12, starting transfers between devices, ring(): lax.ppermute(values, axis, [(i, (i + step) % count) for i in range(count)])  21.6 us
    ppermute x12, waiting for transfers between devices, ring(): lax.ppermute(values, axis, [(i, (i + step) % count) for i in range(count)])  17.5 us
    ppermute x6, waiting for transfers between devices, trade(): lax.ppermute(values, axis, [(i, i ^ step) for i in range(lax.axis_size(ax...  9.12 us
    ppermute x4, starting transfers between devices, along_z(): return lax.ppermute(values, ('gy', 'gz'), pairs)  8.25 us
    ppermute x6, starting transfers between devices, trade(): lax.ppermute(values, axis, [(i, i ^ step) for i in range(lax.axis_size(ax...  7.44 us
    all_gather x2, blocking collectives, both_cores(): lax.all_gather(values, 'gy', axis=0, axis_index_groups=[[i, i + 1] for i...  5.45 us
    ppermute x4, waiting for transfers between devices, along_z(): return lax.ppermute(values, ('gy', 'gz'), pairs)  3.06 us
  transfers between devices with their start and end apart: 22, of which 12 were waited for; matrix products, arithmetic and copies ran while one was open for 0% of the time, Pallas kernels for 0%

profile of v4, /device:TPU:1, one launch (start us, length us, event | category | flops | bytes accessed | tf_op | source)
XLA Modules:
  0.0 101.3 jit_solution(4475554580630003378)
XLA Ops:
  0.0 0.0 copy-start
  0.0 0.9 copy-done
  1.0 0.0 copy-start.1
  1.0 0.9 copy-done.1
  1.9 1.0 %shard_map.28 = (f32[16,2,16,128]{3,2,1,0:T(8,128)S(1)}, f32[16,2,16,128]{3,2,1,0:T(8,128)S(1)}, f32[2,2,16,128]{3,2,1,0:T(8,128)S(1)}, f32[2,2,16,128]{3,2,1,0:T(8,128)S(1)}) custom-call(f32[16,32,128]{2,1,0:T(8,128)S(1)} %copy-done, f32[16,32,128]{2,1,0:T(8,128)S(1)} %copy-done.1), custom_call_target="tpu_custom_call" | custom-call | tf_op jit(solution)/shard_map/pallas_call | solution.py:727
  2.9 2.5 %collective-permute-start.2 = (f32[2,2,16,128]{3,2,1,0:T(8,128)S(1)}, f32[2,2,16,128]{3,2,1,0:T(8,128)S(1)}, u32[]{:S(2)}, u32[]{:S(2)}) collective-permute-start(f32[2,2,16,128]{3,2,1,0:T(8,128)S(1)} %get-tuple-element.35), channel_id=1, source_target_pairs={{0,1},{1,2},{2,3},{3,4},{4,5},{5,6},{6,7},{7,0},{8,9},{9,10},{10,1... | collective-permute-start | bytes 98312 | tf_op jit(solution)/shard_map/ppermute | solution.py:739
  5.5 4.0 %collective-permute-start.3 = (f32[2,2,16,128]{3,2,1,0:T(8,128)S(1)}, f32[2,2,16,128]{3,2,1,0:T(8,128)S(1)}, u32[]{:S(2)}, u32[]{:S(2)}) collective-permute-start(f32[2,2,16,128]{3,2,1,0:T(8,128)S(1)} %get-tuple-element.36), channel_id=1, source_target_pairs={{0,7},{1,0},{2,1},{3,2},{4,3},{5,4},{6,5},{7,6},{8,15},{9,8},{10,9... | collective-permute-start | bytes 98312 | tf_op jit(solution)/shard_map/ppermute | solution.py:739
  9.5 1.2 %collective-permute-start = (f32[16,2,16,128]{3,2,1,0:T(8,128)S(1)}, f32[16,2,16,128]{3,2,1,0:T(8,128)S(1)}, u32[]{:S(2)}, u32[]{:S(2)}) collective-permute-start(f32[16,2,16,128]{3,2,1,0:T(8,128)S(1)} %get-tuple-element.33.refs_2_.m2), channel_id=1, source_target_pairs={{0,64},{64,128},{128,192},{192,0},{1,65},{65,129},{129,193},{193,1... | collective-permute-start | bytes 786440 | tf_op jit(solution)/shard_map/ppermute | solution.py:739
  10.7 1.5 %collective-permute-start.1 = (f32[16,2,16,128]{3,2,1,0:T(8,128)S(1)}, f32[16,2,16,128]{3,2,1,0:T(8,128)S(1)}, u32[]{:S(2)}, u32[]{:S(2)}) collective-permute-start(f32[16,2,16,128]{3,2,1,0:T(8,128)S(1)} %get-tuple-element.34.refs_1_.m1), channel_id=1, source_target_pairs={{0,192},{64,0},{128,64},{192,128},{1,193},{65,1},{129,65},{193,129... | collective-permute-start | bytes 786440 | tf_op jit(solution)/shard_map/ppermute | solution.py:739
  12.2 0.0 collective-permute-done.2
  12.2 0.0 collective-permute-done.3
  12.2 0.1 collective-permute-start.4
  12.3 2.7 %collective-permute-start.5 = (f32[2,2,16,128]{3,2,1,0:T(8,128)S(1)}, f32[2,2,16,128]{3,2,1,0:T(8,128)S(1)}, u32[]{:S(2)}, u32[]{:S(2)}) collective-permute-start(f32[2,2,16,128]{3,2,1,0:T(8,128)S(1)} %pad_maximum_fusion.3.refs_5_.s1), channel_id=1, source_target_pairs={{0,192},{64,0},{128,64},{192,128},{1,193},{65,1},{129,65},{193,129... | collective-permute-start | bytes 98312 | tf_op jit(solution)/shard_map/ppermute | solution.py:739
  15.0 3.3 %collective-permute-done.4.refs_4_.s0 = f32[2,2,16,128]{3,2,1,0:T(8,128)S(1)} collective-permute-done((f32[2,2,16,128]{3,2,1,0:T(8,128)S(1)}, f32[2,2,16,128]{3,2,1,0:T(8,128)S(1)}, u32[]{:S(2)}, u32[]{:S(2)}) %collective-permute-start.4) | collective-permute-done | bytes 32800 | tf_op jit(solution)/shard_map/ppermute | solution.py:739
  18.3 0.0 collective-permute-done.5.refs_7_.s3
  18.3 0.0 collective-permute-done.refs_0_.m0
  18.3 0.0 collective-permute-done.1.refs_3_.m3
  18.3 0.1 shard_map.29
  18.4 3.1 %collective-permute-start.6 = (f32[72,8,128]{2,1,0:T(8,128)S(1)}, f32[72,8,128]{2,1,0:T(8,128)S(1)}, u32[]{:S(2)}, u32[]{:S(2)}) collective-permute-start(f32[72,8,128]{2,1,0:T(8,128)S(1)} %get-tuple-element.37), channel_id=1, source_target_pairs={{0,8},{8,16},{16,24},{24,32},{32,40},{40,48},{48,56},{56,0},{1,9},... | collective-permute-start | bytes 884744 | tf_op jit(solution)/shard_map/ppermute | solution.py:739
  21.4 0.0 collective-permute-start.7
  21.4 0.1 pad_add_fusion.scal
  21.5 3.6 %collective-permute-done.6.yl_ref = f32[72,8,128]{2,1,0:T(8,128)S(1)} collective-permute-done((f32[72,8,128]{2,1,0:T(8,128)S(1)}, f32[72,8,128]{2,1,0:T(8,128)S(1)}, u32[]{:S(2)}, u32[]{:S(2)}) %collective-permute-start.6) | collective-permute-done | bytes 294944 | tf_op jit(solution)/shard_map/ppermute | solution.py:739
  25.1 2.5 %collective-permute-done.7.yr_ref = f32[72,8,128]{2,1,0:T(8,128)S(1)} collective-permute-done((f32[72,8,128]{2,1,0:T(8,128)S(1)}, f32[72,8,128]{2,1,0:T(8,128)S(1)}, u32[]{:S(2)}, u32[]{:S(2)}) %collective-permute-start.7) | collective-permute-done | bytes 294944 | tf_op jit(solution)/shard_map/ppermute | solution.py:739
  27.6 6.7 %shard_map.30 = (f32[16,2,8,128]{3,2,1,0:T(8,128)S(1)}, f32[4,2,8,128]{3,2,1,0:T(8,128)S(1)}, f32[4,2,8,128]{3,2,1,0:T(8,128)S(1)}, f32[32,2,24,128]{3,2,1,0:T(8...) custom-call(s32[3]{0:T(128)S(1)} %pad_add_fusion.scal, ...), custom_call_target="tpu_custom_call" | custom-call | tf_op jit(solution)/shard_map/pallas_call | solution.py:727
  34.3 0.1 collective-permute-start.8
  34.4 2.7 %collective-permute-start.9 = (f32[4,2,8,128]{3,2,1,0:T(8,128)S(1)}, f32[4,2,8,128]{3,2,1,0:T(8,128)S(1)}, u32[]{:S(2)}, u32[]{:S(2)}) collective-permute-start(f32[4,2,8,128]{3,2,1,0:T(8,128)S(1)} %get-tuple-element.41), channel_id=1, source_target_pairs={{0,7},{1,0},{2,1},{3,2},{4,3},{5,4},{6,5},{7,6},{8,15},{9,8},{10,9... | collective-permute-start | bytes 98312 | tf_op jit(solution)/shard_map/ppermute | solution.py:739
  37.0 1.3 %collective-permute-done.8.left_ref = f32[4,2,8,128]{3,2,1,0:T(8,128)S(1)} collective-permute-done((f32[4,2,8,128]{3,2,1,0:T(8,128)S(1)}, f32[4,2,8,128]{3,2,1,0:T(8,128)S(1)}, u32[]{:S(2)}, u32[]{:S(2)}) %collective-permute-start.8) | collective-permute-done | bytes 32800 | tf_op jit(solution)/shard_map/ppermute | solution.py:739
  38.3 0.0 collective-permute-done.9.right_ref
  38.3 0.2 shard_map.31.a_ref
  38.6 2.8 %collective-permute-start.12 = (f32[16,2,8,128]{3,2,1,0:T(8,128)S(1)}, f32[16,2,8,128]{3,2,1,0:T(8,128)S(1)}, u32[]{:S(2)}, u32[]{:S(2)}) collective-permute-start(f32[16,2,8,128]{3,2,1,0:T(8,128)S(1)} %shard_map.31.a_ref), channel_id=1, source_target_pairs={{0,192},{64,128},{128,64},{192,0},{1,193},{65,129},{129,65},{193,1... | collective-permute-start | bytes 393224 | tf_op jit(solution)/shard_map/ppermute | solution.py:743
  41.3 0.3 collective-permute-start.11
  41.6 0.4 collective-permute-start.10
  42.0 4.7 %collective-permute-done.12.d_ref = f32[16,2,8,128]{3,2,1,0:T(8,128)S(1)} collective-permute-done((f32[16,2,8,128]{3,2,1,0:T(8,128)S(1)}, f32[16,2,8,128]{3,2,1,0:T(8,128)S(1)}, u32[]{:S(2)}, u32[]{:S(2)}) %collective-permute-start.12) | collective-permute-done | bytes 131104 | tf_op jit(solution)/shard_map/ppermute | solution.py:743
  46.7 0.0 collective-permute-done.11.c_ref
  46.7 0.0 collective-permute-done.10.b_ref
  46.8 0.1 shard_map.32
  46.9 3.8 %collective-permute-start.13 = (f32[80,8,128]{2,1,0:T(8,128)S(1)}, f32[80,8,128]{2,1,0:T(8,128)S(1)}, u32[]{:S(2)}, u32[]{:S(2)}) collective-permute-start(f32[80,8,128]{2,1,0:T(8,128)S(1)} %get-tuple-element.42), channel_id=1, source_target_pairs={{0,8},{8,16},{16,24},{24,32},{32,40},{40,48},{48,56},{56,0},{1,9},... | collective-permute-start | bytes 983048 | tf_op jit(solution)/shard_map/ppermute | solution.py:739
  50.7 0.0 collective-permute-start.14
  50.7 4.0 %collective-permute-done.13.yl_ref = f32[80,8,128]{2,1,0:T(8,128)S(1)} collective-permute-done((f32[80,8,128]{2,1,0:T(8,128)S(1)}, f32[80,8,128]{2,1,0:T(8,128)S(1)}, u32[]{:S(2)}, u32[]{:S(2)}) %collective-permute-start.13) | collective-permute-done | bytes 327712 | tf_op jit(solution)/shard_map/ppermute | solution.py:739
  54.7 2.8 %collective-permute-done.14.yr_ref = f32[80,8,128]{2,1,0:T(8,128)S(1)} collective-permute-done((f32[80,8,128]{2,1,0:T(8,128)S(1)}, f32[80,8,128]{2,1,0:T(8,128)S(1)}, u32[]{:S(2)}, u32[]{:S(2)}) %collective-permute-start.14) | collective-permute-done | bytes 327712 | tf_op jit(solution)/shard_map/ppermute | solution.py:739
  57.5 4.5 %shard_map.33 = (f32[16,8,128]{2,1,0:T(8,128)S(1)}, f32[16,2,24,128]{3,2,1,0:T(8,128)S(1)}, f32[6,16,2,24,128]{4,3,2,1,0:T(8,128)S(1)}, f32[6,16,2,24,128]{4,3,2...) custom-call(s32[3]{0:T(128)S(1)} %pad_add_fusion.scal, ...), custom_call_target="tpu_custom_call" | custom-call | tf_op jit(solution)/shard_map/pallas_call | solution.py:727
  62.1 3.3 %collective-permute-start.17 = (f32[1,16,8,128]{3,2,1,0:T(8,128)S(1)}, f32[1,16,8,128]{3,2,1,0:T(8,128)S(1)}, u32[]{:S(2)}, u32[]{:S(2)}) collective-permute-start(f32[1,16,8,128]{3,2,1,0:T(8,128)S(1)} %bitcast.12), channel_id=1, source_target_pairs={{0,48},{8,56},{16,32},{24,40},{32,16},{40,24},{48,0},{56,8},{1,49}... | collective-permute-start | bytes 196616 | tf_op jit(solution)/shard_map/ppermute | solution.py:743
  65.4 0.0 collective-permute-start.16
  65.4 0.7 collective-permute-start.15
  66.1 1.5 %collective-permute-done.17 = f32[1,16,8,128]{3,2,1,0:T(8,128)S(1)} collective-permute-done((f32[1,16,8,128]{3,2,1,0:T(8,128)S(1)}, f32[1,16,8,128]{3,2,1,0:T(8,128)S(1)}, u32[]{:S(2)}, u32[]{:S(2)}) %collective-permute-start.17) | collective-permute-done | bytes 65568 | tf_op jit(solution)/shard_map/ppermute | solution.py:743
  67.5 2.9 %collective-permute-done.16 = f32[1,16,8,128]{3,2,1,0:T(8,128)S(1)} collective-permute-done((f32[1,16,8,128]{3,2,1,0:T(8,128)S(1)}, f32[1,16,8,128]{3,2,1,0:T(8,128)S(1)}, u32[]{:S(2)}, u32[]{:S(2)}) %collective-permute-start.16) | collective-permute-done | bytes 65568 | tf_op jit(solution)/shard_map/ppermute | solution.py:743
  70.4 0.0 collective-permute-done.15
  70.5 2.2 %all-gather = f32[8,16,8,128]{3,2,1,0:T(8,128)S(1)} all-gather(f32[4,16,8,128]{3,2,1,0:T(8,128)S(1)} %pad_maximum_fusion), channel_id=2, replica_groups={{0,8},{16,24},{32,40},{48,56},{1,9},{17,25},{33,41},{49,57},{2,10},{18,..., dimensions={0}, use_global_device_ids=true | all-gather | bytes 786432 | tf_op jit(solution)/shard_map/all_gather | solution.py:748
  72.7 2.4 %shard_map.34 = (f32[8,8,128]{2,1,0:T(8,128)S(1)}, f32[16,2,8,128]{3,2,1,0:T(8,128)S(1)}, f32[6,16,2,8,128]{4,3,2,1,0:T(8,128)S(1)}, f32[6,16,2,8,128]{4,3,2,1,0...) custom-call(s32[3]{0:T(128)S(1)} %pad_add_fusion.scal, f32[2,4,16,8,128]{4,3,2,1,0:T(8,128)S(1)} %bitcast.10), custom_call_target="tpu_custom_call" | custom-call | tf_op jit(solution)/shard_map/pallas_call | solution.py:727
  75.0 4.0 %collective-permute-start.21 = (f32[8,8,128]{2,1,0:T(8,128)S(1)}, f32[8,8,128]{2,1,0:T(8,128)S(1)}, u32[]{:S(2)}, u32[]{:S(2)}) collective-permute-start(f32[8,8,128]{2,1,0:T(8,128)S(1)} %get-tuple-element.45.own_ref), channel_id=1, source_target_pairs={{0,4},{1,5},{2,6},{3,7},{4,0},{5,1},{6,2},{7,3},{8,12},{9,13},{10,... | collective-permute-start | bytes 98312 | tf_op jit(solution)/shard_map/ppermute | solution.py:757
  79.0 0.6 collective-permute-start.20
  79.7 3.6 %collective-permute-start.19 = (f32[8,8,128]{2,1,0:T(8,128)S(1)}, f32[8,8,128]{2,1,0:T(8,128)S(1)}, u32[]{:S(2)}, u32[]{:S(2)}) collective-permute-start(f32[8,8,128]{2,1,0:T(8,128)S(1)} %get-tuple-element.45.own_ref), channel_id=1, source_target_pairs={{0,2},{1,3},{2,4},{3,5},{4,6},{5,7},{6,0},{7,1},{8,14},{9,15},{10,... | collective-permute-start | bytes 98312 | tf_op jit(solution)/shard_map/ppermute | solution.py:757
  83.3 0.0 collective-permute-start.18
  83.3 0.0 collective-permute-done.21
  83.3 0.3 collective-permute-done.20
  83.6 2.2 %collective-permute-done.19 = f32[8,8,128]{2,1,0:T(8,128)S(1)} collective-permute-done((f32[8,8,128]{2,1,0:T(8,128)S(1)}, f32[8,8,128]{2,1,0:T(8,128)S(1)}, u32[]{:S(2)}, u32[]{:S(2)}) %collective-permute-start.19) | collective-permute-done | bytes 32800 | tf_op jit(solution)/shard_map/ppermute | solution.py:757
  85.9 0.5 collective-permute-done.18
  86.4 3.3 %all-gather.1 = f32[8,8,8,128]{3,2,1,0:T(8,128)S(1)} all-gather(f32[4,8,8,128]{3,2,1,0:T(8,128)S(1)} %pad_maximum_fusion.1), channel_id=3, replica_groups={{0,8},{16,24},{32,40},{48,56},{1,9},{17,25},{33,41},{49,57},{2,10},{18,..., dimensions={0}, use_global_device_ids=true | all-gather | bytes 393216 | tf_op jit(solution)/shard_map/all_gather | solution.py:748
  89.6 11.6 %shard_map.35 = f32[16,32,128]{2,1,0:T(8,128)} custom-call(s32[3]{0:T(128)S(1)} %pad_add_fusion.scal, f32[8,8,128]{2,1,0:T(8,128)S(1)} %get-tuple-element.45.own_ref, f32[2,4,8,8,128]{4,3,2,1,0:T(8,128)S(1)} %bitcast.11, f32[16,2,8,128]{3,2,1,0:T(8,128)S(1)} %get-tuple-element.46.refs_0_, f32[6,16,2,8,128]{4,3,2,1,0:T(8,128)S(1)} %get-tuple-element.47.refs_1_, ...), custom_call_target="tpu_custom_call" | custom-call | tf_op jit(solution)/shard_map/pallas_call | solution.py:727
  (6 shorter events, 0.0 us)
Async XLA Ops:
  0.0 0.9 copy-start
  1.0 0.9 copy-start.1
  2.9 9.3 %collective-permute-start.2 = (f32[2,2,16,128]{3,2,1,0:T(8,128)S(1)}, f32[2,2,16,128]{3,2,1,0:T(8,128)S(1)}, u32[]{:S(2)}, u32[]{:S(2)}) collective-permute-start(f32[2,2,16,128]{3,2,1,0:T(8,128)S(1)} %get-tuple-element.35), channel_id=1, source_target_pairs={{0,1},{1,2},{2,3},{3,4},{4,5},{5,6},{6,7},{7,0},{8,9},{9,10},{10,1... | collective-permute-start | bytes 98312 | tf_op jit(solution)/shard_map/ppermute | solution.py:739
  5.5 6.7 %collective-permute-start.3 = (f32[2,2,16,128]{3,2,1,0:T(8,128)S(1)}, f32[2,2,16,128]{3,2,1,0:T(8,128)S(1)}, u32[]{:S(2)}, u32[]{:S(2)}) collective-permute-start(f32[2,2,16,128]{3,2,1,0:T(8,128)S(1)} %get-tuple-element.36), channel_id=1, source_target_pairs={{0,7},{1,0},{2,1},{3,2},{4,3},{5,4},{6,5},{7,6},{8,15},{9,8},{10,9... | collective-permute-start | bytes 98312 | tf_op jit(solution)/shard_map/ppermute | solution.py:739
  9.5 8.8 %collective-permute-start = (f32[16,2,16,128]{3,2,1,0:T(8,128)S(1)}, f32[16,2,16,128]{3,2,1,0:T(8,128)S(1)}, u32[]{:S(2)}, u32[]{:S(2)}) collective-permute-start(f32[16,2,16,128]{3,2,1,0:T(8,128)S(1)} %get-tuple-element.33.refs_2_.m2), channel_id=1, source_target_pairs={{0,64},{64,128},{128,192},{192,0},{1,65},{65,129},{129,193},{193,1... | collective-permute-start | bytes 786440 | tf_op jit(solution)/shard_map/ppermute | solution.py:739
  10.7 7.6 %collective-permute-start.1 = (f32[16,2,16,128]{3,2,1,0:T(8,128)S(1)}, f32[16,2,16,128]{3,2,1,0:T(8,128)S(1)}, u32[]{:S(2)}, u32[]{:S(2)}) collective-permute-start(f32[16,2,16,128]{3,2,1,0:T(8,128)S(1)} %get-tuple-element.34.refs_1_.m1), channel_id=1, source_target_pairs={{0,192},{64,0},{128,64},{192,128},{1,193},{65,1},{129,65},{193,129... | collective-permute-start | bytes 786440 | tf_op jit(solution)/shard_map/ppermute | solution.py:739
  12.2 6.1 %collective-permute-start.4 = (f32[2,2,16,128]{3,2,1,0:T(8,128)S(1)}, f32[2,2,16,128]{3,2,1,0:T(8,128)S(1)}, u32[]{:S(2)}, u32[]{:S(2)}) collective-permute-start(f32[2,2,16,128]{3,2,1,0:T(8,128)S(1)} %pad_maximum_fusion.2.refs_6_.s2), channel_id=1, source_target_pairs={{0,64},{64,128},{128,192},{192,0},{1,65},{65,129},{129,193},{193,1... | collective-permute-start | bytes 98312 | tf_op jit(solution)/shard_map/ppermute | solution.py:739
  12.3 6.0 %collective-permute-start.5 = (f32[2,2,16,128]{3,2,1,0:T(8,128)S(1)}, f32[2,2,16,128]{3,2,1,0:T(8,128)S(1)}, u32[]{:S(2)}, u32[]{:S(2)}) collective-permute-start(f32[2,2,16,128]{3,2,1,0:T(8,128)S(1)} %pad_maximum_fusion.3.refs_5_.s1), channel_id=1, source_target_pairs={{0,192},{64,0},{128,64},{192,128},{1,193},{65,1},{129,65},{193,129... | collective-permute-start | bytes 98312 | tf_op jit(solution)/shard_map/ppermute | solution.py:739
  18.4 6.7 %collective-permute-start.6 = (f32[72,8,128]{2,1,0:T(8,128)S(1)}, f32[72,8,128]{2,1,0:T(8,128)S(1)}, u32[]{:S(2)}, u32[]{:S(2)}) collective-permute-start(f32[72,8,128]{2,1,0:T(8,128)S(1)} %get-tuple-element.37), channel_id=1, source_target_pairs={{0,8},{8,16},{16,24},{24,32},{32,40},{40,48},{48,56},{56,0},{1,9},... | collective-permute-start | bytes 884744 | tf_op jit(solution)/shard_map/ppermute | solution.py:739
  21.4 6.1 %collective-permute-start.7 = (f32[72,8,128]{2,1,0:T(8,128)S(1)}, f32[72,8,128]{2,1,0:T(8,128)S(1)}, u32[]{:S(2)}, u32[]{:S(2)}) collective-permute-start(f32[72,8,128]{2,1,0:T(8,128)S(1)} %get-tuple-element.38), channel_id=1, source_target_pairs={{0,56},{8,0},{16,8},{24,16},{32,24},{40,32},{48,40},{56,48},{1,57}... | collective-permute-start | bytes 884744 | tf_op jit(solution)/shard_map/ppermute | solution.py:739
  34.3 4.1 %collective-permute-start.8 = (f32[4,2,8,128]{3,2,1,0:T(8,128)S(1)}, f32[4,2,8,128]{3,2,1,0:T(8,128)S(1)}, u32[]{:S(2)}, u32[]{:S(2)}) collective-permute-start(f32[4,2,8,128]{3,2,1,0:T(8,128)S(1)} %get-tuple-element.40), channel_id=1, source_target_pairs={{0,1},{1,2},{2,3},{3,4},{4,5},{5,6},{6,7},{7,0},{8,9},{9,10},{10,1... | collective-permute-start | bytes 98312 | tf_op jit(solution)/shard_map/ppermute | solution.py:739
  34.4 4.0 %collective-permute-start.9 = (f32[4,2,8,128]{3,2,1,0:T(8,128)S(1)}, f32[4,2,8,128]{3,2,1,0:T(8,128)S(1)}, u32[]{:S(2)}, u32[]{:S(2)}) collective-permute-start(f32[4,2,8,128]{3,2,1,0:T(8,128)S(1)} %get-tuple-element.41), channel_id=1, source_target_pairs={{0,7},{1,0},{2,1},{3,2},{4,3},{5,4},{6,5},{7,6},{8,15},{9,8},{10,9... | collective-permute-start | bytes 98312 | tf_op jit(solution)/shard_map/ppermute | solution.py:739
  38.6 8.2 %collective-permute-start.12 = (f32[16,2,8,128]{3,2,1,0:T(8,128)S(1)}, f32[16,2,8,128]{3,2,1,0:T(8,128)S(1)}, u32[]{:S(2)}, u32[]{:S(2)}) collective-permute-start(f32[16,2,8,128]{3,2,1,0:T(8,128)S(1)} %shard_map.31.a_ref), channel_id=1, source_target_pairs={{0,192},{64,128},{128,64},{192,0},{1,193},{65,129},{129,65},{193,1... | collective-permute-start | bytes 393224 | tf_op jit(solution)/shard_map/ppermute | solution.py:743
  41.3 5.4 %collective-permute-start.11 = (f32[16,2,8,128]{3,2,1,0:T(8,128)S(1)}, f32[16,2,8,128]{3,2,1,0:T(8,128)S(1)}, u32[]{:S(2)}, u32[]{:S(2)}) collective-permute-start(f32[16,2,8,128]{3,2,1,0:T(8,128)S(1)} %shard_map.31.a_ref), channel_id=1, source_target_pairs={{0,128},{64,192},{128,0},{192,64},{1,129},{65,193},{129,1},{193,65... | collective-permute-start | bytes 393224 | tf_op jit(solution)/shard_map/ppermute | solution.py:743
  41.6 5.1 %collective-permute-start.10 = (f32[16,2,8,128]{3,2,1,0:T(8,128)S(1)}, f32[16,2,8,128]{3,2,1,0:T(8,128)S(1)}, u32[]{:S(2)}, u32[]{:S(2)}) collective-permute-start(f32[16,2,8,128]{3,2,1,0:T(8,128)S(1)} %shard_map.31.a_ref), channel_id=1, source_target_pairs={{0,64},{64,0},{128,192},{192,128},{1,65},{65,1},{129,193},{193,129... | collective-permute-start | bytes 393224 | tf_op jit(solution)/shard_map/ppermute | solution.py:743
  46.9 7.9 %collective-permute-start.13 = (f32[80,8,128]{2,1,0:T(8,128)S(1)}, f32[80,8,128]{2,1,0:T(8,128)S(1)}, u32[]{:S(2)}, u32[]{:S(2)}) collective-permute-start(f32[80,8,128]{2,1,0:T(8,128)S(1)} %get-tuple-element.42), channel_id=1, source_target_pairs={{0,8},{8,16},{16,24},{24,32},{32,40},{40,48},{48,56},{56,0},{1,9},... | collective-permute-start | bytes 983048 | tf_op jit(solution)/shard_map/ppermute | solution.py:739
  50.7 6.8 %collective-permute-start.14 = (f32[80,8,128]{2,1,0:T(8,128)S(1)}, f32[80,8,128]{2,1,0:T(8,128)S(1)}, u32[]{:S(2)}, u32[]{:S(2)}) collective-permute-start(f32[80,8,128]{2,1,0:T(8,128)S(1)} %get-tuple-element.43), channel_id=1, source_target_pairs={{0,56},{8,0},{16,8},{24,16},{32,24},{40,32},{48,40},{56,48},{1,57}... | collective-permute-start | bytes 983048 | tf_op jit(solution)/shard_map/ppermute | solution.py:739
  62.1 5.5 %collective-permute-start.17 = (f32[1,16,8,128]{3,2,1,0:T(8,128)S(1)}, f32[1,16,8,128]{3,2,1,0:T(8,128)S(1)}, u32[]{:S(2)}, u32[]{:S(2)}) collective-permute-start(f32[1,16,8,128]{3,2,1,0:T(8,128)S(1)} %bitcast.12), channel_id=1, source_target_pairs={{0,48},{8,56},{16,32},{24,40},{32,16},{40,24},{48,0},{56,8},{1,49}... | collective-permute-start | bytes 196616 | tf_op jit(solution)/shard_map/ppermute | solution.py:743
  65.4 5.0 %collective-permute-start.16 = (f32[1,16,8,128]{3,2,1,0:T(8,128)S(1)}, f32[1,16,8,128]{3,2,1,0:T(8,128)S(1)}, u32[]{:S(2)}, u32[]{:S(2)}) collective-permute-start(f32[1,16,8,128]{3,2,1,0:T(8,128)S(1)} %bitcast.13), channel_id=1, source_target_pairs={{0,32},{8,40},{16,48},{24,56},{32,0},{40,8},{48,16},{56,24},{1,33}... | collective-permute-start | bytes 196616 | tf_op jit(solution)/shard_map/ppermute | solution.py:743
  65.4 5.0 %collective-permute-start.15 = (f32[1,16,8,128]{3,2,1,0:T(8,128)S(1)}, f32[1,16,8,128]{3,2,1,0:T(8,128)S(1)}, u32[]{:S(2)}, u32[]{:S(2)}) collective-permute-start(f32[1,16,8,128]{3,2,1,0:T(8,128)S(1)} %bitcast.14), channel_id=1, source_target_pairs={{0,16},{8,24},{16,0},{24,8},{32,48},{40,56},{48,32},{56,40},{1,17}... | collective-permute-start | bytes 196616 | tf_op jit(solution)/shard_map/ppermute | solution.py:743
  75.0 8.3 %collective-permute-start.21 = (f32[8,8,128]{2,1,0:T(8,128)S(1)}, f32[8,8,128]{2,1,0:T(8,128)S(1)}, u32[]{:S(2)}, u32[]{:S(2)}) collective-permute-start(f32[8,8,128]{2,1,0:T(8,128)S(1)} %get-tuple-element.45.own_ref), channel_id=1, source_target_pairs={{0,4},{1,5},{2,6},{3,7},{4,0},{5,1},{6,2},{7,3},{8,12},{9,13},{10,... | collective-permute-start | bytes 98312 | tf_op jit(solution)/shard_map/ppermute | solution.py:757
  79.0 4.6 %collective-permute-start.20 = (f32[8,8,128]{2,1,0:T(8,128)S(1)}, f32[8,8,128]{2,1,0:T(8,128)S(1)}, u32[]{:S(2)}, u32[]{:S(2)}) collective-permute-start(f32[8,8,128]{2,1,0:T(8,128)S(1)} %get-tuple-element.45.own_ref), channel_id=1, source_target_pairs={{0,3},{1,4},{2,5},{3,6},{4,7},{5,0},{6,1},{7,2},{8,13},{9,14},{10,... | collective-permute-start | bytes 98312 | tf_op jit(solution)/shard_map/ppermute | solution.py:757
  79.7 6.2 %collective-permute-start.19 = (f32[8,8,128]{2,1,0:T(8,128)S(1)}, f32[8,8,128]{2,1,0:T(8,128)S(1)}, u32[]{:S(2)}, u32[]{:S(2)}) collective-permute-start(f32[8,8,128]{2,1,0:T(8,128)S(1)} %get-tuple-element.45.own_ref), channel_id=1, source_target_pairs={{0,2},{1,3},{2,4},{3,5},{4,6},{5,7},{6,0},{7,1},{8,14},{9,15},{10,... | collective-permute-start | bytes 98312 | tf_op jit(solution)/shard_map/ppermute | solution.py:757
  83.3 3.1 %collective-permute-start.18 = (f32[8,8,128]{2,1,0:T(8,128)S(1)}, f32[8,8,128]{2,1,0:T(8,128)S(1)}, u32[]{:S(2)}, u32[]{:S(2)}) collective-permute-start(f32[8,8,128]{2,1,0:T(8,128)S(1)} %get-tuple-element.45.own_ref), channel_id=1, source_target_pairs={{0,1},{1,2},{2,3},{3,4},{4,5},{5,6},{6,7},{7,0},{8,15},{9,8},{10,9... | collective-permute-start | bytes 98312 | tf_op jit(solution)/shard_map/ppermute | solution.py:757

commit v5 on v4

--- a/solution.py
+++ b/solution.py
@@ -164,7 +164,7 @@
             if colour == 0:
                 dd[x, q] = total
 
-    planes(0, level.count, 4 if level.rows == 8 else 1, body, *rec)
+    planes(0, level.count, 4 if level.rows == 8 else 2, body, *rec)
 
 
 def relaxed(level, colour, x, at, q, window, wd, fd):
@@ -181,7 +181,7 @@
     def body(x, at, q, windows):
         v[colour][x + 1, q] = relaxed(level, colour, x, at, q, windows[0], wd, fd)
 
-    planes(first, level.count if last is None else last, 8 if level.rows == 8 else 4, body, v[1 - colour])
+    planes(first, level.count if last is None else last, 8 if level.rows == 8 else 7, body, v[1 - colour])
     if level.fold == "x":
         fill_ends(level, v[colour])
 

time: 101 us -> 99.8 us (0.988)
  Pallas kernels: 26.7 us -> 25.2 us
    pallas_call x8, Pallas kernels: 26.7 us -> 25.2 us  [call(): pl.pallas_call(kernel, out_shape=outs, in_specs=specs, out_specs=jax.tree...]
where the time goes in v5:
time: 99.8 us; the launch traced here: 99.6 us
  starting transfers between devices  37.2 us (37%)
  waiting for transfers between devices  29.6 us (30%)
  Pallas kernels  25.2 us (25%)
  blocking collectives  5.45 us (5%)
  local copies, waits for them, and re-layouts  1.91 us (2%)
    pallas_call x8, Pallas kernels, call(): pl.pallas_call(kernel, out_shape=outs, in_specs=specs, out_specs=jax.tree...  25.2 us
    ppermute x12, starting transfers between devices, ring(): lax.ppermute(values, axis, [(i, (i + step) % count) for i in range(count)])  21.6 us
    ppermute x12, waiting for transfers between devices, ring(): lax.ppermute(values, axis, [(i, (i + step) % count) for i in range(count)])  17.5 us
    ppermute x6, waiting for transfers between devices, trade(): lax.ppermute(values, axis, [(i, i ^ step) for i in range(lax.axis_size(ax...  9.12 us
    ppermute x4, starting transfers between devices, along_z(): return lax.ppermute(values, ('gy', 'gz'), pairs)  8.25 us
    ppermute x6, starting transfers between devices, trade(): lax.ppermute(values, axis, [(i, i ^ step) for i in range(lax.axis_size(ax...  7.26 us
    all_gather x2, blocking collectives, both_cores(): lax.all_gather(values, 'gy', axis=0, axis_index_groups=[[i, i + 1] for i...  5.45 us
    ppermute x4, waiting for transfers between devices, along_z(): return lax.ppermute(values, ('gy', 'gz'), pairs)  3.06 us
  transfers between devices with their start and end apart: 22, of which 12 were waited for; matrix products, arithmetic and copies ran while one was open for 0% of the time, Pallas kernels for 0%

profile of v5, /device:TPU:1, one launch (start us, length us, event | category | flops | bytes accessed | tf_op | source)
XLA Modules:
  0.0 99.6 jit_solution(3531609968442364488)
XLA Ops:
  0.0 0.0 copy-start
  0.0 0.9 copy-done
  1.0 0.0 copy-start.1
  1.0 0.9 copy-done.1
  1.9 1.0 %shard_map.28 = (f32[16,2,16,128]{3,2,1,0:T(8,128)S(1)}, f32[16,2,16,128]{3,2,1,0:T(8,128)S(1)}, f32[2,2,16,128]{3,2,1,0:T(8,128)S(1)}, f32[2,2,16,128]{3,2,1,0:T(8,128)S(1)}) custom-call(f32[16,32,128]{2,1,0:T(8,128)S(1)} %copy-done, f32[16,32,128]{2,1,0:T(8,128)S(1)} %copy-done.1), custom_call_target="tpu_custom_call" | custom-call | tf_op jit(solution)/shard_map/pallas_call | solution.py:727
  2.9 2.5 %collective-permute-start.2 = (f32[2,2,16,128]{3,2,1,0:T(8,128)S(1)}, f32[2,2,16,128]{3,2,1,0:T(8,128)S(1)}, u32[]{:S(2)}, u32[]{:S(2)}) collective-permute-start(f32[2,2,16,128]{3,2,1,0:T(8,128)S(1)} %get-tuple-element.35), channel_id=1, source_target_pairs={{0,1},{1,2},{2,3},{3,4},{4,5},{5,6},{6,7},{7,0},{8,9},{9,10},{10,1... | collective-permute-start | bytes 98312 | tf_op jit(solution)/shard_map/ppermute | solution.py:739
  5.5 4.0 %collective-permute-start.3 = (f32[2,2,16,128]{3,2,1,0:T(8,128)S(1)}, f32[2,2,16,128]{3,2,1,0:T(8,128)S(1)}, u32[]{:S(2)}, u32[]{:S(2)}) collective-permute-start(f32[2,2,16,128]{3,2,1,0:T(8,128)S(1)} %get-tuple-element.36), channel_id=1, source_target_pairs={{0,7},{1,0},{2,1},{3,2},{4,3},{5,4},{6,5},{7,6},{8,15},{9,8},{10,9... | collective-permute-start | bytes 98312 | tf_op jit(solution)/shard_map/ppermute | solution.py:739
  9.5 1.2 %collective-permute-start = (f32[16,2,16,128]{3,2,1,0:T(8,128)S(1)}, f32[16,2,16,128]{3,2,1,0:T(8,128)S(1)}, u32[]{:S(2)}, u32[]{:S(2)}) collective-permute-start(f32[16,2,16,128]{3,2,1,0:T(8,128)S(1)} %get-tuple-element.33.refs_2_.m2), channel_id=1, source_target_pairs={{0,64},{64,128},{128,192},{192,0},{1,65},{65,129},{129,193},{193,1... | collective-permute-start | bytes 786440 | tf_op jit(solution)/shard_map/ppermute | solution.py:739
  10.7 1.5 %collective-permute-start.1 = (f32[16,2,16,128]{3,2,1,0:T(8,128)S(1)}, f32[16,2,16,128]{3,2,1,0:T(8,128)S(1)}, u32[]{:S(2)}, u32[]{:S(2)}) collective-permute-start(f32[16,2,16,128]{3,2,1,0:T(8,128)S(1)} %get-tuple-element.34.refs_1_.m1), channel_id=1, source_target_pairs={{0,192},{64,0},{128,64},{192,128},{1,193},{65,1},{129,65},{193,129... | collective-permute-start | bytes 786440 | tf_op jit(solution)/shard_map/ppermute | solution.py:739
  12.2 0.0 collective-permute-done.2
  12.2 0.0 collective-permute-done.3
  12.2 0.1 collective-permute-start.4
  12.3 2.7 %collective-permute-start.5 = (f32[2,2,16,128]{3,2,1,0:T(8,128)S(1)}, f32[2,2,16,128]{3,2,1,0:T(8,128)S(1)}, u32[]{:S(2)}, u32[]{:S(2)}) collective-permute-start(f32[2,2,16,128]{3,2,1,0:T(8,128)S(1)} %pad_maximum_fusion.3.refs_5_.s1), channel_id=1, source_target_pairs={{0,192},{64,0},{128,64},{192,128},{1,193},{65,1},{129,65},{193,129... | collective-permute-start | bytes 98312 | tf_op jit(solution)/shard_map/ppermute | solution.py:739
  15.0 3.3 %collective-permute-done.4.refs_4_.s0 = f32[2,2,16,128]{3,2,1,0:T(8,128)S(1)} collective-permute-done((f32[2,2,16,128]{3,2,1,0:T(8,128)S(1)}, f32[2,2,16,128]{3,2,1,0:T(8,128)S(1)}, u32[]{:S(2)}, u32[]{:S(2)}) %collective-permute-start.4) | collective-permute-done | bytes 32800 | tf_op jit(solution)/shard_map/ppermute | solution.py:739
  18.3 0.0 collective-permute-done.5.refs_7_.s3
  18.3 0.0 collective-permute-done.refs_0_.m0
  18.3 0.0 collective-permute-done.1.refs_3_.m3
  18.3 0.1 shard_map.29
  18.4 3.1 %collective-permute-start.6 = (f32[72,8,128]{2,1,0:T(8,128)S(1)}, f32[72,8,128]{2,1,0:T(8,128)S(1)}, u32[]{:S(2)}, u32[]{:S(2)}) collective-permute-start(f32[72,8,128]{2,1,0:T(8,128)S(1)} %get-tuple-element.37), channel_id=1, source_target_pairs={{0,8},{8,16},{16,24},{24,32},{32,40},{40,48},{48,56},{56,0},{1,9},... | collective-permute-start | bytes 884744 | tf_op jit(solution)/shard_map/ppermute | solution.py:739
  21.4 0.0 collective-permute-start.7
  21.4 0.1 pad_add_fusion.scal
  21.5 3.6 %collective-permute-done.6.yl_ref = f32[72,8,128]{2,1,0:T(8,128)S(1)} collective-permute-done((f32[72,8,128]{2,1,0:T(8,128)S(1)}, f32[72,8,128]{2,1,0:T(8,128)S(1)}, u32[]{:S(2)}, u32[]{:S(2)}) %collective-permute-start.6) | collective-permute-done | bytes 294944 | tf_op jit(solution)/shard_map/ppermute | solution.py:739
  25.1 2.5 %collective-permute-done.7.yr_ref = f32[72,8,128]{2,1,0:T(8,128)S(1)} collective-permute-done((f32[72,8,128]{2,1,0:T(8,128)S(1)}, f32[72,8,128]{2,1,0:T(8,128)S(1)}, u32[]{:S(2)}, u32[]{:S(2)}) %collective-permute-start.7) | collective-permute-done | bytes 294944 | tf_op jit(solution)/shard_map/ppermute | solution.py:739
  27.6 5.8 %shard_map.30 = (f32[16,2,8,128]{3,2,1,0:T(8,128)S(1)}, f32[4,2,8,128]{3,2,1,0:T(8,128)S(1)}, f32[4,2,8,128]{3,2,1,0:T(8,128)S(1)}, f32[32,2,24,128]{3,2,1,0:T(8...) custom-call(s32[3]{0:T(128)S(1)} %pad_add_fusion.scal, ...), custom_call_target="tpu_custom_call" | custom-call | tf_op jit(solution)/shard_map/pallas_call | solution.py:727
  33.4 0.1 collective-permute-start.8
  33.5 2.7 %collective-permute-start.9 = (f32[4,2,8,128]{3,2,1,0:T(8,128)S(1)}, f32[4,2,8,128]{3,2,1,0:T(8,128)S(1)}, u32[]{:S(2)}, u32[]{:S(2)}) collective-permute-start(f32[4,2,8,128]{3,2,1,0:T(8,128)S(1)} %get-tuple-element.41), channel_id=1, source_target_pairs={{0,7},{1,0},{2,1},{3,2},{4,3},{5,4},{6,5},{7,6},{8,15},{9,8},{10,9... | collective-permute-start | bytes 98312 | tf_op jit(solution)/shard_map/ppermute | solution.py:739
  36.1 1.3 %collective-permute-done.8.left_ref = f32[4,2,8,128]{3,2,1,0:T(8,128)S(1)} collective-permute-done((f32[4,2,8,128]{3,2,1,0:T(8,128)S(1)}, f32[4,2,8,128]{3,2,1,0:T(8,128)S(1)}, u32[]{:S(2)}, u32[]{:S(2)}) %collective-permute-start.8) | collective-permute-done | bytes 32800 | tf_op jit(solution)/shard_map/ppermute | solution.py:739
  37.4 0.0 collective-permute-done.9.right_ref
  37.4 0.2 shard_map.31.a_ref
  37.7 2.8 %collective-permute-start.12 = (f32[16,2,8,128]{3,2,1,0:T(8,128)S(1)}, f32[16,2,8,128]{3,2,1,0:T(8,128)S(1)}, u32[]{:S(2)}, u32[]{:S(2)}) collective-permute-start(f32[16,2,8,128]{3,2,1,0:T(8,128)S(1)} %shard_map.31.a_ref), channel_id=1, source_target_pairs={{0,192},{64,128},{128,64},{192,0},{1,193},{65,129},{129,65},{193,1... | collective-permute-start | bytes 393224 | tf_op jit(solution)/shard_map/ppermute | solution.py:743
  40.4 0.3 collective-permute-start.11
  40.7 0.4 collective-permute-start.10
  41.1 4.7 %collective-permute-done.12.d_ref = f32[16,2,8,128]{3,2,1,0:T(8,128)S(1)} collective-permute-done((f32[16,2,8,128]{3,2,1,0:T(8,128)S(1)}, f32[16,2,8,128]{3,2,1,0:T(8,128)S(1)}, u32[]{:S(2)}, u32[]{:S(2)}) %collective-permute-start.12) | collective-permute-done | bytes 131104 | tf_op jit(solution)/shard_map/ppermute | solution.py:743
  45.8 0.0 collective-permute-done.11.c_ref
  45.8 0.0 collective-permute-done.10.b_ref
  45.8 0.1 shard_map.32
  46.0 3.8 %collective-permute-start.13 = (f32[80,8,128]{2,1,0:T(8,128)S(1)}, f32[80,8,128]{2,1,0:T(8,128)S(1)}, u32[]{:S(2)}, u32[]{:S(2)}) collective-permute-start(f32[80,8,128]{2,1,0:T(8,128)S(1)} %get-tuple-element.42), channel_id=1, source_target_pairs={{0,8},{8,16},{16,24},{24,32},{32,40},{40,48},{48,56},{56,0},{1,9},... | collective-permute-start | bytes 983048 | tf_op jit(solution)/shard_map/ppermute | solution.py:739
  49.8 0.0 collective-permute-start.14
  49.8 4.0 %collective-permute-done.13.yl_ref = f32[80,8,128]{2,1,0:T(8,128)S(1)} collective-permute-done((f32[80,8,128]{2,1,0:T(8,128)S(1)}, f32[80,8,128]{2,1,0:T(8,128)S(1)}, u32[]{:S(2)}, u32[]{:S(2)}) %collective-permute-start.13) | collective-permute-done | bytes 327712 | tf_op jit(solution)/shard_map/ppermute | solution.py:739
  53.8 2.8 %collective-permute-done.14.yr_ref = f32[80,8,128]{2,1,0:T(8,128)S(1)} collective-permute-done((f32[80,8,128]{2,1,0:T(8,128)S(1)}, f32[80,8,128]{2,1,0:T(8,128)S(1)}, u32[]{:S(2)}, u32[]{:S(2)}) %collective-permute-start.14) | collective-permute-done | bytes 327712 | tf_op jit(solution)/shard_map/ppermute | solution.py:739
  56.6 4.3 %shard_map.33 = (f32[16,8,128]{2,1,0:T(8,128)S(1)}, f32[16,2,24,128]{3,2,1,0:T(8,128)S(1)}, f32[6,16,2,24,128]{4,3,2,1,0:T(8,128)S(1)}, f32[6,16,2,24,128]{4,3,2...) custom-call(s32[3]{0:T(128)S(1)} %pad_add_fusion.scal, ...), custom_call_target="tpu_custom_call" | custom-call | tf_op jit(solution)/shard_map/pallas_call | solution.py:727
  60.9 3.2 %collective-permute-start.17 = (f32[1,16,8,128]{3,2,1,0:T(8,128)S(1)}, f32[1,16,8,128]{3,2,1,0:T(8,128)S(1)}, u32[]{:S(2)}, u32[]{:S(2)}) collective-permute-start(f32[1,16,8,128]{3,2,1,0:T(8,128)S(1)} %bitcast.12), channel_id=1, source_target_pairs={{0,48},{8,56},{16,32},{24,40},{32,16},{40,24},{48,0},{56,8},{1,49}... | collective-permute-start | bytes 196616 | tf_op jit(solution)/shard_map/ppermute | solution.py:743
  64.1 0.0 collective-permute-start.16
  64.1 0.7 collective-permute-start.15
  64.7 1.5 %collective-permute-done.17 = f32[1,16,8,128]{3,2,1,0:T(8,128)S(1)} collective-permute-done((f32[1,16,8,128]{3,2,1,0:T(8,128)S(1)}, f32[1,16,8,128]{3,2,1,0:T(8,128)S(1)}, u32[]{:S(2)}, u32[]{:S(2)}) %collective-permute-start.17) | collective-permute-done | bytes 65568 | tf_op jit(solution)/shard_map/ppermute | solution.py:743
  66.2 2.9 %collective-permute-done.16 = f32[1,16,8,128]{3,2,1,0:T(8,128)S(1)} collective-permute-done((f32[1,16,8,128]{3,2,1,0:T(8,128)S(1)}, f32[1,16,8,128]{3,2,1,0:T(8,128)S(1)}, u32[]{:S(2)}, u32[]{:S(2)}) %collective-permute-start.16) | collective-permute-done | bytes 65568 | tf_op jit(solution)/shard_map/ppermute | solution.py:743
  69.1 0.0 collective-permute-done.15
  69.1 2.2 %all-gather = f32[8,16,8,128]{3,2,1,0:T(8,128)S(1)} all-gather(f32[4,16,8,128]{3,2,1,0:T(8,128)S(1)} %pad_maximum_fusion), channel_id=2, replica_groups={{0,8},{16,24},{32,40},{48,56},{1,9},{17,25},{33,41},{49,57},{2,10},{18,..., dimensions={0}, use_global_device_ids=true | all-gather | bytes 786432 | tf_op jit(solution)/shard_map/all_gather | solution.py:748
  71.3 2.4 %shard_map.34 = (f32[8,8,128]{2,1,0:T(8,128)S(1)}, f32[16,2,8,128]{3,2,1,0:T(8,128)S(1)}, f32[6,16,2,8,128]{4,3,2,1,0:T(8,128)S(1)}, f32[6,16,2,8,128]{4,3,2,1,0...) custom-call(s32[3]{0:T(128)S(1)} %pad_add_fusion.scal, f32[2,4,16,8,128]{4,3,2,1,0:T(8,128)S(1)} %bitcast.10), custom_call_target="tpu_custom_call" | custom-call | tf_op jit(solution)/shard_map/pallas_call | solution.py:727
  73.7 4.0 %collective-permute-start.21 = (f32[8,8,128]{2,1,0:T(8,128)S(1)}, f32[8,8,128]{2,1,0:T(8,128)S(1)}, u32[]{:S(2)}, u32[]{:S(2)}) collective-permute-start(f32[8,8,128]{2,1,0:T(8,128)S(1)} %get-tuple-element.45.own_ref), channel_id=1, source_target_pairs={{0,4},{1,5},{2,6},{3,7},{4,0},{5,1},{6,2},{7,3},{8,12},{9,13},{10,... | collective-permute-start | bytes 98312 | tf_op jit(solution)/shard_map/ppermute | solution.py:757
  77.7 0.6 collective-permute-start.20
  78.3 3.6 %collective-permute-start.19 = (f32[8,8,128]{2,1,0:T(8,128)S(1)}, f32[8,8,128]{2,1,0:T(8,128)S(1)}, u32[]{:S(2)}, u32[]{:S(2)}) collective-permute-start(f32[8,8,128]{2,1,0:T(8,128)S(1)} %get-tuple-element.45.own_ref), channel_id=1, source_target_pairs={{0,2},{1,3},{2,4},{3,5},{4,6},{5,7},{6,0},{7,1},{8,14},{9,15},{10,... | collective-permute-start | bytes 98312 | tf_op jit(solution)/shard_map/ppermute | solution.py:757
  81.9 0.0 collective-permute-start.18
  81.9 0.0 collective-permute-done.21
  82.0 0.3 collective-permute-done.20
  82.3 2.2 %collective-permute-done.19 = f32[8,8,128]{2,1,0:T(8,128)S(1)} collective-permute-done((f32[8,8,128]{2,1,0:T(8,128)S(1)}, f32[8,8,128]{2,1,0:T(8,128)S(1)}, u32[]{:S(2)}, u32[]{:S(2)}) %collective-permute-start.19) | collective-permute-done | bytes 32800 | tf_op jit(solution)/shard_map/ppermute | solution.py:757
  84.5 0.5 collective-permute-done.18
  85.0 3.3 %all-gather.1 = f32[8,8,8,128]{3,2,1,0:T(8,128)S(1)} all-gather(f32[4,8,8,128]{3,2,1,0:T(8,128)S(1)} %pad_maximum_fusion.1), channel_id=3, replica_groups={{0,8},{16,24},{32,40},{48,56},{1,9},{17,25},{33,41},{49,57},{2,10},{18,..., dimensions={0}, use_global_device_ids=true | all-gather | bytes 393216 | tf_op jit(solution)/shard_map/all_gather | solution.py:748
  88.3 11.3 %shard_map.35 = f32[16,32,128]{2,1,0:T(8,128)} custom-call(s32[3]{0:T(128)S(1)} %pad_add_fusion.scal, f32[8,8,128]{2,1,0:T(8,128)S(1)} %get-tuple-element.45.own_ref, f32[2,4,8,8,128]{4,3,2,1,0:T(8,128)S(1)} %bitcast.11, f32[16,2,8,128]{3,2,1,0:T(8,128)S(1)} %get-tuple-element.46.refs_0_, f32[6,16,2,8,128]{4,3,2,1,0:T(8,128)S(1)} %get-tuple-element.47.refs_1_, ...), custom_call_target="tpu_custom_call" | custom-call | tf_op jit(solution)/shard_map/pallas_call | solution.py:727
  (6 shorter events, 0.0 us)
Async XLA Ops:
  0.0 0.9 copy-start
  1.0 0.9 copy-start.1
  2.9 9.3 %collective-permute-start.2 = (f32[2,2,16,128]{3,2,1,0:T(8,128)S(1)}, f32[2,2,16,128]{3,2,1,0:T(8,128)S(1)}, u32[]{:S(2)}, u32[]{:S(2)}) collective-permute-start(f32[2,2,16,128]{3,2,1,0:T(8,128)S(1)} %get-tuple-element.35), channel_id=1, source_target_pairs={{0,1},{1,2},{2,3},{3,4},{4,5},{5,6},{6,7},{7,0},{8,9},{9,10},{10,1... | collective-permute-start | bytes 98312 | tf_op jit(solution)/shard_map/ppermute | solution.py:739
  5.5 6.7 %collective-permute-start.3 = (f32[2,2,16,128]{3,2,1,0:T(8,128)S(1)}, f32[2,2,16,128]{3,2,1,0:T(8,128)S(1)}, u32[]{:S(2)}, u32[]{:S(2)}) collective-permute-start(f32[2,2,16,128]{3,2,1,0:T(8,128)S(1)} %get-tuple-element.36), channel_id=1, source_target_pairs={{0,7},{1,0},{2,1},{3,2},{4,3},{5,4},{6,5},{7,6},{8,15},{9,8},{10,9... | collective-permute-start | bytes 98312 | tf_op jit(solution)/shard_map/ppermute | solution.py:739
  9.5 8.8 %collective-permute-start = (f32[16,2,16,128]{3,2,1,0:T(8,128)S(1)}, f32[16,2,16,128]{3,2,1,0:T(8,128)S(1)}, u32[]{:S(2)}, u32[]{:S(2)}) collective-permute-start(f32[16,2,16,128]{3,2,1,0:T(8,128)S(1)} %get-tuple-element.33.refs_2_.m2), channel_id=1, source_target_pairs={{0,64},{64,128},{128,192},{192,0},{1,65},{65,129},{129,193},{193,1... | collective-permute-start | bytes 786440 | tf_op jit(solution)/shard_map/ppermute | solution.py:739
  10.7 7.6 %collective-permute-start.1 = (f32[16,2,16,128]{3,2,1,0:T(8,128)S(1)}, f32[16,2,16,128]{3,2,1,0:T(8,128)S(1)}, u32[]{:S(2)}, u32[]{:S(2)}) collective-permute-start(f32[16,2,16,128]{3,2,1,0:T(8,128)S(1)} %get-tuple-element.34.refs_1_.m1), channel_id=1, source_target_pairs={{0,192},{64,0},{128,64},{192,128},{1,193},{65,1},{129,65},{193,129... | collective-permute-start | bytes 786440 | tf_op jit(solution)/shard_map/ppermute | solution.py:739
  12.2 6.1 %collective-permute-start.4 = (f32[2,2,16,128]{3,2,1,0:T(8,128)S(1)}, f32[2,2,16,128]{3,2,1,0:T(8,128)S(1)}, u32[]{:S(2)}, u32[]{:S(2)}) collective-permute-start(f32[2,2,16,128]{3,2,1,0:T(8,128)S(1)} %pad_maximum_fusion.2.refs_6_.s2), channel_id=1, source_target_pairs={{0,64},{64,128},{128,192},{192,0},{1,65},{65,129},{129,193},{193,1... | collective-permute-start | bytes 98312 | tf_op jit(solution)/shard_map/ppermute | solution.py:739
  12.3 6.0 %collective-permute-start.5 = (f32[2,2,16,128]{3,2,1,0:T(8,128)S(1)}, f32[2,2,16,128]{3,2,1,0:T(8,128)S(1)}, u32[]{:S(2)}, u32[]{:S(2)}) collective-permute-start(f32[2,2,16,128]{3,2,1,0:T(8,128)S(1)} %pad_maximum_fusion.3.refs_5_.s1), channel_id=1, source_target_pairs={{0,192},{64,0},{128,64},{192,128},{1,193},{65,1},{129,65},{193,129... | collective-permute-start | bytes 98312 | tf_op jit(solution)/shard_map/ppermute | solution.py:739
  18.4 6.7 %collective-permute-start.6 = (f32[72,8,128]{2,1,0:T(8,128)S(1)}, f32[72,8,128]{2,1,0:T(8,128)S(1)}, u32[]{:S(2)}, u32[]{:S(2)}) collective-permute-start(f32[72,8,128]{2,1,0:T(8,128)S(1)} %get-tuple-element.37), channel_id=1, source_target_pairs={{0,8},{8,16},{16,24},{24,32},{32,40},{40,48},{48,56},{56,0},{1,9},... | collective-permute-start | bytes 884744 | tf_op jit(solution)/shard_map/ppermute | solution.py:739
  21.4 6.1 %collective-permute-start.7 = (f32[72,8,128]{2,1,0:T(8,128)S(1)}, f32[72,8,128]{2,1,0:T(8,128)S(1)}, u32[]{:S(2)}, u32[]{:S(2)}) collective-permute-start(f32[72,8,128]{2,1,0:T(8,128)S(1)} %get-tuple-element.38), channel_id=1, source_target_pairs={{0,56},{8,0},{16,8},{24,16},{32,24},{40,32},{48,40},{56,48},{1,57}... | collective-permute-start | bytes 884744 | tf_op jit(solution)/shard_map/ppermute | solution.py:739
  33.4 4.1 %collective-permute-start.8 = (f32[4,2,8,128]{3,2,1,0:T(8,128)S(1)}, f32[4,2,8,128]{3,2,1,0:T(8,128)S(1)}, u32[]{:S(2)}, u32[]{:S(2)}) collective-permute-start(f32[4,2,8,128]{3,2,1,0:T(8,128)S(1)} %get-tuple-element.40), channel_id=1, source_target_pairs={{0,1},{1,2},{2,3},{3,4},{4,5},{5,6},{6,7},{7,0},{8,9},{9,10},{10,1... | collective-permute-start | bytes 98312 | tf_op jit(solution)/shard_map/ppermute | solution.py:739
  33.5 4.0 %collective-permute-start.9 = (f32[4,2,8,128]{3,2,1,0:T(8,128)S(1)}, f32[4,2,8,128]{3,2,1,0:T(8,128)S(1)}, u32[]{:S(2)}, u32[]{:S(2)}) collective-permute-start(f32[4,2,8,128]{3,2,1,0:T(8,128)S(1)} %get-tuple-element.41), channel_id=1, source_target_pairs={{0,7},{1,0},{2,1},{3,2},{4,3},{5,4},{6,5},{7,6},{8,15},{9,8},{10,9... | collective-permute-start | bytes 98312 | tf_op jit(solution)/shard_map/ppermute | solution.py:739
  37.7 8.2 %collective-permute-start.12 = (f32[16,2,8,128]{3,2,1,0:T(8,128)S(1)}, f32[16,2,8,128]{3,2,1,0:T(8,128)S(1)}, u32[]{:S(2)}, u32[]{:S(2)}) collective-permute-start(f32[16,2,8,128]{3,2,1,0:T(8,128)S(1)} %shard_map.31.a_ref), channel_id=1, source_target_pairs={{0,192},{64,128},{128,64},{192,0},{1,193},{65,129},{129,65},{193,1... | collective-permute-start | bytes 393224 | tf_op jit(solution)/shard_map/ppermute | solution.py:743
  40.4 5.4 %collective-permute-start.11 = (f32[16,2,8,128]{3,2,1,0:T(8,128)S(1)}, f32[16,2,8,128]{3,2,1,0:T(8,128)S(1)}, u32[]{:S(2)}, u32[]{:S(2)}) collective-permute-start(f32[16,2,8,128]{3,2,1,0:T(8,128)S(1)} %shard_map.31.a_ref), channel_id=1, source_target_pairs={{0,128},{64,192},{128,0},{192,64},{1,129},{65,193},{129,1},{193,65... | collective-permute-start | bytes 393224 | tf_op jit(solution)/shard_map/ppermute | solution.py:743
  40.7 5.1 %collective-permute-start.10 = (f32[16,2,8,128]{3,2,1,0:T(8,128)S(1)}, f32[16,2,8,128]{3,2,1,0:T(8,128)S(1)}, u32[]{:S(2)}, u32[]{:S(2)}) collective-permute-start(f32[16,2,8,128]{3,2,1,0:T(8,128)S(1)} %shard_map.31.a_ref), channel_id=1, source_target_pairs={{0,64},{64,0},{128,192},{192,128},{1,65},{65,1},{129,193},{193,129... | collective-permute-start | bytes 393224 | tf_op jit(solution)/shard_map/ppermute | solution.py:743
  46.0 7.9 %collective-permute-start.13 = (f32[80,8,128]{2,1,0:T(8,128)S(1)}, f32[80,8,128]{2,1,0:T(8,128)S(1)}, u32[]{:S(2)}, u32[]{:S(2)}) collective-permute-start(f32[80,8,128]{2,1,0:T(8,128)S(1)} %get-tuple-element.42), channel_id=1, source_target_pairs={{0,8},{8,16},{16,24},{24,32},{32,40},{40,48},{48,56},{56,0},{1,9},... | collective-permute-start | bytes 983048 | tf_op jit(solution)/shard_map/ppermute | solution.py:739
  49.8 6.8 %collective-permute-start.14 = (f32[80,8,128]{2,1,0:T(8,128)S(1)}, f32[80,8,128]{2,1,0:T(8,128)S(1)}, u32[]{:S(2)}, u32[]{:S(2)}) collective-permute-start(f32[80,8,128]{2,1,0:T(8,128)S(1)} %get-tuple-element.43), channel_id=1, source_target_pairs={{0,56},{8,0},{16,8},{24,16},{32,24},{40,32},{48,40},{56,48},{1,57}... | collective-permute-start | bytes 983048 | tf_op jit(solution)/shard_map/ppermute | solution.py:739
  60.9 5.3 %collective-permute-start.17 = (f32[1,16,8,128]{3,2,1,0:T(8,128)S(1)}, f32[1,16,8,128]{3,2,1,0:T(8,128)S(1)}, u32[]{:S(2)}, u32[]{:S(2)}) collective-permute-start(f32[1,16,8,128]{3,2,1,0:T(8,128)S(1)} %bitcast.12), channel_id=1, source_target_pairs={{0,48},{8,56},{16,32},{24,40},{32,16},{40,24},{48,0},{56,8},{1,49}... | collective-permute-start | bytes 196616 | tf_op jit(solution)/shard_map/ppermute | solution.py:743
  64.1 5.0 %collective-permute-start.16 = (f32[1,16,8,128]{3,2,1,0:T(8,128)S(1)}, f32[1,16,8,128]{3,2,1,0:T(8,128)S(1)}, u32[]{:S(2)}, u32[]{:S(2)}) collective-permute-start(f32[1,16,8,128]{3,2,1,0:T(8,128)S(1)} %bitcast.13), channel_id=1, source_target_pairs={{0,32},{8,40},{16,48},{24,56},{32,0},{40,8},{48,16},{56,24},{1,33}... | collective-permute-start | bytes 196616 | tf_op jit(solution)/shard_map/ppermute | solution.py:743
  64.1 5.0 %collective-permute-start.15 = (f32[1,16,8,128]{3,2,1,0:T(8,128)S(1)}, f32[1,16,8,128]{3,2,1,0:T(8,128)S(1)}, u32[]{:S(2)}, u32[]{:S(2)}) collective-permute-start(f32[1,16,8,128]{3,2,1,0:T(8,128)S(1)} %bitcast.14), channel_id=1, source_target_pairs={{0,16},{8,24},{16,0},{24,8},{32,48},{40,56},{48,32},{56,40},{1,17}... | collective-permute-start | bytes 196616 | tf_op jit(solution)/shard_map/ppermute | solution.py:743
  73.7 8.3 %collective-permute-start.21 = (f32[8,8,128]{2,1,0:T(8,128)S(1)}, f32[8,8,128]{2,1,0:T(8,128)S(1)}, u32[]{:S(2)}, u32[]{:S(2)}) collective-permute-start(f32[8,8,128]{2,1,0:T(8,128)S(1)} %get-tuple-element.45.own_ref), channel_id=1, source_target_pairs={{0,4},{1,5},{2,6},{3,7},{4,0},{5,1},{6,2},{7,3},{8,12},{9,13},{10,... | collective-permute-start | bytes 98312 | tf_op jit(solution)/shard_map/ppermute | solution.py:757
  77.7 4.6 %collective-permute-start.20 = (f32[8,8,128]{2,1,0:T(8,128)S(1)}, f32[8,8,128]{2,1,0:T(8,128)S(1)}, u32[]{:S(2)}, u32[]{:S(2)}) collective-permute-start(f32[8,8,128]{2,1,0:T(8,128)S(1)} %get-tuple-element.45.own_ref), channel_id=1, source_target_pairs={{0,3},{1,4},{2,5},{3,6},{4,7},{5,0},{6,1},{7,2},{8,13},{9,14},{10,... | collective-permute-start | bytes 98312 | tf_op jit(solution)/shard_map/ppermute | solution.py:757
  78.3 6.2 %collective-permute-start.19 = (f32[8,8,128]{2,1,0:T(8,128)S(1)}, f32[8,8,128]{2,1,0:T(8,128)S(1)}, u32[]{:S(2)}, u32[]{:S(2)}) collective-permute-start(f32[8,8,128]{2,1,0:T(8,128)S(1)} %get-tuple-element.45.own_ref), channel_id=1, source_target_pairs={{0,2},{1,3},{2,4},{3,5},{4,6},{5,7},{6,0},{7,1},{8,14},{9,15},{10,... | collective-permute-start | bytes 98312 | tf_op jit(solution)/shard_map/ppermute | solution.py:757
  81.9 3.1 %collective-permute-start.18 = (f32[8,8,128]{2,1,0:T(8,128)S(1)}, f32[8,8,128]{2,1,0:T(8,128)S(1)}, u32[]{:S(2)}, u32[]{:S(2)}) collective-permute-start(f32[8,8,128]{2,1,0:T(8,128)S(1)} %get-tuple-element.45.own_ref), channel_id=1, source_target_pairs={{0,1},{1,2},{2,3},{3,4},{4,5},{5,6},{6,7},{7,0},{8,15},{9,8},{10,9... | collective-permute-start | bytes 98312 | tf_op jit(solution)/shard_map/ppermute | solution.py:757

commit v6 on v5

--- a/solution.py
+++ b/solution.py
@@ -207,21 +207,21 @@
     first, last = ranges[3]
 
     def body(i, carry):
-        window = Window(v[1], first + 4 * i)
-        for u in (0, 1):
+        window = Window(v[1], first + 8 * i)
+        for u in range(4):
             left = jnp.zeros((level.rows, 128), F32)
             mean = jnp.zeros((level.rows, 128), F32)
             for a in (0, 1):
                 for q in (0, 1):
                     at = 2 * u + a
-                    x = first + 4 * i + at
+                    x = first + 8 * i + at
                     left = left + dd[x, q] * (relaxed(level, 0, x, at, q, window, wd, fd) - v[0][x + 1, q])
                     mean = mean + (cond[0][x, q] + cond[1][x, q])
-            out_f[2 * i + u] = left
-            out_b[2 * i + u] = 0.125 * mean
+            out_f[4 * i + u] = left
+            out_b[4 * i + u] = 0.125 * mean
         return carry
 
-    lax.fori_loop(0, (last - first) // 4, body, 0)
+    lax.fori_loop(0, (last - first) // 8, body, 0)
 
 
 def ascend(level, v, wd, fd, ranges=None):
@@ -561,8 +561,9 @@
     lane = lanes(8)
     slabs[gz] = own_ref[...]
     for j in range(4):
-        slabs[(gz + 7 - j) % 8] = all_ref[0, j]
-        slabs[(gz + 1 + j) % 8] = all_ref[1, j]
+        slabs[gz ^ (1 + j)] = all_ref[0, j]
+        if j < 3:
+            slabs[gz ^ (5 + j)] = all_ref[1, j]
 
     for x in range(8):
         for c, cells in enumerate(exchange([slabs[r, x] for r in range(8)], 8)):
@@ -753,7 +754,7 @@
     pairs = []
     for i in range(rows):
         for k in range(count):
-            pairs.append((i * count + k, i * count + (k + (-step if i % 2 else step)) % count))
+            pairs.append((i * count + k, i * count + (k ^ (step | 4 * (i % 2)))))
     return lax.ppermute(values, ("gy", "gz"), pairs)
 
 

time: 99.8 us -> 99.4 us (level)
  waiting for transfers between devices: 29.6 us -> 31 us
  blocking collectives: 5.45 us -> 4.18 us
    ppermute x4, waiting for transfers between devices: 3.06 us -> 4.45 us  [along_z(): return lax.ppermute(values, ('gy', 'gz'), pairs)]
    all_gather x2, blocking collectives: 5.45 us -> 4.18 us  [both_cores(): lax.all_gather(values, 'gy', axis=0, axis_index_groups=[[i, i + 1] for i...]
where the time goes in v6:
time: 99.4 us; the launch traced here: 99.3 us
  starting transfers between devices  37.2 us (37%)
  waiting for transfers between devices  31 us (31%)
  Pallas kernels  24.7 us (25%)
  blocking collectives  4.18 us (4%)
  local copies, waits for them, and re-layouts  1.91 us (2%)
    pallas_call x8, Pallas kernels, call(): pl.pallas_call(kernel, out_shape=outs, in_specs=specs, out_specs=jax.tree...  24.7 us
    ppermute x12, starting transfers between devices, ring(): lax.ppermute(values, axis, [(i, (i + step) % count) for i in range(count)])  21.6 us
    ppermute x12, waiting for transfers between devices, ring(): lax.ppermute(values, axis, [(i, (i + step) % count) for i in range(count)])  17.5 us
    ppermute x6, waiting for transfers between devices, trade(): lax.ppermute(values, axis, [(i, i ^ step) for i in range(lax.axis_size(ax...  9.12 us
    ppermute x4, starting transfers between devices, along_z(): return lax.ppermute(values, ('gy', 'gz'), pairs)  8.25 us
    ppermute x6, starting transfers between devices, trade(): lax.ppermute(values, axis, [(i, i ^ step) for i in range(lax.axis_size(ax...  7.26 us
    ppermute x4, waiting for transfers between devices, along_z(): return lax.ppermute(values, ('gy', 'gz'), pairs)  4.45 us
    all_gather x2, blocking collectives, both_cores(): lax.all_gather(values, 'gy', axis=0, axis_index_groups=[[i, i + 1] for i...  4.18 us
  transfers between devices with their start and end apart: 22, of which 12 were waited for; matrix products, arithmetic and copies ran while one was open for 0% of the time, Pallas kernels for 0%

profile of v6, /device:TPU:1, one launch (start us, length us, event | category | flops | bytes accessed | tf_op | source)
XLA Modules:
  0.0 99.3 jit_solution(3290361122402430372)
XLA Ops:
  0.0 0.0 copy-start
  0.0 0.9 copy-done
  1.0 0.0 copy-start.1
  1.0 0.9 copy-done.1
  1.9 1.0 %shard_map.28 = (f32[16,2,16,128]{3,2,1,0:T(8,128)S(1)}, f32[16,2,16,128]{3,2,1,0:T(8,128)S(1)}, f32[2,2,16,128]{3,2,1,0:T(8,128)S(1)}, f32[2,2,16,128]{3,2,1,0:T(8,128)S(1)}) custom-call(f32[16,32,128]{2,1,0:T(8,128)S(1)} %copy-done, f32[16,32,128]{2,1,0:T(8,128)S(1)} %copy-done.1), custom_call_target="tpu_custom_call" | custom-call | tf_op jit(solution)/shard_map/pallas_call | solution.py:728
  2.9 2.5 %collective-permute-start.2 = (f32[2,2,16,128]{3,2,1,0:T(8,128)S(1)}, f32[2,2,16,128]{3,2,1,0:T(8,128)S(1)}, u32[]{:S(2)}, u32[]{:S(2)}) collective-permute-start(f32[2,2,16,128]{3,2,1,0:T(8,128)S(1)} %get-tuple-element.35), channel_id=1, source_target_pairs={{0,1},{1,2},{2,3},{3,4},{4,5},{5,6},{6,7},{7,0},{8,9},{9,10},{10,1... | collective-permute-start | bytes 98312 | tf_op jit(solution)/shard_map/ppermute | solution.py:740
  5.5 4.0 %collective-permute-start.3 = (f32[2,2,16,128]{3,2,1,0:T(8,128)S(1)}, f32[2,2,16,128]{3,2,1,0:T(8,128)S(1)}, u32[]{:S(2)}, u32[]{:S(2)}) collective-permute-start(f32[2,2,16,128]{3,2,1,0:T(8,128)S(1)} %get-tuple-element.36), channel_id=1, source_target_pairs={{0,7},{1,0},{2,1},{3,2},{4,3},{5,4},{6,5},{7,6},{8,15},{9,8},{10,9... | collective-permute-start | bytes 98312 | tf_op jit(solution)/shard_map/ppermute | solution.py:740
  9.5 1.2 %collective-permute-start = (f32[16,2,16,128]{3,2,1,0:T(8,128)S(1)}, f32[16,2,16,128]{3,2,1,0:T(8,128)S(1)}, u32[]{:S(2)}, u32[]{:S(2)}) collective-permute-start(f32[16,2,16,128]{3,2,1,0:T(8,128)S(1)} %get-tuple-element.33.refs_2_.m2), channel_id=1, source_target_pairs={{0,64},{64,128},{128,192},{192,0},{1,65},{65,129},{129,193},{193,1... | collective-permute-start | bytes 786440 | tf_op jit(solution)/shard_map/ppermute | solution.py:740
  10.7 1.5 %collective-permute-start.1 = (f32[16,2,16,128]{3,2,1,0:T(8,128)S(1)}, f32[16,2,16,128]{3,2,1,0:T(8,128)S(1)}, u32[]{:S(2)}, u32[]{:S(2)}) collective-permute-start(f32[16,2,16,128]{3,2,1,0:T(8,128)S(1)} %get-tuple-element.34.refs_1_.m1), channel_id=1, source_target_pairs={{0,192},{64,0},{128,64},{192,128},{1,193},{65,1},{129,65},{193,129... | collective-permute-start | bytes 786440 | tf_op jit(solution)/shard_map/ppermute | solution.py:740
  12.2 0.0 collective-permute-done.2
  12.2 0.0 collective-permute-done.3
  12.2 0.1 collective-permute-start.4
  12.3 2.7 %collective-permute-start.5 = (f32[2,2,16,128]{3,2,1,0:T(8,128)S(1)}, f32[2,2,16,128]{3,2,1,0:T(8,128)S(1)}, u32[]{:S(2)}, u32[]{:S(2)}) collective-permute-start(f32[2,2,16,128]{3,2,1,0:T(8,128)S(1)} %pad_maximum_fusion.3.refs_5_.s1), channel_id=1, source_target_pairs={{0,192},{64,0},{128,64},{192,128},{1,193},{65,1},{129,65},{193,129... | collective-permute-start | bytes 98312 | tf_op jit(solution)/shard_map/ppermute | solution.py:740
  15.0 3.3 %collective-permute-done.4.refs_4_.s0 = f32[2,2,16,128]{3,2,1,0:T(8,128)S(1)} collective-permute-done((f32[2,2,16,128]{3,2,1,0:T(8,128)S(1)}, f32[2,2,16,128]{3,2,1,0:T(8,128)S(1)}, u32[]{:S(2)}, u32[]{:S(2)}) %collective-permute-start.4) | collective-permute-done | bytes 32800 | tf_op jit(solution)/shard_map/ppermute | solution.py:740
  18.3 0.0 collective-permute-done.5.refs_7_.s3
  18.3 0.0 collective-permute-done.refs_0_.m0
  18.3 0.0 collective-permute-done.1.refs_3_.m3
  18.3 0.1 shard_map.29
  18.4 3.1 %collective-permute-start.6 = (f32[72,8,128]{2,1,0:T(8,128)S(1)}, f32[72,8,128]{2,1,0:T(8,128)S(1)}, u32[]{:S(2)}, u32[]{:S(2)}) collective-permute-start(f32[72,8,128]{2,1,0:T(8,128)S(1)} %get-tuple-element.37), channel_id=1, source_target_pairs={{0,8},{8,16},{16,24},{24,32},{32,40},{40,48},{48,56},{56,0},{1,9},... | collective-permute-start | bytes 884744 | tf_op jit(solution)/shard_map/ppermute | solution.py:740
  21.4 0.0 collective-permute-start.7
  21.4 0.1 pad_add_fusion.scal
  21.5 3.6 %collective-permute-done.6.yl_ref = f32[72,8,128]{2,1,0:T(8,128)S(1)} collective-permute-done((f32[72,8,128]{2,1,0:T(8,128)S(1)}, f32[72,8,128]{2,1,0:T(8,128)S(1)}, u32[]{:S(2)}, u32[]{:S(2)}) %collective-permute-start.6) | collective-permute-done | bytes 294944 | tf_op jit(solution)/shard_map/ppermute | solution.py:740
  25.1 2.5 %collective-permute-done.7.yr_ref = f32[72,8,128]{2,1,0:T(8,128)S(1)} collective-permute-done((f32[72,8,128]{2,1,0:T(8,128)S(1)}, f32[72,8,128]{2,1,0:T(8,128)S(1)}, u32[]{:S(2)}, u32[]{:S(2)}) %collective-permute-start.7) | collective-permute-done | bytes 294944 | tf_op jit(solution)/shard_map/ppermute | solution.py:740
  27.6 5.7 %shard_map.30 = (f32[16,2,8,128]{3,2,1,0:T(8,128)S(1)}, f32[4,2,8,128]{3,2,1,0:T(8,128)S(1)}, f32[4,2,8,128]{3,2,1,0:T(8,128)S(1)}, f32[32,2,24,128]{3,2,1,0:T(8...) custom-call(s32[3]{0:T(128)S(1)} %pad_add_fusion.scal, ...), custom_call_target="tpu_custom_call" | custom-call | tf_op jit(solution)/shard_map/pallas_call | solution.py:728
  33.3 0.1 collective-permute-start.8
  33.4 2.7 %collective-permute-start.9 = (f32[4,2,8,128]{3,2,1,0:T(8,128)S(1)}, f32[4,2,8,128]{3,2,1,0:T(8,128)S(1)}, u32[]{:S(2)}, u32[]{:S(2)}) collective-permute-start(f32[4,2,8,128]{3,2,1,0:T(8,128)S(1)} %get-tuple-element.41), channel_id=1, source_target_pairs={{0,7},{1,0},{2,1},{3,2},{4,3},{5,4},{6,5},{7,6},{8,15},{9,8},{10,9... | collective-permute-start | bytes 98312 | tf_op jit(solution)/shard_map/ppermute | solution.py:740
  36.1 1.3 %collective-permute-done.8.left_ref = f32[4,2,8,128]{3,2,1,0:T(8,128)S(1)} collective-permute-done((f32[4,2,8,128]{3,2,1,0:T(8,128)S(1)}, f32[4,2,8,128]{3,2,1,0:T(8,128)S(1)}, u32[]{:S(2)}, u32[]{:S(2)}) %collective-permute-start.8) | collective-permute-done | bytes 32800 | tf_op jit(solution)/shard_map/ppermute | solution.py:740
  37.4 0.0 collective-permute-done.9.right_ref
  37.4 0.2 shard_map.31.a_ref
  37.6 2.8 %collective-permute-start.12 = (f32[16,2,8,128]{3,2,1,0:T(8,128)S(1)}, f32[16,2,8,128]{3,2,1,0:T(8,128)S(1)}, u32[]{:S(2)}, u32[]{:S(2)}) collective-permute-start(f32[16,2,8,128]{3,2,1,0:T(8,128)S(1)} %shard_map.31.a_ref), channel_id=1, source_target_pairs={{0,192},{64,128},{128,64},{192,0},{1,193},{65,129},{129,65},{193,1... | collective-permute-start | bytes 393224 | tf_op jit(solution)/shard_map/ppermute | solution.py:744
  40.3 0.3 collective-permute-start.11
  40.7 0.4 collective-permute-start.10
  41.0 4.7 %collective-permute-done.12.d_ref = f32[16,2,8,128]{3,2,1,0:T(8,128)S(1)} collective-permute-done((f32[16,2,8,128]{3,2,1,0:T(8,128)S(1)}, f32[16,2,8,128]{3,2,1,0:T(8,128)S(1)}, u32[]{:S(2)}, u32[]{:S(2)}) %collective-permute-start.12) | collective-permute-done | bytes 131104 | tf_op jit(solution)/shard_map/ppermute | solution.py:744
  45.8 0.0 collective-permute-done.11.c_ref
  45.8 0.0 collective-permute-done.10.b_ref
  45.8 0.1 shard_map.32
  45.9 3.8 %collective-permute-start.13 = (f32[80,8,128]{2,1,0:T(8,128)S(1)}, f32[80,8,128]{2,1,0:T(8,128)S(1)}, u32[]{:S(2)}, u32[]{:S(2)}) collective-permute-start(f32[80,8,128]{2,1,0:T(8,128)S(1)} %get-tuple-element.42), channel_id=1, source_target_pairs={{0,8},{8,16},{16,24},{24,32},{32,40},{40,48},{48,56},{56,0},{1,9},... | collective-permute-start | bytes 983048 | tf_op jit(solution)/shard_map/ppermute | solution.py:740
  49.8 0.0 collective-permute-start.14
  49.8 4.0 %collective-permute-done.13.yl_ref = f32[80,8,128]{2,1,0:T(8,128)S(1)} collective-permute-done((f32[80,8,128]{2,1,0:T(8,128)S(1)}, f32[80,8,128]{2,1,0:T(8,128)S(1)}, u32[]{:S(2)}, u32[]{:S(2)}) %collective-permute-start.13) | collective-permute-done | bytes 327712 | tf_op jit(solution)/shard_map/ppermute | solution.py:740
  53.8 2.8 %collective-permute-done.14.yr_ref = f32[80,8,128]{2,1,0:T(8,128)S(1)} collective-permute-done((f32[80,8,128]{2,1,0:T(8,128)S(1)}, f32[80,8,128]{2,1,0:T(8,128)S(1)}, u32[]{:S(2)}, u32[]{:S(2)}) %collective-permute-start.14) | collective-permute-done | bytes 327712 | tf_op jit(solution)/shard_map/ppermute | solution.py:740
  56.5 4.2 %shard_map.33 = (f32[16,8,128]{2,1,0:T(8,128)S(1)}, f32[16,2,24,128]{3,2,1,0:T(8,128)S(1)}, f32[6,16,2,24,128]{4,3,2,1,0:T(8,128)S(1)}, f32[6,16,2,24,128]{4,3,2...) custom-call(s32[3]{0:T(128)S(1)} %pad_add_fusion.scal, ...), custom_call_target="tpu_custom_call" | custom-call | tf_op jit(solution)/shard_map/pallas_call | solution.py:728
  60.8 3.2 %collective-permute-start.17 = (f32[1,16,8,128]{3,2,1,0:T(8,128)S(1)}, f32[1,16,8,128]{3,2,1,0:T(8,128)S(1)}, u32[]{:S(2)}, u32[]{:S(2)}) collective-permute-start(f32[1,16,8,128]{3,2,1,0:T(8,128)S(1)} %bitcast.12), channel_id=1, source_target_pairs={{0,48},{8,56},{16,32},{24,40},{32,16},{40,24},{48,0},{56,8},{1,49}... | collective-permute-start | bytes 196616 | tf_op jit(solution)/shard_map/ppermute | solution.py:744
  63.9 0.0 collective-permute-start.16
  63.9 0.7 collective-permute-start.15
  64.6 1.5 %collective-permute-done.17 = f32[1,16,8,128]{3,2,1,0:T(8,128)S(1)} collective-permute-done((f32[1,16,8,128]{3,2,1,0:T(8,128)S(1)}, f32[1,16,8,128]{3,2,1,0:T(8,128)S(1)}, u32[]{:S(2)}, u32[]{:S(2)}) %collective-permute-start.17) | collective-permute-done | bytes 65568 | tf_op jit(solution)/shard_map/ppermute | solution.py:744
  66.1 2.9 %collective-permute-done.16 = f32[1,16,8,128]{3,2,1,0:T(8,128)S(1)} collective-permute-done((f32[1,16,8,128]{3,2,1,0:T(8,128)S(1)}, f32[1,16,8,128]{3,2,1,0:T(8,128)S(1)}, u32[]{:S(2)}, u32[]{:S(2)}) %collective-permute-start.16) | collective-permute-done | bytes 65568 | tf_op jit(solution)/shard_map/ppermute | solution.py:744
  69.0 0.0 collective-permute-done.15
  69.0 2.2 %all-gather = f32[8,16,8,128]{3,2,1,0:T(8,128)S(1)} all-gather(f32[4,16,8,128]{3,2,1,0:T(8,128)S(1)} %pad_maximum_fusion), channel_id=2, replica_groups={{0,8},{16,24},{32,40},{48,56},{1,9},{17,25},{33,41},{49,57},{2,10},{18,..., dimensions={0}, use_global_device_ids=true | all-gather | bytes 786432 | tf_op jit(solution)/shard_map/all_gather | solution.py:749
  71.2 2.2 %shard_map.34 = (f32[8,8,128]{2,1,0:T(8,128)S(1)}, f32[16,2,8,128]{3,2,1,0:T(8,128)S(1)}, f32[6,16,2,8,128]{4,3,2,1,0:T(8,128)S(1)}, f32[6,16,2,8,128]{4,3,2,1,0...) custom-call(s32[3]{0:T(128)S(1)} %pad_add_fusion.scal, f32[2,4,16,8,128]{4,3,2,1,0:T(8,128)S(1)} %bitcast.10), custom_call_target="tpu_custom_call" | custom-call | tf_op jit(solution)/shard_map/pallas_call | solution.py:728
  73.4 4.0 %collective-permute-start.21 = (f32[8,8,128]{2,1,0:T(8,128)S(1)}, f32[8,8,128]{2,1,0:T(8,128)S(1)}, u32[]{:S(2)}, u32[]{:S(2)}) collective-permute-start(f32[8,8,128]{2,1,0:T(8,128)S(1)} %get-tuple-element.45.own_ref), channel_id=1, source_target_pairs={{0,4},{1,5},{2,6},{3,7},{4,0},{5,1},{6,2},{7,3},{8,12},{9,13},{10,... | collective-permute-start | bytes 98312 | tf_op jit(solution)/shard_map/ppermute | solution.py:758
  77.4 2.8 %collective-permute-start.20 = (f32[8,8,128]{2,1,0:T(8,128)S(1)}, f32[8,8,128]{2,1,0:T(8,128)S(1)}, u32[]{:S(2)}, u32[]{:S(2)}) collective-permute-start(f32[8,8,128]{2,1,0:T(8,128)S(1)} %get-tuple-element.45.own_ref), channel_id=1, source_target_pairs={{0,3},{1,2},{2,1},{3,0},{4,7},{5,6},{6,5},{7,4},{8,15},{9,14},{10,... | collective-permute-start | bytes 98312 | tf_op jit(solution)/shard_map/ppermute | solution.py:758
  80.2 0.1 collective-permute-start.19
  80.3 1.4 %collective-permute-start.18 = (f32[8,8,128]{2,1,0:T(8,128)S(1)}, f32[8,8,128]{2,1,0:T(8,128)S(1)}, u32[]{:S(2)}, u32[]{:S(2)}) collective-permute-start(f32[8,8,128]{2,1,0:T(8,128)S(1)} %get-tuple-element.45.own_ref), channel_id=1, source_target_pairs={{0,1},{1,0},{2,3},{3,2},{4,5},{5,4},{6,7},{7,6},{8,13},{9,12},{10,... | collective-permute-start | bytes 98312 | tf_op jit(solution)/shard_map/ppermute | solution.py:758
  81.7 0.0 collective-permute-done.21
  81.7 0.2 collective-permute-done.20
  81.9 3.2 %collective-permute-done.19 = f32[8,8,128]{2,1,0:T(8,128)S(1)} collective-permute-done((f32[8,8,128]{2,1,0:T(8,128)S(1)}, f32[8,8,128]{2,1,0:T(8,128)S(1)}, u32[]{:S(2)}, u32[]{:S(2)}) %collective-permute-start.19) | collective-permute-done | bytes 32800 | tf_op jit(solution)/shard_map/ppermute | solution.py:758
  85.1 1.0 %collective-permute-done.18 = f32[8,8,128]{2,1,0:T(8,128)S(1)} collective-permute-done((f32[8,8,128]{2,1,0:T(8,128)S(1)}, f32[8,8,128]{2,1,0:T(8,128)S(1)}, u32[]{:S(2)}, u32[]{:S(2)}) %collective-permute-start.18) | collective-permute-done | bytes 32800 | tf_op jit(solution)/shard_map/ppermute | solution.py:758
  86.2 2.0 %all-gather.1 = f32[8,8,8,128]{3,2,1,0:T(8,128)S(1)} all-gather(f32[4,8,8,128]{3,2,1,0:T(8,128)S(1)} %pad_maximum_fusion.1), channel_id=3, replica_groups={{0,8},{16,24},{32,40},{48,56},{1,9},{17,25},{33,41},{49,57},{2,10},{18,..., dimensions={0}, use_global_device_ids=true | all-gather | bytes 393216 | tf_op jit(solution)/shard_map/all_gather | solution.py:749
  88.1 11.1 %shard_map.35 = f32[16,32,128]{2,1,0:T(8,128)} custom-call(s32[3]{0:T(128)S(1)} %pad_add_fusion.scal, f32[8,8,128]{2,1,0:T(8,128)S(1)} %get-tuple-element.45.own_ref, f32[2,4,8,8,128]{4,3,2,1,0:T(8,128)S(1)} %bitcast.11, f32[16,2,8,128]{3,2,1,0:T(8,128)S(1)} %get-tuple-element.46.refs_0_, f32[6,16,2,8,128]{4,3,2,1,0:T(8,128)S(1)} %get-tuple-element.47.refs_1_, ...), custom_call_target="tpu_custom_call" | custom-call | tf_op jit(solution)/shard_map/pallas_call | solution.py:728
  (6 shorter events, 0.0 us)
Async XLA Ops:
  0.0 0.9 copy-start
  1.0 0.9 copy-start.1
  2.9 9.3 %collective-permute-start.2 = (f32[2,2,16,128]{3,2,1,0:T(8,128)S(1)}, f32[2,2,16,128]{3,2,1,0:T(8,128)S(1)}, u32[]{:S(2)}, u32[]{:S(2)}) collective-permute-start(f32[2,2,16,128]{3,2,1,0:T(8,128)S(1)} %get-tuple-element.35), channel_id=1, source_target_pairs={{0,1},{1,2},{2,3},{3,4},{4,5},{5,6},{6,7},{7,0},{8,9},{9,10},{10,1... | collective-permute-start | bytes 98312 | tf_op jit(solution)/shard_map/ppermute | solution.py:740
  5.5 6.7 %collective-permute-start.3 = (f32[2,2,16,128]{3,2,1,0:T(8,128)S(1)}, f32[2,2,16,128]{3,2,1,0:T(8,128)S(1)}, u32[]{:S(2)}, u32[]{:S(2)}) collective-permute-start(f32[2,2,16,128]{3,2,1,0:T(8,128)S(1)} %get-tuple-element.36), channel_id=1, source_target_pairs={{0,7},{1,0},{2,1},{3,2},{4,3},{5,4},{6,5},{7,6},{8,15},{9,8},{10,9... | collective-permute-start | bytes 98312 | tf_op jit(solution)/shard_map/ppermute | solution.py:740
  9.5 8.8 %collective-permute-start = (f32[16,2,16,128]{3,2,1,0:T(8,128)S(1)}, f32[16,2,16,128]{3,2,1,0:T(8,128)S(1)}, u32[]{:S(2)}, u32[]{:S(2)}) collective-permute-start(f32[16,2,16,128]{3,2,1,0:T(8,128)S(1)} %get-tuple-element.33.refs_2_.m2), channel_id=1, source_target_pairs={{0,64},{64,128},{128,192},{192,0},{1,65},{65,129},{129,193},{193,1... | collective-permute-start | bytes 786440 | tf_op jit(solution)/shard_map/ppermute | solution.py:740
  10.7 7.6 %collective-permute-start.1 = (f32[16,2,16,128]{3,2,1,0:T(8,128)S(1)}, f32[16,2,16,128]{3,2,1,0:T(8,128)S(1)}, u32[]{:S(2)}, u32[]{:S(2)}) collective-permute-start(f32[16,2,16,128]{3,2,1,0:T(8,128)S(1)} %get-tuple-element.34.refs_1_.m1), channel_id=1, source_target_pairs={{0,192},{64,0},{128,64},{192,128},{1,193},{65,1},{129,65},{193,129... | collective-permute-start | bytes 786440 | tf_op jit(solution)/shard_map/ppermute | solution.py:740
  12.2 6.1 %collective-permute-start.4 = (f32[2,2,16,128]{3,2,1,0:T(8,128)S(1)}, f32[2,2,16,128]{3,2,1,0:T(8,128)S(1)}, u32[]{:S(2)}, u32[]{:S(2)}) collective-permute-start(f32[2,2,16,128]{3,2,1,0:T(8,128)S(1)} %pad_maximum_fusion.2.refs_6_.s2), channel_id=1, source_target_pairs={{0,64},{64,128},{128,192},{192,0},{1,65},{65,129},{129,193},{193,1... | collective-permute-start | bytes 98312 | tf_op jit(solution)/shard_map/ppermute | solution.py:740
  12.3 6.0 %collective-permute-start.5 = (f32[2,2,16,128]{3,2,1,0:T(8,128)S(1)}, f32[2,2,16,128]{3,2,1,0:T(8,128)S(1)}, u32[]{:S(2)}, u32[]{:S(2)}) collective-permute-start(f32[2,2,16,128]{3,2,1,0:T(8,128)S(1)} %pad_maximum_fusion.3.refs_5_.s1), channel_id=1, source_target_pairs={{0,192},{64,0},{128,64},{192,128},{1,193},{65,1},{129,65},{193,129... | collective-permute-start | bytes 98312 | tf_op jit(solution)/shard_map/ppermute | solution.py:740
  18.4 6.7 %collective-permute-start.6 = (f32[72,8,128]{2,1,0:T(8,128)S(1)}, f32[72,8,128]{2,1,0:T(8,128)S(1)}, u32[]{:S(2)}, u32[]{:S(2)}) collective-permute-start(f32[72,8,128]{2,1,0:T(8,128)S(1)} %get-tuple-element.37), channel_id=1, source_target_pairs={{0,8},{8,16},{16,24},{24,32},{32,40},{40,48},{48,56},{56,0},{1,9},... | collective-permute-start | bytes 884744 | tf_op jit(solution)/shard_map/ppermute | solution.py:740
  21.4 6.1 %collective-permute-start.7 = (f32[72,8,128]{2,1,0:T(8,128)S(1)}, f32[72,8,128]{2,1,0:T(8,128)S(1)}, u32[]{:S(2)}, u32[]{:S(2)}) collective-permute-start(f32[72,8,128]{2,1,0:T(8,128)S(1)} %get-tuple-element.38), channel_id=1, source_target_pairs={{0,56},{8,0},{16,8},{24,16},{32,24},{40,32},{48,40},{56,48},{1,57}... | collective-permute-start | bytes 884744 | tf_op jit(solution)/shard_map/ppermute | solution.py:740
  33.3 4.1 %collective-permute-start.8 = (f32[4,2,8,128]{3,2,1,0:T(8,128)S(1)}, f32[4,2,8,128]{3,2,1,0:T(8,128)S(1)}, u32[]{:S(2)}, u32[]{:S(2)}) collective-permute-start(f32[4,2,8,128]{3,2,1,0:T(8,128)S(1)} %get-tuple-element.40), channel_id=1, source_target_pairs={{0,1},{1,2},{2,3},{3,4},{4,5},{5,6},{6,7},{7,0},{8,9},{9,10},{10,1... | collective-permute-start | bytes 98312 | tf_op jit(solution)/shard_map/ppermute | solution.py:740
  33.4 4.0 %collective-permute-start.9 = (f32[4,2,8,128]{3,2,1,0:T(8,128)S(1)}, f32[4,2,8,128]{3,2,1,0:T(8,128)S(1)}, u32[]{:S(2)}, u32[]{:S(2)}) collective-permute-start(f32[4,2,8,128]{3,2,1,0:T(8,128)S(1)} %get-tuple-element.41), channel_id=1, source_target_pairs={{0,7},{1,0},{2,1},{3,2},{4,3},{5,4},{6,5},{7,6},{8,15},{9,8},{10,9... | collective-permute-start | bytes 98312 | tf_op jit(solution)/shard_map/ppermute | solution.py:740
  37.6 8.2 %collective-permute-start.12 = (f32[16,2,8,128]{3,2,1,0:T(8,128)S(1)}, f32[16,2,8,128]{3,2,1,0:T(8,128)S(1)}, u32[]{:S(2)}, u32[]{:S(2)}) collective-permute-start(f32[16,2,8,128]{3,2,1,0:T(8,128)S(1)} %shard_map.31.a_ref), channel_id=1, source_target_pairs={{0,192},{64,128},{128,64},{192,0},{1,193},{65,129},{129,65},{193,1... | collective-permute-start | bytes 393224 | tf_op jit(solution)/shard_map/ppermute | solution.py:744
  40.3 5.4 %collective-permute-start.11 = (f32[16,2,8,128]{3,2,1,0:T(8,128)S(1)}, f32[16,2,8,128]{3,2,1,0:T(8,128)S(1)}, u32[]{:S(2)}, u32[]{:S(2)}) collective-permute-start(f32[16,2,8,128]{3,2,1,0:T(8,128)S(1)} %shard_map.31.a_ref), channel_id=1, source_target_pairs={{0,128},{64,192},{128,0},{192,64},{1,129},{65,193},{129,1},{193,65... | collective-permute-start | bytes 393224 | tf_op jit(solution)/shard_map/ppermute | solution.py:744
  40.7 5.1 %collective-permute-start.10 = (f32[16,2,8,128]{3,2,1,0:T(8,128)S(1)}, f32[16,2,8,128]{3,2,1,0:T(8,128)S(1)}, u32[]{:S(2)}, u32[]{:S(2)}) collective-permute-start(f32[16,2,8,128]{3,2,1,0:T(8,128)S(1)} %shard_map.31.a_ref), channel_id=1, source_target_pairs={{0,64},{64,0},{128,192},{192,128},{1,65},{65,1},{129,193},{193,129... | collective-permute-start | bytes 393224 | tf_op jit(solution)/shard_map/ppermute | solution.py:744
  45.9 7.9 %collective-permute-start.13 = (f32[80,8,128]{2,1,0:T(8,128)S(1)}, f32[80,8,128]{2,1,0:T(8,128)S(1)}, u32[]{:S(2)}, u32[]{:S(2)}) collective-permute-start(f32[80,8,128]{2,1,0:T(8,128)S(1)} %get-tuple-element.42), channel_id=1, source_target_pairs={{0,8},{8,16},{16,24},{24,32},{32,40},{40,48},{48,56},{56,0},{1,9},... | collective-permute-start | bytes 983048 | tf_op jit(solution)/shard_map/ppermute | solution.py:740
  49.8 6.8 %collective-permute-start.14 = (f32[80,8,128]{2,1,0:T(8,128)S(1)}, f32[80,8,128]{2,1,0:T(8,128)S(1)}, u32[]{:S(2)}, u32[]{:S(2)}) collective-permute-start(f32[80,8,128]{2,1,0:T(8,128)S(1)} %get-tuple-element.43), channel_id=1, source_target_pairs={{0,56},{8,0},{16,8},{24,16},{32,24},{40,32},{48,40},{56,48},{1,57}... | collective-permute-start | bytes 983048 | tf_op jit(solution)/shard_map/ppermute | solution.py:740
  60.8 5.3 %collective-permute-start.17 = (f32[1,16,8,128]{3,2,1,0:T(8,128)S(1)}, f32[1,16,8,128]{3,2,1,0:T(8,128)S(1)}, u32[]{:S(2)}, u32[]{:S(2)}) collective-permute-start(f32[1,16,8,128]{3,2,1,0:T(8,128)S(1)} %bitcast.12), channel_id=1, source_target_pairs={{0,48},{8,56},{16,32},{24,40},{32,16},{40,24},{48,0},{56,8},{1,49}... | collective-permute-start | bytes 196616 | tf_op jit(solution)/shard_map/ppermute | solution.py:744
  63.9 5.0 %collective-permute-start.16 = (f32[1,16,8,128]{3,2,1,0:T(8,128)S(1)}, f32[1,16,8,128]{3,2,1,0:T(8,128)S(1)}, u32[]{:S(2)}, u32[]{:S(2)}) collective-permute-start(f32[1,16,8,128]{3,2,1,0:T(8,128)S(1)} %bitcast.13), channel_id=1, source_target_pairs={{0,32},{8,40},{16,48},{24,56},{32,0},{40,8},{48,16},{56,24},{1,33}... | collective-permute-start | bytes 196616 | tf_op jit(solution)/shard_map/ppermute | solution.py:744
  63.9 5.0 %collective-permute-start.15 = (f32[1,16,8,128]{3,2,1,0:T(8,128)S(1)}, f32[1,16,8,128]{3,2,1,0:T(8,128)S(1)}, u32[]{:S(2)}, u32[]{:S(2)}) collective-permute-start(f32[1,16,8,128]{3,2,1,0:T(8,128)S(1)} %bitcast.14), channel_id=1, source_target_pairs={{0,16},{8,24},{16,0},{24,8},{32,48},{40,56},{48,32},{56,40},{1,17}... | collective-permute-start | bytes 196616 | tf_op jit(solution)/shard_map/ppermute | solution.py:744
  73.4 8.3 %collective-permute-start.21 = (f32[8,8,128]{2,1,0:T(8,128)S(1)}, f32[8,8,128]{2,1,0:T(8,128)S(1)}, u32[]{:S(2)}, u32[]{:S(2)}) collective-permute-start(f32[8,8,128]{2,1,0:T(8,128)S(1)} %get-tuple-element.45.own_ref), channel_id=1, source_target_pairs={{0,4},{1,5},{2,6},{3,7},{4,0},{5,1},{6,2},{7,3},{8,12},{9,13},{10,... | collective-permute-start | bytes 98312 | tf_op jit(solution)/shard_map/ppermute | solution.py:758
  77.4 4.4 %collective-permute-start.20 = (f32[8,8,128]{2,1,0:T(8,128)S(1)}, f32[8,8,128]{2,1,0:T(8,128)S(1)}, u32[]{:S(2)}, u32[]{:S(2)}) collective-permute-start(f32[8,8,128]{2,1,0:T(8,128)S(1)} %get-tuple-element.45.own_ref), channel_id=1, source_target_pairs={{0,3},{1,2},{2,1},{3,0},{4,7},{5,6},{6,5},{7,4},{8,15},{9,14},{10,... | collective-permute-start | bytes 98312 | tf_op jit(solution)/shard_map/ppermute | solution.py:758
  80.2 4.9 %collective-permute-start.19 = (f32[8,8,128]{2,1,0:T(8,128)S(1)}, f32[8,8,128]{2,1,0:T(8,128)S(1)}, u32[]{:S(2)}, u32[]{:S(2)}) collective-permute-start(f32[8,8,128]{2,1,0:T(8,128)S(1)} %get-tuple-element.45.own_ref), channel_id=1, source_target_pairs={{0,2},{1,3},{2,0},{3,1},{4,6},{5,7},{6,4},{7,5},{8,14},{9,15},{10,... | collective-permute-start | bytes 98312 | tf_op jit(solution)/shard_map/ppermute | solution.py:758
  80.3 5.9 %collective-permute-start.18 = (f32[8,8,128]{2,1,0:T(8,128)S(1)}, f32[8,8,128]{2,1,0:T(8,128)S(1)}, u32[]{:S(2)}, u32[]{:S(2)}) collective-permute-start(f32[8,8,128]{2,1,0:T(8,128)S(1)} %get-tuple-element.45.own_ref), channel_id=1, source_target_pairs={{0,1},{1,0},{2,3},{3,2},{4,5},{5,4},{6,7},{7,6},{8,13},{9,12},{10,... | collective-permute-start | bytes 98312 | tf_op jit(solution)/shard_map/ppermute | solution.py:758
